TPU v7x, 32 devices: a whole 2x2x4 slice. The times are simulated.
32 devices in a mesh: chan: 8 (over z, core), freq: 4 (over y, x).
Axes of the slice: x: 2, y: 2, z: 4, core: 2. Of those that a mesh axis runs over, the one named last changes fastest.
Arguments:
- segments: bfloat16 [64, 2048, 1024], P('freq', 'chan'), may hold values from -120 to 120, as said below
- available: int32 [64, 2048], P('freq', 'chan'), may hold values 0 or 1
- node_windows: int32 [4], P('freq'), may hold values from 1 to 16, 40 in all
Outputs:
- cross_stack: bfloat16 [2, 128, 2048, 2048], P(None, 'freq', 'chan')
Inputs may be any that keep to these rules, and one draw needn't show every extreme that they name: `segments`: samples are finite and of moderate size. `node_windows`: A node's windows fill its first slots; the counts of all nodes sum to 40.
All inputs are finite; a program needn't handle non-finite values. No bound on the sum of `available` or of `node_windows` on one device may be relied on, other than what follows from the above.
Results may differ from a plain program's by a relative error of at most 0.013.
Values may be sent and summed in bfloat16 or wider, within the bound.
No kernel may reach another device: no remote copies, remote signals or barrier semaphores. Data moves between devices by JAX's collectives and lax.ppermute only.
A program may use at most 448 MiB of HBM per device.

v0:
```python
import math

import jax
import jax.numpy as jnp
from jax import lax
from jax.sharding import PartitionSpec as P

FREQS = 128
FIRST_BIN = 64


epsilon = 1e-06


def transform_cols(sample_count, bin_count, first_bin):
    sample_index = jnp.arange(sample_count, dtype=jnp.int32)[None, :]
    bin_index = (first_bin + jnp.arange(bin_count, dtype=jnp.int32))[:, None]
    angles = (bin_index * sample_index % sample_count).astype(jnp.float32) * (
        2.0 * math.pi / sample_count
    )
    return jnp.concatenate([jnp.cos(angles), -jnp.sin(angles)], axis=0).astype(jnp.bfloat16)


def pair_products(rows_block, cols_block, stack_scale):
    flipped = jnp.stack([rows_block[1], -rows_block[0]])
    real_part = jnp.einsum(
        "rfwi,rfwj->fij", rows_block, cols_block, preferred_element_type=jnp.float32
    )
    imag_part = jnp.einsum(
        "rfwi,rfwj->fij", flipped, cols_block, preferred_element_type=jnp.float32
    )
    return (jnp.stack([real_part, imag_part]) * stack_scale).astype(jnp.bfloat16)


def shards(segments, available, node_windows):
    slot_count, local_chan, sample_count = segments.shape
    bin_count = FREQS
    cos_sin = transform_cols(sample_count, bin_count, FIRST_BIN)
    raw_spectra = jnp.einsum("kl,wcl->kwc", cos_sin, segments, preferred_element_type=jnp.float32)
    raw_spectra = raw_spectra.reshape(2, bin_count, slot_count, local_chan)
    slot_index = jnp.arange(slot_count, dtype=jnp.int32)
    live_mask = available * (slot_index < node_windows[0]).astype(jnp.int32)[:, None]
    spectra = (raw_spectra * live_mask.astype(jnp.float32)[None, None]).astype(jnp.bfloat16)
    spectra_wide = spectra.astype(jnp.float32)
    energy = jnp.sum(spectra_wide * spectra_wide, axis=(0, 1)) / bin_count
    whitened = (spectra_wide * lax.rsqrt(energy + epsilon)[None, None]).astype(jnp.bfloat16)
    my_bins = lax.all_to_all(whitened, "freq", split_axis=1, concat_axis=2, tiled=True)
    all_slots = my_bins.shape[2]
    window_total = all_slots * 5 // 8
    stack_scale = jnp.float32(1.0 / window_total)
    return pair_products(my_bins, lax.all_gather(my_bins, "chan", axis=3, tiled=True), stack_scale)


def solution(mesh):
    placed = (P("freq", "chan", None), P("freq", "chan"), P("freq"))
    return jax.shard_map(
        shards, mesh=mesh, in_specs=placed, out_specs=P(None, "freq", "chan", None), check_vma=False
    )
```

profile of v0, /device:TPU:0, one launch (start us, length us, event | category | flops | bytes accessed | tf_op | source)
XLA Modules:
  0.0 336.9 jit_solution(5432680264078391013)
XLA Ops:
  6.5 0.0 all-gather.2.cloned.1.call-start
  7.2 2.4 cosine_convert_fusion
  9.7 0.8 multiply_convert_fusion.3
  10.4 5.8 %multiply_reduce_fusion = (f32[16,256]{1,0:T(8,128)S(1)}, f32[256,16,256]{2,0,1:T(8,128)S(1)}) fusion(f32[16,256]{1,0:T(8,128)S(1)} %multiply_convert_fusion.3, bf16[16,256,1024]{2,1,0:T(8,128)(2,1)} %param.3, bf16[128,1024]{1,0:T(8,128)(2,1)S(1)} %get-tuple-element.10, bf16[128,1024]{1,0:T(8,128)(2,1)S(1)} %get-tuple-element.9), kind=kOutput, calls=%fused_computation.5 | convolution fusion | flops 2153771008 | bytes 13139968 | tf_op jit(solution)/shard_map/kl,wcl->kwc/dot_general | solution.py:39
  16.3 2.4 copy.7
  18.7 0.6 multiply_convert_fusion
  19.3 3.3 copy.8
  22.6 30.3 %all_to_all.18 = bf16[2,128,16,256]{3,0,2,1:T(2,128)(2,1)S(1)} all-to-all(bf16[2,128,16,256]{3,0,2,1:T(2,128)(2,1)S(1)} %copy.8), channel_id=1, replica_groups=mesh['chan'=8,'freq'=4] {'freq'}, dimensions={1} | all-to-all | bytes 4194304 | tf_op jit(solution)/shard_map/all_to_all | solution.py:47
  52.9 1.8 copy.14
  54.7 0.0 copy-start
  54.7 0.0 all-gather.2.cloned.1.call-update
  54.7 2.8 fusion.15
  57.5 148.9 %all-gather.2.cloned.1.call-done = bf16[2,32,64,2048]{3,2,0,1:T(8,128)(2,1)} async-done(((bf16[2,32,64,256]{3,2,0,1:T(8,128)(2,1)}), bf16[2,32,64,2048]{3,2,0,1:T(8,128)(2,1)}) %all-gather.2.cloned.1.call-update) | async-done | bytes 16777232 | tf_op jit(solution)/shard_map/all_gather | solution.py:51
  206.4 0.0 copy-done
  206.4 0.0 copy-start.1
  206.4 29.9 %convolution_bitcast_fusion.1 = f32[1,32,256,2048]{3,2,1,0:T(8,128)} fusion(bf16[2,32,64,256]{3,2,0,1:T(8,128)(2,1)S(1)} %bitcast.30, bf16[2,32,64,2048]{3,2,0,1:T(8,128)(2,1)} %all-gather.2.cloned.1.call-done), kind=kOutput, calls=%fused_computation.3 | convolution fusion | flops 4294967296 | bytes 85983232 | tf_op jit(solution)/shard_map/rfwi,rfwj->fij/dot_general | solution.py:26
  236.4 0.0 copy-done.1
  236.4 29.8 %convolution_bitcast_fusion = f32[1,32,256,2048]{3,2,1,0:T(8,128)} fusion(bf16[2,32,64,2048]{3,2,0,1:T(8,128)(2,1)} %all-gather.2.cloned.1.call-done, bf16[1,32,64,256]{3,2,0,1:T(8,128)(2,1)S(1)} %bitcast.34, bf16[1,32,64,256]{3,2,0,1:T(8,128)(2,1)S(1)} %bitcast.33), kind=kOutput, calls=%fused_computation.2 | convolution fusion | flops 4296015872 | bytes 85983232 | tf_op jit(solution)/shard_map/rfwi,rfwj->fij/dot_general | solution.py:29
  266.2 63.9 %fusion = bf16[2,32,256,2048]{3,2,1,0:T(8,128)(2,1)} fusion(f32[1,32,256,2048]{3,2,1,0:T(8,128)} %convolution_bitcast_fusion, f32[1,32,256,2048]{3,2,1,0:T(8,128)} %convolution_bitcast_fusion.1), kind=kLoop, calls=%fused_computation.1 | loop fusion | flops 100663296 | bytes 201326592 | tf_op jit(solution)/shard_map/convert_element_type | solution.py:32
  (3 shorter events, 0.0 us)
Async XLA Ops:
  6.5 199.9 %all-gather.2.cloned.1.call-start = ((), (), s32[]{:S(2)}) async-start(), calls=%async_computation.1 | async-start | bytes 18874368 | tf_op jit(solution)/shard_map/all_gather | solution.py:51
  54.7 151.7 %copy-start = (bf16[2,4,32,16,256]{4,3,1,0,2:T(8,128)(2,1)S(1)}, bf16[2,4,32,16,256]{4,3,1,0,2:T(8,128)(2,1)}, u32[]{:S(2)}) copy-start(bf16[2,4,32,16,256]{4,3,1,0,2:T(8,128)(2,1)} %copy.14) | copy-start | bytes 6291460
  206.4 29.9 %copy-start.1 = (bf16[1,32,4,16,256]{4,3,2,0,1:T(8,128)(2,1)S(1)}, bf16[1,32,4,16,256]{4,3,2,0,1:T(8,128)(2,1)}, u32[]{:S(2)}) copy-start(bf16[1,32,4,16,256]{4,3,2,0,1:T(8,128)(2,1)} %get-tuple-element.6) | copy-start | bytes 3145732
Sparse Core Ops, SparseCore 0:
  54.9 151.5 all-gather.1
where the time goes:
time: 337 us
  waiting for transfers between devices  149 us (44%)
  other arithmetic  70.6 us (21%)
  matrix products  65.5 us (19%)
  blocking collectives  30.3 us (9%)
  between operations  14.1 us (4%)
  local copies, waits for them, and re-layouts  7.5 us (2%)
    all_gather x1, waiting for transfers between devices, shards(): lax.all_gather(my_bins, 'chan', axis=3, tiled=True)  149 us
    convert_element_type x1, other arithmetic, pair_products(): (jnp.stack([real_part, imag_part]) * stack_scale).astype(jnp.bfloat16)  63.9 us
    all_to_all x1, blocking collectives, shards(): lax.all_to_all(whitened, 'freq', split_axis=1, concat_axis=2, tiled=True)  30.3 us
    dot_general x1, matrix products, pair_products(): jnp.einsum('rfwi,rfwj->fij', rows_block, cols_block, preferred_element_ty...  29.9 us
    dot_general x1, matrix products, pair_products(): jnp.einsum('rfwi,rfwj->fij', flipped, cols_block, preferred_element_type=...  29.8 us
  transfers between devices with their start and end apart: 1, of which 1 were waited for; matrix products, arithmetic and copies ran while one was open for 1% of the time, Pallas kernels for 0%

commit v1 on v0

v1 whole, which is shorter than its diff:
```python
import functools
import math

import jax
import jax.numpy as jnp
import ml_dtypes
import numpy as np
from jax import lax
from jax.experimental import pallas as pl
from jax.experimental.pallas import tpu as pltpu
from jax.sharding import PartitionSpec as P

FREQS = 128
FIRST_BIN = 64
EPSILON = 1e-06
CHUNK_BINS = 8
VMEM_LIMIT = 40 << 20


def transform_table(nodes, chunks, chunk_bins, samples):
    sample_index = np.arange(samples, dtype=np.int64)[None, :]
    bin_index = (FIRST_BIN + np.arange(FREQS, dtype=np.int64))[:, None]
    angles = (bin_index * sample_index % samples).astype(np.float64) * (2.0 * math.pi / samples)
    parts = np.stack([np.cos(angles), -np.sin(angles)]).astype(np.float32).astype(ml_dtypes.bfloat16)
    parts = parts.reshape(2, nodes, chunks, chunk_bins, samples).transpose(1, 2, 0, 3, 4)
    return parts.reshape(nodes, chunks * 2 * chunk_bins, samples)


def spectra_kernel(nodes, chunks, piece_rows, me_ref, count_ref, seg_ref, avail_ref, table_ref, *refs):
    pieces, table = refs[:-1], refs[-1]
    step = pl.program_id(0)
    node_rows = chunks * piece_rows

    @pl.when(step == 0)
    def _():
        for d in range(nodes):
            table[d * node_rows:(d + 1) * node_rows, :] = table_ref[me_ref[0] ^ d]

    block = seg_ref.shape[0]
    for i in range(block):
        w = step * block + i
        raw = lax.dot_general(
            table[...], seg_ref[i], (((1,), (1,)), ((), ())), preferred_element_type=jnp.float32
        )
        live = jnp.where(w < count_ref[0], avail_ref[pl.ds(w, 1), :], 0).astype(jnp.float32)
        spectra = (raw * live).astype(jnp.bfloat16).astype(jnp.float32)
        energy = jnp.sum(spectra * spectra, axis=0, keepdims=True) / FREQS
        whitened = (spectra * lax.rsqrt(energy + EPSILON)).astype(jnp.bfloat16)
        for p, piece in enumerate(pieces):
            piece[w] = whitened[p * piece_rows:(p + 1) * piece_rows]


def spectra_pieces(me, node_windows, segments, available, table, chunks, chunk_bins):
    slots, chan, samples = segments.shape
    nodes = table.shape[0]
    piece = jax.ShapeDtypeStruct((slots, 2 * chunk_bins, chan), jnp.bfloat16)
    block = 2
    out = pl.pallas_call(
        functools.partial(spectra_kernel, nodes, chunks, 2 * chunk_bins),
        grid=(slots // block,),
        in_specs=[
            pl.BlockSpec(memory_space=pltpu.SMEM),
            pl.BlockSpec(memory_space=pltpu.SMEM),
            pl.BlockSpec((block, chan, samples), lambda i: (i, 0, 0)),
            pl.BlockSpec((slots, chan), lambda i: (0, 0)),
            pl.BlockSpec(table.shape, lambda i: (0, 0, 0)),
        ],
        out_specs=[pl.BlockSpec(piece.shape, lambda i: (0, 0, 0))] * (nodes * chunks),
        out_shape=[piece] * (nodes * chunks),
        scratch_shapes=[pltpu.VMEM((2 * FREQS, samples), jnp.bfloat16)],
        compiler_params=pltpu.CompilerParams(vmem_limit_bytes=VMEM_LIMIT),
        cost_estimate=pl.CostEstimate(
            flops=2 * slots * chan * samples * 2 * FREQS, bytes_accessed=2 * slots * chan * samples, transcendentals=0
        ),
        name="spectra",
    )(me, node_windows, segments, available, table)
    return [out[d * chunks:(d + 1) * chunks] for d in range(nodes)]


def pack_kernel(nodes, slots, chunk_bins, windows, me_ref, *refs):
    counts, pieces, (packed_ref, flipped_ref) = refs[:nodes], refs[nodes:2 * nodes], refs[2 * nodes:]
    me = me_ref[0]
    chan = packed_ref.shape[2]
    out_rows, in_rows = chunk_bins * 2 * windows, slots * 2 * chunk_bins
    col = lax.broadcasted_iota(jnp.int32, (1, in_rows), 1)
    slot, part, fbin = col // (2 * chunk_bins), (col // chunk_bins) % 2, col % chunk_bins
    row = lax.broadcasted_iota(jnp.int32, (out_rows, in_rows), 0)
    sign = jnp.where(part == 1, 1.0, -1.0)
    packed = jnp.zeros((out_rows, chan), jnp.float32)
    flipped = jnp.zeros((out_rows, chan), jnp.float32)
    for d in range(nodes):
        start = 0
        for e in range(nodes):
            start = start + jnp.where((me ^ e) < (me ^ d), counts[e][0], 0)
        place = fbin * (2 * windows) + start + slot
        alive = slot < counts[d][0]
        own = jnp.where(alive, place + part * windows, -1)
        other = jnp.where(alive, place + (1 - part) * windows, -1)
        rows = pieces[d][...].reshape(in_rows, chan)
        packed += jnp.dot(
            jnp.where(row == own, 1.0, 0.0).astype(jnp.bfloat16), rows, preferred_element_type=jnp.float32
        )
        flipped += jnp.dot(
            jnp.where(row == other, sign, 0.0).astype(jnp.bfloat16), rows, preferred_element_type=jnp.float32
        )
    packed_ref[...] = packed.astype(jnp.bfloat16).reshape(packed_ref.shape)
    flipped_ref[...] = flipped.astype(jnp.bfloat16).reshape(flipped_ref.shape)


def pack_windows(me, counts, pieces, chunk_bins, windows):
    slots, _, chan = pieces[0].shape
    nodes = len(pieces)
    shape = jax.ShapeDtypeStruct((chunk_bins, 2 * windows, chan), jnp.bfloat16)
    whole = pl.BlockSpec(memory_space=pltpu.VMEM)
    return pl.pallas_call(
        functools.partial(pack_kernel, nodes, slots, chunk_bins, windows),
        in_specs=[pl.BlockSpec(memory_space=pltpu.SMEM)] * (1 + nodes) + [whole] * nodes,
        out_specs=[whole, whole],
        out_shape=[shape, shape],
        compiler_params=pltpu.CompilerParams(vmem_limit_bytes=VMEM_LIMIT),
        cost_estimate=pl.CostEstimate(
            flops=1 << 30, bytes_accessed=1 << 21, transcendentals=0
        ),
        name="pack",
    )(me, *counts, *pieces)


def pairs_kernel(steps, chan, scale, place_ref, flipped_ref, *refs):
    blocks, out_ref = refs[:2 * steps], refs[-1]
    z, core = place_ref[0] // 2, place_ref[0] % 2
    both = jnp.concatenate([blocks[0][0], flipped_ref[0]], axis=1)
    rows = jnp.transpose(both, (1, 0))
    for t in range(steps):
        source = lax.rem(z - t + steps, steps) * 2
        for k in range(2):
            column = (source + (core if k == 0 else 1 - core)) * chan
            product = jnp.dot(rows, blocks[2 * t + k][0], preferred_element_type=jnp.float32) * scale
            product = product.astype(jnp.bfloat16)
            columns = pl.ds(pl.multiple_of(column, chan), chan)
            out_ref[0, 0, :, columns] = product[:chan]
            out_ref[1, 0, :, columns] = product[chan:]


def pair_products(place, flipped, blocks, out, bins, chunk, scale):
    chunk_bins, depth, chan = flipped.shape
    steps = len(blocks) // 2
    total = chan * 2 * steps
    block_spec = pl.BlockSpec((1, depth, chan), lambda i: (i, 0, 0))
    specs = [pl.BlockSpec(memory_space=pltpu.SMEM)] + [block_spec] * (1 + len(blocks))
    operands = [place, flipped, *blocks]
    aliases = {}
    if out is not None:
        specs.append(pl.BlockSpec(memory_space=pl.ANY))
        aliases = {len(operands): 0}
        operands.append(out)
    return pl.pallas_call(
        functools.partial(pairs_kernel, steps, chan, scale),
        grid=(chunk_bins,),
        in_specs=specs,
        out_specs=pl.BlockSpec((2, 1, chan, total), lambda i: (0, chunk * chunk_bins + i, 0, 0)),
        out_shape=jax.ShapeDtypeStruct((2, bins, chan, total), jnp.bfloat16),
        input_output_aliases=aliases,
        compiler_params=pltpu.CompilerParams(vmem_limit_bytes=VMEM_LIMIT),
        cost_estimate=pl.CostEstimate(
            flops=4 * chunk_bins * depth * chan * total,
            bytes_accessed=4 * chunk_bins * chan * total,
            transcendentals=0,
        ),
        name="pairs",
    )(*operands)


def shards(nodes, groups, segments, available, node_windows):
    slots, chan, samples = segments.shape
    bins = FREQS // nodes
    chunk_bins = math.gcd(bins, CHUNK_BINS)
    chunks = bins // chunk_bins
    windows = slots * nodes * 5 // 8
    steps = groups // 2
    me = lax.axis_index("freq").astype(jnp.int32).reshape(1)
    place = lax.axis_index("chan").astype(jnp.int32).reshape(1)
    swap = [[(f, f ^ d) for f in range(nodes)] for d in range(nodes)]
    ring = [(i, (i + 2) % groups) for i in range(groups)]
    cores = [(i, i ^ 1) for i in range(groups)]

    counts = [node_windows] + [lax.ppermute(node_windows, "freq", swap[d]) for d in range(1, nodes)]
    table = jnp.asarray(transform_table(nodes, chunks, chunk_bins, samples))
    pieces = spectra_pieces(me, node_windows, segments, available, table, chunks, chunk_bins)
    packed, flipped = [], []
    for c in range(chunks):
        mine = [pieces[0][c]] + [lax.ppermute(pieces[d][c], "freq", swap[d]) for d in range(1, nodes)]
        p, f = pack_windows(me, counts, mine, chunk_bins, windows)
        packed.append(p)
        flipped.append(f)
    out = None
    scale = 1.0 / windows
    for c in range(chunks):
        block, blocks = packed[c], []
        for t in range(steps):
            blocks += [block, lax.ppermute(block, "chan", cores)]
            if t < steps - 1:
                block = lax.ppermute(block, "chan", ring)
        out = pair_products(place, flipped[c], blocks, out, bins, c, scale)
    return out


def solution(mesh):
    placed = (P("freq", "chan", None), P("freq", "chan"), P("freq"))
    return jax.shard_map(
        functools.partial(shards, mesh.shape["freq"], mesh.shape["chan"]),
        mesh=mesh,
        in_specs=placed,
        out_specs=P(None, "freq", "chan", None),
        check_vma=False,
    )
```

time: 337 us -> 175 us (0.52)
  waiting for transfers between devices: 149 us -> 66.3 us
  other arithmetic: 70.6 us -> 0 us
  matrix products: 65.5 us -> 0 us
  Pallas kernels: 0 us -> 56.9 us
  blocking collectives: 30.3 us -> 0 us
  starting transfers between devices: 0.01 us -> 29.9 us
  between operations: 14.1 us -> 0.9 us
  local copies, waits for them, and re-layouts: 7.5 us -> 19.3 us
    all_gather x1 -> x0, waiting for transfers between devices: 149 us -> none  [shards(): lax.all_gather(my_bins, 'chan', axis=3, tiled=True)]
    ppermute x0 -> x43, waiting for transfers between devices: none -> 66.3 us  [the longest x12 60.4 us: shards(): block = lax.ppermute(block, 'chan', ring)]
    dot_general x3 -> x0, matrix products: 65.5 us -> none  [the longest x1 29.9 us: pair_products(): jnp.einsum('rfwi,rfwj->fij', rows_block, cols_block, preferred_element_ty...]
    convert_element_type x4 -> x0, other arithmetic: 65.3 us -> none  [the longest x1 63.9 us: pair_products(): (jnp.stack([real_part, imag_part]) * stack_scale).astype(jnp.bfloat16)]
    pallas_call x0 -> x9, Pallas kernels: none -> 56.9 us  [the longest x4 41.8 us: pair_products(): pl.pallas_call(functools.partial(pairs_kernel, steps, chan, scale), grid=...]
    all_to_all x1 -> x0, blocking collectives: 30.3 us -> none  [shards(): lax.all_to_all(whitened, 'freq', split_axis=1, concat_axis=2, tiled=True)]
    ppermute x0 -> x43, starting transfers between devices: none -> 29.9 us  [the longest x12 15.1 us: shards(): lax.ppermute(pieces[d][c], 'freq', swap[d])]
    unnamed x4 -> x54, local copies, waits for them, and re-layouts: 0.01 us -> 19.3 us
  transfers between devices with their start and end apart: 1 -> 43, of which waited for: 1 -> 13; matrix products, arithmetic and copies ran while one was open for 1% -> 0% of each run, Pallas kernels for 0% -> 24%
where the time goes in v1:
time: 175 us; the launch traced here: 173 us
  waiting for transfers between devices  66.3 us (38%)
  Pallas kernels  56.9 us (33%)
  starting transfers between devices  29.9 us (17%)
  local copies, waits for them, and re-layouts  19.3 us (11%)
    ppermute x12, waiting for transfers between devices, shards(): block = lax.ppermute(block, 'chan', ring)  60.4 us
    pallas_call x4, Pallas kernels, pair_products(): pl.pallas_call(functools.partial(pairs_kernel, steps, chan, scale), grid=...  41.8 us
    unnamed x54, local copies, waits for them, and re-layouts  19.3 us
    ppermute x12, starting transfers between devices, shards(): lax.ppermute(pieces[d][c], 'freq', swap[d])  15.1 us
    pallas_call x4, Pallas kernels, pack_windows(): pl.pallas_call(functools.partial(pack_kernel, nodes, slots, chunk_bins, w...  10.6 us
    ppermute x12, starting transfers between devices, shards(): block = lax.ppermute(block, 'chan', ring)  6.75 us
    ppermute x3, starting transfers between devices, shards(): lax.ppermute(node_windows, 'freq', swap[d])  6.05 us
    pallas_call x1, Pallas kernels, spectra_pieces(): pl.pallas_call(functools.partial(spectra_kernel, nodes, chunks, 2 * chunk...  4.48 us
  transfers between devices with their start and end apart: 43, of which 13 were waited for; matrix products, arithmetic and copies ran while one was open for 0% of the time, Pallas kernels for 24%

profile of v1, /device:TPU:0, one launch (start us, length us, event | category | flops | bytes accessed | tf_op | source)
XLA Modules:
  0.0 173.3 jit_solution(3642662610630109373)
XLA Ops:
  0.7 3.4 %copy-done = bf16[16,256,1024]{2,1,0:T(8,128)(2,1)S(1)} copy-done((bf16[16,256,1024]{2,1,0:T(8,128)(2,1)S(1)}, bf16[16,256,1024]{2,1,0:T(8,128)(2,1)}, u32[]{:S(2)}) %copy-start) | copy-done | bytes 8388632
  4.0 1.0 copy-done.1
  5.8 4.5 %spectra.1 = (bf16[16,16,256]{2,1,0:T(8,128)(2,1)S(1)}, bf16[16,16,256]{2,1,0:T(8,128)(2,1)S(1)}, bf16[16,16,256]{2,1,0:T(8,128)(2,1)S(1)}, bf16[16,16,256]{2,1,...) custom-call(s32[1]{0:T(128)} %bitcast.1.me_ref, ...), custom_call_target="tpu_custom_call" | custom-call | flops 2147483648 | bytes 8388608 | tf_op jit(solution)/shard_map/spectra/pallas_call | solution.py:58
  10.3 3.0 %collective-permute-start.33 = (bf16[16,16,256]{2,1,0:T(8,128)(2,1)S(1)}, bf16[16,16,256]{2,1,0:T(8,128)(2,1)S(1)}, u32[]{:S(2)}, u32[]{:S(2)}) collective-permute-start(bf16[16,16,256]{2,1,0:T(8,128)(2,1)S(1)} %get-tuple-element.48), channel_id=1, source_target_pairs={{0,1},{1,0},{2,3},{3,2},{4,5},{5,4},{6,7},{7,6},{8,9},{9,8},{10,11... | collective-permute-start | bytes 393224 | tf_op jit(solution)/shard_map/ppermute | solution.py:191
  13.3 1.5 collective-permute-start.34
  14.8 1.9 %collective-permute-start = (s32[1]{0:T(128)}, s32[1]{0:T(128)}, u32[]{:S(2)}, u32[]{:S(2)}) collective-permute-start(s32[1]{0:T(128)} %param.6), channel_id=1, source_target_pairs={{0,1},{1,0},{2,3},{3,2},{4,5},{5,4},{6,7},{7,6},{8,9},{9,8},{10,11... | collective-permute-start | bytes 20 | tf_op jit(solution)/shard_map/ppermute | solution.py:186
  16.8 1.5 collective-permute-start.1
  18.3 1.5 collective-permute-done.refs_1_
  19.8 2.6 %collective-permute-start.2 = (s32[1]{0:T(128)}, s32[1]{0:T(128)}, u32[]{:S(2)}, u32[]{:S(2)}) collective-permute-start(s32[1]{0:T(128)} %param.6), channel_id=1, source_target_pairs={{0,3},{1,2},{2,1},{3,0},{4,7},{5,6},{6,5},{7,4},{8,11},{9,10},{10,... | collective-permute-start | bytes 20 | tf_op jit(solution)/shard_map/ppermute | solution.py:186
  23.0 1.6 collective-permute-done.2.refs_3_
  24.5 1.7 collective-permute-start.24
  26.2 1.4 collective-permute-start.25
  28.0 1.7 collective-permute-start.14
  29.7 2.7 %pack.7 = (bf16[8,80,256]{2,1,0:T(8,128)(2,1)S(1)}, bf16[8,80,256]{2,1,0:T(8,128)(2,1)S(1)}) custom-call(s32[1]{0:T(128)} %bitcast.1.me_ref, s32[1]{0:T(128)S(6)} %copy.11.count_ref.refs_0_, s32[1]{0:T(128)} %collective-permute-done.refs_1_, s32[1]{0:T(128)} %collective-permute-done.1.refs_2_, s32[1]{0:T(128)} %collective-permute-done.2.refs_3_, ...), custom_call_target="tpu_custom_call" | custom-call | flops 1073741824 | bytes 2097152 | tf_op jit(solution)/shard_map/pack/pallas_call | solution.py:115
  32.4 1.5 collective-permute-start.15
  34.3 1.7 collective-permute-start.37
  36.0 2.7 %pack.6 = (bf16[8,80,256]{2,1,0:T(8,128)(2,1)S(1)}, bf16[8,80,256]{2,1,0:T(8,128)(2,1)S(1)}) custom-call(s32[1]{0:T(128)} %bitcast.1.me_ref, s32[1]{0:T(128)S(6)} %copy.11.count_ref.refs_0_, s32[1]{0:T(128)} %collective-permute-done.refs_1_, s32[1]{0:T(128)} %collective-permute-done.1.refs_2_, s32[1]{0:T(128)} %collective-permute-done.2.refs_3_, ...), custom_call_target="tpu_custom_call" | custom-call | flops 1073741824 | bytes 2097152 | tf_op jit(solution)/shard_map/pack/pallas_call | solution.py:115
  38.8 1.6 collective-permute-start.27
  40.4 1.5 collective-permute-start.4
  41.9 1.4 collective-permute-start.5
  43.3 2.7 %pack.5 = (bf16[8,80,256]{2,1,0:T(8,128)(2,1)S(1)}, bf16[8,80,256]{2,1,0:T(8,128)(2,1)S(1)}) custom-call(s32[1]{0:T(128)} %bitcast.1.me_ref, s32[1]{0:T(128)S(6)} %copy.11.count_ref.refs_0_, s32[1]{0:T(128)} %collective-permute-done.refs_1_, s32[1]{0:T(128)} %collective-permute-done.1.refs_2_, s32[1]{0:T(128)} %collective-permute-done.2.refs_3_, ...), custom_call_target="tpu_custom_call" | custom-call | flops 1073741824 | bytes 2097152 | tf_op jit(solution)/shard_map/pack/pallas_call | solution.py:115
  46.0 2.8 %collective-permute-done.4.refs_6_ = bf16[16,16,256]{2,1,0:T(8,128)(2,1)S(1)} collective-permute-done((bf16[16,16,256]{2,1,0:T(8,128)(2,1)S(1)}, bf16[16,16,256]{2,1,0:T(8,128)(2,1)S(1)}, u32[]{:S(2)}, u32[]{:S(2)}) %collective-permute-start.4) | collective-permute-done | bytes 131104 | tf_op jit(solution)/shard_map/ppermute | solution.py:191
  48.8 1.6 collective-permute-start.17
  50.4 2.7 %pack.4 = (bf16[8,80,256]{2,1,0:T(8,128)(2,1)S(1)}, bf16[8,80,256]{2,1,0:T(8,128)(2,1)S(1)}) custom-call(s32[1]{0:T(128)} %bitcast.1.me_ref, s32[1]{0:T(128)S(6)} %copy.11.count_ref.refs_0_, s32[1]{0:T(128)} %collective-permute-done.refs_1_, s32[1]{0:T(128)} %collective-permute-done.1.refs_2_, s32[1]{0:T(128)} %collective-permute-done.2.refs_3_, ...), custom_call_target="tpu_custom_call" | custom-call | flops 1073741824 | bytes 2097152 | tf_op jit(solution)/shard_map/pack/pallas_call | solution.py:115
  54.4 1.4 collective-permute-start.39
  56.6 4.5 %collective-permute-done.17.refs_2_ = bf16[8,80,256]{2,1,0:T(8,128)(2,1)S(1)} collective-permute-done((bf16[8,80,256]{2,1,0:T(8,128)(2,1)S(1)}, bf16[8,80,256]{2,1,0:T(8,128)(2,1)S(1)}, u32[]{:S(2)}, u32[]{:S(2)}) %collective-permute-start.17) | collective-permute-done | bytes 327712 | tf_op jit(solution)/shard_map/ppermute | solution.py:202
  61.8 6.3 %collective-permute-done.7.refs_2_ = bf16[8,80,256]{2,1,0:T(8,128)(2,1)S(1)} collective-permute-done((bf16[8,80,256]{2,1,0:T(8,128)(2,1)S(1)}, bf16[8,80,256]{2,1,0:T(8,128)(2,1)S(1)}, u32[]{:S(2)}, u32[]{:S(2)}) %collective-permute-start.7) | collective-permute-done | bytes 327712 | tf_op jit(solution)/shard_map/ppermute | solution.py:202
  68.1 7.0 %collective-permute-done.39.refs_4_ = bf16[8,80,256]{2,1,0:T(8,128)(2,1)S(1)} collective-permute-done((bf16[8,80,256]{2,1,0:T(8,128)(2,1)S(1)}, bf16[8,80,256]{2,1,0:T(8,128)(2,1)S(1)}, u32[]{:S(2)}, u32[]{:S(2)}) %collective-permute-start.39) | collective-permute-done | bytes 327712 | tf_op jit(solution)/shard_map/ppermute | solution.py:202
  75.9 6.3 %collective-permute-done.29.refs_4_ = bf16[8,80,256]{2,1,0:T(8,128)(2,1)S(1)} collective-permute-done((bf16[8,80,256]{2,1,0:T(8,128)(2,1)S(1)}, bf16[8,80,256]{2,1,0:T(8,128)(2,1)S(1)}, u32[]{:S(2)}, u32[]{:S(2)}) %collective-permute-start.29) | collective-permute-done | bytes 327712 | tf_op jit(solution)/shard_map/ppermute | solution.py:202
  82.2 0.7 copy-done.8
  83.6 5.6 %collective-permute-done.19.refs_4_ = bf16[8,80,256]{2,1,0:T(8,128)(2,1)} collective-permute-done((bf16[8,80,256]{2,1,0:T(8,128)(2,1)S(1)}, bf16[8,80,256]{2,1,0:T(8,128)(2,1)}, u32[]{:S(2)}, u32[]{:S(2)}) %collective-permute-start.19) | collective-permute-done | bytes 327712 | tf_op jit(solution)/shard_map/ppermute | solution.py:202
  89.3 0.7 copy-done.6
  90.7 5.6 %collective-permute-done.9.refs_4_ = bf16[8,80,256]{2,1,0:T(8,128)(2,1)} collective-permute-done((bf16[8,80,256]{2,1,0:T(8,128)(2,1)S(1)}, bf16[8,80,256]{2,1,0:T(8,128)(2,1)}, u32[]{:S(2)}, u32[]{:S(2)}) %collective-permute-start.9) | collective-permute-done | bytes 327712 | tf_op jit(solution)/shard_map/ppermute | solution.py:202
  96.3 7.0 %collective-permute-done.41.refs_6_ = bf16[8,80,256]{2,1,0:T(8,128)(2,1)} collective-permute-done((bf16[8,80,256]{2,1,0:T(8,128)(2,1)S(1)}, bf16[8,80,256]{2,1,0:T(8,128)(2,1)}, u32[]{:S(2)}, u32[]{:S(2)}) %collective-permute-start.41) | collective-permute-done | bytes 327712 | tf_op jit(solution)/shard_map/ppermute | solution.py:202
  104.0 6.3 %collective-permute-done.31.refs_6_ = bf16[8,80,256]{2,1,0:T(8,128)(2,1)} collective-permute-done((bf16[8,80,256]{2,1,0:T(8,128)(2,1)S(1)}, bf16[8,80,256]{2,1,0:T(8,128)(2,1)}, u32[]{:S(2)}, u32[]{:S(2)}) %collective-permute-start.31) | collective-permute-done | bytes 327712 | tf_op jit(solution)/shard_map/ppermute | solution.py:202
  111.6 5.8 %collective-permute-done.21.refs_6_ = bf16[8,80,256]{2,1,0:T(8,128)(2,1)} collective-permute-done((bf16[8,80,256]{2,1,0:T(8,128)(2,1)}, bf16[8,80,256]{2,1,0:T(8,128)(2,1)}, u32[]{:S(2)}, u32[]{:S(2)}) %collective-permute-start.21) | collective-permute-done | bytes 327712 | tf_op jit(solution)/shard_map/ppermute | solution.py:202
  118.0 6.0 %collective-permute-done.11.refs_6_ = bf16[8,80,256]{2,1,0:T(8,128)(2,1)} collective-permute-done((bf16[8,80,256]{2,1,0:T(8,128)(2,1)}, bf16[8,80,256]{2,1,0:T(8,128)(2,1)}, u32[]{:S(2)}, u32[]{:S(2)}) %collective-permute-start.11) | collective-permute-done | bytes 327712 | tf_op jit(solution)/shard_map/ppermute | solution.py:202
  124.6 1.0 copy-done.13
  125.6 1.0 copy-done.15
  126.5 1.0 copy-done.17
  127.5 1.0 copy-done.19
  128.5 1.0 copy-done.21
  129.5 1.0 copy-done.23
  130.4 1.0 copy-done.25
  131.4 10.4 %pairs.4.refs_8_ = bf16[2,32,256,2048]{3,2,1,0:T(8,128)(2,1)} custom-call(s32[1]{0:T(128)} %bitcast.place_ref, bf16[8,80,256]{2,1,0:T(8,128)(2,1)S(1)} %copy-done.15, bf16[8,80,256]{2,1,0:T(8,128)(2,1)S(1)} %copy-done.13, bf16[8,80,256]{2,1,0:T(8,128)(2,1)S(1)} %copy-done.19, bf16[8,80,256]{2,1,0:T(8,128)(2,1)S(1)} %copy-done.17, ...), custom_call_target="tpu_custom_call" | custom-call | flops 1342177280 | bytes 16777216 | tf_op jit(solution)/shard_map/pairs/pallas_call | solution.py:156
  141.8 10.5 %pairs.5.refs_8_ = bf16[2,32,256,2048]{3,2,1,0:T(8,128)(2,1)} custom-call(s32[1]{0:T(128)} %bitcast.place_ref, bf16[8,80,256]{2,1,0:T(8,128)(2,1)S(1)} %get-tuple-element.45.flipped_ref, bf16[8,80,256]{2,1,0:T(8,128)(2,1)S(1)} %get-tuple-element.46.refs_0_, bf16[8,80,256]{2,1,0:T(8,128)(2,1)S(1)} %collective-permute-done.26.refs_1_, ...), custom_call_target="tpu_custom_call", output_to_operand_aliasing={{}: (10, {})} | custom-call | flops 1342177280 | bytes 16777216 | tf_op jit(solution)/shard_map/pairs/pallas_call | solution.py:156
  152.3 10.6 %pairs.6.refs_8_ = bf16[2,32,256,2048]{3,2,1,0:T(8,128)(2,1)} custom-call(s32[1]{0:T(128)} %bitcast.place_ref, bf16[8,80,256]{2,1,0:T(8,128)(2,1)S(1)} %get-tuple-element.39.flipped_ref, bf16[8,80,256]{2,1,0:T(8,128)(2,1)S(1)} %get-tuple-element.40.refs_0_, bf16[8,80,256]{2,1,0:T(8,128)(2,1)S(1)} %copy-done.3, ...), custom_call_target="tpu_custom_call", output_to_operand_aliasing={{}: (10, {})} | custom-call | flops 1342177280 | bytes 16777216 | tf_op jit(solution)/shard_map/pairs/pallas_call | solution.py:156
  162.9 10.4 %pairs.7 = bf16[2,32,256,2048]{3,2,1,0:T(8,128)(2,1)} custom-call(s32[1]{0:T(128)} %bitcast.place_ref, bf16[8,80,256]{2,1,0:T(8,128)(2,1)S(1)} %get-tuple-element.33.flipped_ref, bf16[8,80,256]{2,1,0:T(8,128)(2,1)S(1)} %get-tuple-element.34.refs_0_, bf16[8,80,256]{2,1,0:T(8,128)(2,1)S(1)} %collective-permute-done.6.refs_1_, ...), custom_call_target="tpu_custom_call", output_to_operand_aliasing={{}: (10, {})} | custom-call | flops 1342177280 | bytes 16777216 | tf_op jit(solution)/shard_map/pairs/pallas_call | solution.py:156
  (101 shorter events, 10.5 us)
Async XLA Ops:
  10.3 15.9 %collective-permute-start.33 = (bf16[16,16,256]{2,1,0:T(8,128)(2,1)S(1)}, bf16[16,16,256]{2,1,0:T(8,128)(2,1)S(1)}, u32[]{:S(2)}, u32[]{:S(2)}) collective-permute-start(bf16[16,16,256]{2,1,0:T(8,128)(2,1)S(1)} %get-tuple-element.48), channel_id=1, source_target_pairs={{0,1},{1,0},{2,3},{3,2},{4,5},{5,4},{6,7},{7,6},{8,9},{9,8},{10,11... | collective-permute-start | bytes 393224 | tf_op jit(solution)/shard_map/ppermute | solution.py:191
  13.3 14.3 %collective-permute-start.34 = (bf16[16,16,256]{2,1,0:T(8,128)(2,1)S(1)}, bf16[16,16,256]{2,1,0:T(8,128)(2,1)S(1)}, u32[]{:S(2)}, u32[]{:S(2)}) collective-permute-start(bf16[16,16,256]{2,1,0:T(8,128)(2,1)S(1)} %get-tuple-element.49), channel_id=1, source_target_pairs={{0,2},{1,3},{2,0},{3,1},{4,6},{5,7},{6,4},{7,5},{8,10},{9,11},{10,... | collective-permute-start | bytes 393224 | tf_op jit(solution)/shard_map/ppermute | solution.py:191
  14.8 13.2 %collective-permute-start.35 = (bf16[16,16,256]{2,1,0:T(8,128)(2,1)S(1)}, bf16[16,16,256]{2,1,0:T(8,128)(2,1)S(1)}, u32[]{:S(2)}, u32[]{:S(2)}) collective-permute-start(bf16[16,16,256]{2,1,0:T(8,128)(2,1)S(1)} %get-tuple-element.50), channel_id=1, source_target_pairs={{0,3},{1,2},{2,1},{3,0},{4,7},{5,6},{6,5},{7,4},{8,11},{9,10},{10,... | collective-permute-start | bytes 393224 | tf_op jit(solution)/shard_map/ppermute | solution.py:191
  14.8 5.0 %collective-permute-start = (s32[1]{0:T(128)}, s32[1]{0:T(128)}, u32[]{:S(2)}, u32[]{:S(2)}) collective-permute-start(s32[1]{0:T(128)} %param.6), channel_id=1, source_target_pairs={{0,1},{1,0},{2,3},{3,2},{4,5},{5,4},{6,7},{7,6},{8,9},{9,8},{10,11... | collective-permute-start | bytes 20 | tf_op jit(solution)/shard_map/ppermute | solution.py:186
  16.8 5.6 %collective-permute-start.1 = (s32[1]{0:T(128)}, s32[1]{0:T(128)}, u32[]{:S(2)}, u32[]{:S(2)}) collective-permute-start(s32[1]{0:T(128)} %param.6), channel_id=1, source_target_pairs={{0,2},{1,3},{2,0},{3,1},{4,6},{5,7},{6,4},{7,5},{8,10},{9,11},{10,... | collective-permute-start | bytes 20 | tf_op jit(solution)/shard_map/ppermute | solution.py:186
  19.8 4.7 %collective-permute-start.2 = (s32[1]{0:T(128)}, s32[1]{0:T(128)}, u32[]{:S(2)}, u32[]{:S(2)}) collective-permute-start(s32[1]{0:T(128)} %param.6), channel_id=1, source_target_pairs={{0,3},{1,2},{2,1},{3,0},{4,7},{5,6},{6,5},{7,4},{8,11},{9,10},{10,... | collective-permute-start | bytes 20 | tf_op jit(solution)/shard_map/ppermute | solution.py:186
  22.4 10.0 %collective-permute-start.23 = (bf16[16,16,256]{2,1,0:T(8,128)(2,1)S(1)}, bf16[16,16,256]{2,1,0:T(8,128)(2,1)S(1)}, u32[]{:S(2)}, u32[]{:S(2)}) collective-permute-start(bf16[16,16,256]{2,1,0:T(8,128)(2,1)S(1)} %get-tuple-element.42), channel_id=1, source_target_pairs={{0,1},{1,0},{2,3},{3,2},{4,5},{5,4},{6,7},{7,6},{8,9},{9,8},{10,11... | collective-permute-start | bytes 393224 | tf_op jit(solution)/shard_map/ppermute | solution.py:191
  24.5 9.4 %collective-permute-start.24 = (bf16[16,16,256]{2,1,0:T(8,128)(2,1)S(1)}, bf16[16,16,256]{2,1,0:T(8,128)(2,1)S(1)}, u32[]{:S(2)}, u32[]{:S(2)}) collective-permute-start(bf16[16,16,256]{2,1,0:T(8,128)(2,1)S(1)} %get-tuple-element.43), channel_id=1, source_target_pairs={{0,2},{1,3},{2,0},{3,1},{4,6},{5,7},{6,4},{7,5},{8,10},{9,11},{10,... | collective-permute-start | bytes 393224 | tf_op jit(solution)/shard_map/ppermute | solution.py:191
  26.2 8.1 %collective-permute-start.25 = (bf16[16,16,256]{2,1,0:T(8,128)(2,1)S(1)}, bf16[16,16,256]{2,1,0:T(8,128)(2,1)S(1)}, u32[]{:S(2)}, u32[]{:S(2)}) collective-permute-start(bf16[16,16,256]{2,1,0:T(8,128)(2,1)S(1)} %get-tuple-element.44), channel_id=1, source_target_pairs={{0,3},{1,2},{2,1},{3,0},{4,7},{5,6},{6,5},{7,4},{8,11},{9,10},{10,... | collective-permute-start | bytes 393224 | tf_op jit(solution)/shard_map/ppermute | solution.py:191
  27.6 11.0 %collective-permute-start.13 = (bf16[16,16,256]{2,1,0:T(8,128)(2,1)S(1)}, bf16[16,16,256]{2,1,0:T(8,128)(2,1)S(1)}, u32[]{:S(2)}, u32[]{:S(2)}) collective-permute-start(bf16[16,16,256]{2,1,0:T(8,128)(2,1)S(1)} %get-tuple-element.36), channel_id=1, source_target_pairs={{0,1},{1,0},{2,3},{3,2},{4,5},{5,4},{6,7},{7,6},{8,9},{9,8},{10,11... | collective-permute-start | bytes 393224 | tf_op jit(solution)/shard_map/ppermute | solution.py:191
  28.0 10.7 %collective-permute-start.14 = (bf16[16,16,256]{2,1,0:T(8,128)(2,1)S(1)}, bf16[16,16,256]{2,1,0:T(8,128)(2,1)S(1)}, u32[]{:S(2)}, u32[]{:S(2)}) collective-permute-start(bf16[16,16,256]{2,1,0:T(8,128)(2,1)S(1)} %get-tuple-element.37), channel_id=1, source_target_pairs={{0,2},{1,3},{2,0},{3,1},{4,6},{5,7},{6,4},{7,5},{8,10},{9,11},{10,... | collective-permute-start | bytes 393224 | tf_op jit(solution)/shard_map/ppermute | solution.py:191
  32.4 78.0 %copy-start.12 = (bf16[8,80,256]{2,1,0:T(8,128)(2,1)}, bf16[8,80,256]{2,1,0:T(8,128)(2,1)S(1)}, u32[]{:S(2)}) copy-start(bf16[8,80,256]{2,1,0:T(8,128)(2,1)S(1)} %get-tuple-element.52.refs_0_) | copy-start | bytes 983044
  32.4 79.2 %copy-start.14 = (bf16[8,80,256]{2,1,0:T(8,128)(2,1)}, bf16[8,80,256]{2,1,0:T(8,128)(2,1)S(1)}, u32[]{:S(2)}) copy-start(bf16[8,80,256]{2,1,0:T(8,128)(2,1)S(1)} %get-tuple-element.51.flipped_ref) | copy-start | bytes 983044
  32.4 8.0 %collective-permute-start.15 = (bf16[16,16,256]{2,1,0:T(8,128)(2,1)S(1)}, bf16[16,16,256]{2,1,0:T(8,128)(2,1)S(1)}, u32[]{:S(2)}, u32[]{:S(2)}) collective-permute-start(bf16[16,16,256]{2,1,0:T(8,128)(2,1)S(1)} %get-tuple-element.38), channel_id=1, source_target_pairs={{0,3},{1,2},{2,1},{3,0},{4,7},{5,6},{6,5},{7,4},{8,11},{9,10},{10,... | collective-permute-start | bytes 393224 | tf_op jit(solution)/shard_map/ppermute | solution.py:191
  33.9 8.0 %collective-permute-start.3 = (bf16[16,16,256]{2,1,0:T(8,128)(2,1)S(1)}, bf16[16,16,256]{2,1,0:T(8,128)(2,1)S(1)}, u32[]{:S(2)}, u32[]{:S(2)}) collective-permute-start(bf16[16,16,256]{2,1,0:T(8,128)(2,1)S(1)} %get-tuple-element.30), channel_id=1, source_target_pairs={{0,1},{1,0},{2,3},{3,2},{4,5},{5,4},{6,7},{7,6},{8,9},{9,8},{10,11... | collective-permute-start | bytes 393224 | tf_op jit(solution)/shard_map/ppermute | solution.py:191
  34.3 18.7 %collective-permute-start.37 = (bf16[8,80,256]{2,1,0:T(8,128)(2,1)S(1)}, bf16[8,80,256]{2,1,0:T(8,128)(2,1)S(1)}, u32[]{:S(2)}, u32[]{:S(2)}) collective-permute-start(bf16[8,80,256]{2,1,0:T(8,128)(2,1)S(1)} %get-tuple-element.52.refs_0_), channel_id=1, source_target_pairs={{0,8},{4,12},{8,16},{12,20},{16,24},{20,28},{24,0},{28,4},{1,9},{5... | collective-permute-start | bytes 983048 | tf_op jit(solution)/shard_map/ppermute | solution.py:202
  38.7 14.6 %collective-permute-start.36 = (bf16[8,80,256]{2,1,0:T(8,128)(2,1)S(1)}, bf16[8,80,256]{2,1,0:T(8,128)(2,1)S(1)}, u32[]{:S(2)}, u32[]{:S(2)}) collective-permute-start(bf16[8,80,256]{2,1,0:T(8,128)(2,1)S(1)} %get-tuple-element.52.refs_0_), channel_id=1, source_target_pairs={{0,4},{4,0},{8,12},{12,8},{16,20},{20,16},{24,28},{28,24},{1,5},{5... | collective-permute-start | bytes 983048 | tf_op jit(solution)/shard_map/ppermute | solution.py:200
  38.8 15.7 %collective-permute-start.27 = (bf16[8,80,256]{2,1,0:T(8,128)(2,1)S(1)}, bf16[8,80,256]{2,1,0:T(8,128)(2,1)S(1)}, u32[]{:S(2)}, u32[]{:S(2)}) collective-permute-start(bf16[8,80,256]{2,1,0:T(8,128)(2,1)S(1)} %get-tuple-element.46.refs_0_), channel_id=1, source_target_pairs={{0,8},{4,12},{8,16},{12,20},{16,24},{20,28},{24,0},{28,4},{1,9},{5... | collective-permute-start | bytes 983048 | tf_op jit(solution)/shard_map/ppermute | solution.py:202
  40.4 8.4 %collective-permute-start.4 = (bf16[16,16,256]{2,1,0:T(8,128)(2,1)S(1)}, bf16[16,16,256]{2,1,0:T(8,128)(2,1)S(1)}, u32[]{:S(2)}, u32[]{:S(2)}) collective-permute-start(bf16[16,16,256]{2,1,0:T(8,128)(2,1)S(1)} %get-tuple-element.31), channel_id=1, source_target_pairs={{0,2},{1,3},{2,0},{3,1},{4,6},{5,7},{6,4},{7,5},{8,10},{9,11},{10,... | collective-permute-start | bytes 393224 | tf_op jit(solution)/shard_map/ppermute | solution.py:191
  41.9 6.9 %collective-permute-start.5 = (bf16[16,16,256]{2,1,0:T(8,128)(2,1)S(1)}, bf16[16,16,256]{2,1,0:T(8,128)(2,1)S(1)}, u32[]{:S(2)}, u32[]{:S(2)}) collective-permute-start(bf16[16,16,256]{2,1,0:T(8,128)(2,1)S(1)} %get-tuple-element.32), channel_id=1, source_target_pairs={{0,3},{1,2},{2,1},{3,0},{4,7},{5,6},{6,5},{7,4},{8,11},{9,10},{10,... | collective-permute-start | bytes 393224 | tf_op jit(solution)/shard_map/ppermute | solution.py:191
  48.8 7.1 %collective-permute-start.26 = (bf16[8,80,256]{2,1,0:T(8,128)(2,1)S(1)}, bf16[8,80,256]{2,1,0:T(8,128)(2,1)S(1)}, u32[]{:S(2)}, u32[]{:S(2)}) collective-permute-start(bf16[8,80,256]{2,1,0:T(8,128)(2,1)S(1)} %get-tuple-element.46.refs_0_), channel_id=1, source_target_pairs={{0,4},{4,0},{8,12},{12,8},{16,20},{20,16},{24,28},{28,24},{1,5},{5... | collective-permute-start | bytes 983048 | tf_op jit(solution)/shard_map/ppermute | solution.py:200
  48.8 12.3 %collective-permute-start.17 = (bf16[8,80,256]{2,1,0:T(8,128)(2,1)S(1)}, bf16[8,80,256]{2,1,0:T(8,128)(2,1)S(1)}, u32[]{:S(2)}, u32[]{:S(2)}) collective-permute-start(bf16[8,80,256]{2,1,0:T(8,128)(2,1)S(1)} %get-tuple-element.40.refs_0_), channel_id=1, source_target_pairs={{0,8},{4,12},{8,16},{12,20},{16,24},{20,28},{24,0},{28,4},{1,9},{5... | collective-permute-start | bytes 983048 | tf_op jit(solution)/shard_map/ppermute | solution.py:202
  53.0 8.1 %collective-permute-start.16 = (bf16[8,80,256]{2,1,0:T(8,128)(2,1)S(1)}, bf16[8,80,256]{2,1,0:T(8,128)(2,1)S(1)}, u32[]{:S(2)}, u32[]{:S(2)}) collective-permute-start(bf16[8,80,256]{2,1,0:T(8,128)(2,1)S(1)} %get-tuple-element.40.refs_0_), channel_id=1, source_target_pairs={{0,4},{4,0},{8,12},{12,8},{16,20},{20,16},{24,28},{28,24},{1,5},{5... | collective-permute-start | bytes 983048 | tf_op jit(solution)/shard_map/ppermute | solution.py:200
  54.0 14.1 %collective-permute-start.7 = (bf16[8,80,256]{2,1,0:T(8,128)(2,1)S(1)}, bf16[8,80,256]{2,1,0:T(8,128)(2,1)S(1)}, u32[]{:S(2)}, u32[]{:S(2)}) collective-permute-start(bf16[8,80,256]{2,1,0:T(8,128)(2,1)S(1)} %get-tuple-element.34.refs_0_), channel_id=1, source_target_pairs={{0,8},{4,12},{8,16},{12,20},{16,24},{20,28},{24,0},{28,4},{1,9},{5... | collective-permute-start | bytes 983048 | tf_op jit(solution)/shard_map/ppermute | solution.py:202
  54.4 20.7 %collective-permute-start.39 = (bf16[8,80,256]{2,1,0:T(8,128)(2,1)S(1)}, bf16[8,80,256]{2,1,0:T(8,128)(2,1)S(1)}, u32[]{:S(2)}, u32[]{:S(2)}) collective-permute-start(bf16[8,80,256]{2,1,0:T(8,128)(2,1)S(1)} %collective-permute-done.37.refs_2_), channel_id=1, source_target_pairs={{0,8},{4,12},{8,16},{12,20},{16,24},{20,28},{24,0},{28,4},{1,9},{5... | collective-permute-start | bytes 983048 | tf_op jit(solution)/shard_map/ppermute | solution.py:202
  55.8 19.3 %collective-permute-start.38 = (bf16[8,80,256]{2,1,0:T(8,128)(2,1)S(1)}, bf16[8,80,256]{2,1,0:T(8,128)(2,1)S(1)}, u32[]{:S(2)}, u32[]{:S(2)}) collective-permute-start(bf16[8,80,256]{2,1,0:T(8,128)(2,1)S(1)} %collective-permute-done.37.refs_2_), channel_id=1, source_target_pairs={{0,4},{4,0},{8,12},{12,8},{16,20},{20,16},{24,28},{28,24},{1,5},{5... | collective-permute-start | bytes 983048 | tf_op jit(solution)/shard_map/ppermute | solution.py:200
  61.1 21.1 %collective-permute-start.29 = (bf16[8,80,256]{2,1,0:T(8,128)(2,1)S(1)}, bf16[8,80,256]{2,1,0:T(8,128)(2,1)S(1)}, u32[]{:S(2)}, u32[]{:S(2)}) collective-permute-start(bf16[8,80,256]{2,1,0:T(8,128)(2,1)S(1)} %collective-permute-done.27.refs_2_), channel_id=1, source_target_pairs={{0,8},{4,12},{8,16},{12,20},{16,24},{20,28},{24,0},{28,4},{1,9},{5... | collective-permute-start | bytes 983048 | tf_op jit(solution)/shard_map/ppermute | solution.py:202
  61.8 20.3 %collective-permute-start.28 = (bf16[8,80,256]{2,1,0:T(8,128)(2,1)S(1)}, bf16[8,80,256]{2,1,0:T(8,128)(2,1)S(1)}, u32[]{:S(2)}, u32[]{:S(2)}) collective-permute-start(bf16[8,80,256]{2,1,0:T(8,128)(2,1)S(1)} %collective-permute-done.27.refs_2_), channel_id=1, source_target_pairs={{0,4},{4,0},{8,12},{12,8},{16,20},{20,16},{24,28},{28,24},{1,5},{5... | collective-permute-start | bytes 983048 | tf_op jit(solution)/shard_map/ppermute | solution.py:200
  68.1 21.2 %collective-permute-start.19 = (bf16[8,80,256]{2,1,0:T(8,128)(2,1)S(1)}, bf16[8,80,256]{2,1,0:T(8,128)(2,1)}, u32[]{:S(2)}, u32[]{:S(2)}) collective-permute-start(bf16[8,80,256]{2,1,0:T(8,128)(2,1)S(1)} %collective-permute-done.17.refs_2_), channel_id=1, source_target_pairs={{0,8},{4,12},{8,16},{12,20},{16,24},{20,28},{24,0},{28,4},{1,9},{5... | collective-permute-start | bytes 983048 | tf_op jit(solution)/shard_map/ppermute | solution.py:202
  75.1 14.2 %collective-permute-start.18 = (bf16[8,80,256]{2,1,0:T(8,128)(2,1)S(1)}, bf16[8,80,256]{2,1,0:T(8,128)(2,1)S(1)}, u32[]{:S(2)}, u32[]{:S(2)}) collective-permute-start(bf16[8,80,256]{2,1,0:T(8,128)(2,1)S(1)} %collective-permute-done.17.refs_2_), channel_id=1, source_target_pairs={{0,4},{4,0},{8,12},{12,8},{16,20},{20,16},{24,28},{28,24},{1,5},{5... | collective-permute-start | bytes 983048 | tf_op jit(solution)/shard_map/ppermute | solution.py:200
  75.9 20.4 %collective-permute-start.9 = (bf16[8,80,256]{2,1,0:T(8,128)(2,1)S(1)}, bf16[8,80,256]{2,1,0:T(8,128)(2,1)}, u32[]{:S(2)}, u32[]{:S(2)}) collective-permute-start(bf16[8,80,256]{2,1,0:T(8,128)(2,1)S(1)} %collective-permute-done.7.refs_2_), channel_id=1, source_target_pairs={{0,8},{4,12},{8,16},{12,20},{16,24},{20,28},{24,0},{28,4},{1,9},{5... | collective-permute-start | bytes 983048 | tf_op jit(solution)/shard_map/ppermute | solution.py:202
  82.2 21.2 %collective-permute-start.41 = (bf16[8,80,256]{2,1,0:T(8,128)(2,1)S(1)}, bf16[8,80,256]{2,1,0:T(8,128)(2,1)}, u32[]{:S(2)}, u32[]{:S(2)}) collective-permute-start(bf16[8,80,256]{2,1,0:T(8,128)(2,1)S(1)} %collective-permute-done.39.refs_4_), channel_id=1, source_target_pairs={{0,8},{4,12},{8,16},{12,20},{16,24},{20,28},{24,0},{28,4},{1,9},{5... | collective-permute-start | bytes 983048 | tf_op jit(solution)/shard_map/ppermute | solution.py:202
  82.9 20.4 %collective-permute-start.40 = (bf16[8,80,256]{2,1,0:T(8,128)(2,1)S(1)}, bf16[8,80,256]{2,1,0:T(8,128)(2,1)S(1)}, u32[]{:S(2)}, u32[]{:S(2)}) collective-permute-start(bf16[8,80,256]{2,1,0:T(8,128)(2,1)S(1)} %collective-permute-done.39.refs_4_), channel_id=1, source_target_pairs={{0,4},{4,0},{8,12},{12,8},{16,20},{20,16},{24,28},{28,24},{1,5},{5... | collective-permute-start | bytes 983048 | tf_op jit(solution)/shard_map/ppermute | solution.py:200
  89.3 21.1 %collective-permute-start.31 = (bf16[8,80,256]{2,1,0:T(8,128)(2,1)S(1)}, bf16[8,80,256]{2,1,0:T(8,128)(2,1)}, u32[]{:S(2)}, u32[]{:S(2)}) collective-permute-start(bf16[8,80,256]{2,1,0:T(8,128)(2,1)S(1)} %collective-permute-done.29.refs_4_), channel_id=1, source_target_pairs={{0,8},{4,12},{8,16},{12,20},{16,24},{20,28},{24,0},{28,4},{1,9},{5... | collective-permute-start | bytes 983048 | tf_op jit(solution)/shard_map/ppermute | solution.py:202
  90.0 20.3 %collective-permute-start.30 = (bf16[8,80,256]{2,1,0:T(8,128)(2,1)S(1)}, bf16[8,80,256]{2,1,0:T(8,128)(2,1)S(1)}, u32[]{:S(2)}, u32[]{:S(2)}) collective-permute-start(bf16[8,80,256]{2,1,0:T(8,128)(2,1)S(1)} %collective-permute-done.29.refs_4_), channel_id=1, source_target_pairs={{0,4},{4,0},{8,12},{12,8},{16,20},{20,16},{24,28},{28,24},{1,5},{5... | collective-permute-start | bytes 983048 | tf_op jit(solution)/shard_map/ppermute | solution.py:200
  96.3 21.1 %collective-permute-start.21 = (bf16[8,80,256]{2,1,0:T(8,128)(2,1)}, bf16[8,80,256]{2,1,0:T(8,128)(2,1)}, u32[]{:S(2)}, u32[]{:S(2)}) collective-permute-start(bf16[8,80,256]{2,1,0:T(8,128)(2,1)} %collective-permute-done.19.refs_4_), channel_id=1, source_target_pairs={{0,8},{4,12},{8,16},{12,20},{16,24},{20,28},{24,0},{28,4},{1,9},{5... | collective-permute-start | bytes 983048 | tf_op jit(solution)/shard_map/ppermute | solution.py:202
  103.3 14.1 %collective-permute-start.20 = (bf16[8,80,256]{2,1,0:T(8,128)(2,1)}, bf16[8,80,256]{2,1,0:T(8,128)(2,1)}, u32[]{:S(2)}, u32[]{:S(2)}) collective-permute-start(bf16[8,80,256]{2,1,0:T(8,128)(2,1)} %collective-permute-done.19.refs_4_), channel_id=1, source_target_pairs={{0,4},{4,0},{8,12},{12,8},{16,20},{20,16},{24,28},{28,24},{1,5},{5... | collective-permute-start | bytes 983048 | tf_op jit(solution)/shard_map/ppermute | solution.py:200
  104.0 20.0 %collective-permute-start.11 = (bf16[8,80,256]{2,1,0:T(8,128)(2,1)}, bf16[8,80,256]{2,1,0:T(8,128)(2,1)}, u32[]{:S(2)}, u32[]{:S(2)}) collective-permute-start(bf16[8,80,256]{2,1,0:T(8,128)(2,1)} %collective-permute-done.9.refs_4_), channel_id=1, source_target_pairs={{0,8},{4,12},{8,16},{12,20},{16,24},{20,28},{24,0},{28,4},{1,9},{5... | collective-permute-start | bytes 983048 | tf_op jit(solution)/shard_map/ppermute | solution.py:202
  110.3 13.7 %collective-permute-start.42 = (bf16[8,80,256]{2,1,0:T(8,128)(2,1)}, bf16[8,80,256]{2,1,0:T(8,128)(2,1)}, u32[]{:S(2)}, u32[]{:S(2)}) collective-permute-start(bf16[8,80,256]{2,1,0:T(8,128)(2,1)} %collective-permute-done.41.refs_6_), channel_id=1, source_target_pairs={{0,4},{4,0},{8,12},{12,8},{16,20},{20,16},{24,28},{28,24},{1,5},{5... | collective-permute-start | bytes 983048 | tf_op jit(solution)/shard_map/ppermute | solution.py:200
  111.1 13.4 %collective-permute-start.32 = (bf16[8,80,256]{2,1,0:T(8,128)(2,1)}, bf16[8,80,256]{2,1,0:T(8,128)(2,1)}, u32[]{:S(2)}, u32[]{:S(2)}) collective-permute-start(bf16[8,80,256]{2,1,0:T(8,128)(2,1)} %collective-permute-done.31.refs_6_), channel_id=1, source_target_pairs={{0,4},{4,0},{8,12},{12,8},{16,20},{20,16},{24,28},{28,24},{1,5},{5... | collective-permute-start | bytes 983048 | tf_op jit(solution)/shard_map/ppermute | solution.py:200
  117.4 34.9 %collective-permute-start.22 = (bf16[8,80,256]{2,1,0:T(8,128)(2,1)}, bf16[8,80,256]{2,1,0:T(8,128)(2,1)}, u32[]{:S(2)}, u32[]{:S(2)}) collective-permute-start(bf16[8,80,256]{2,1,0:T(8,128)(2,1)} %collective-permute-done.21.refs_6_), channel_id=1, source_target_pairs={{0,4},{4,0},{8,12},{12,8},{16,20},{20,16},{24,28},{28,24},{1,5},{5... | collective-permute-start | bytes 983048 | tf_op jit(solution)/shard_map/ppermute | solution.py:200
  117.4 24.4 %copy-start.5 = (bf16[8,80,256]{2,1,0:T(8,128)(2,1)S(1)}, bf16[8,80,256]{2,1,0:T(8,128)(2,1)}, u32[]{:S(2)}) copy-start(bf16[8,80,256]{2,1,0:T(8,128)(2,1)} %copy-done.4) | copy-start | bytes 983044
  117.4 24.4 %copy-start.9 = (bf16[8,80,256]{2,1,0:T(8,128)(2,1)S(1)}, bf16[8,80,256]{2,1,0:T(8,128)(2,1)}, u32[]{:S(2)}) copy-start(bf16[8,80,256]{2,1,0:T(8,128)(2,1)} %copy-done.8) | copy-start | bytes 983044
  117.4 24.4 %copy-start.11 = (bf16[8,80,256]{2,1,0:T(8,128)(2,1)S(1)}, bf16[8,80,256]{2,1,0:T(8,128)(2,1)}, u32[]{:S(2)}) copy-start(bf16[8,80,256]{2,1,0:T(8,128)(2,1)} %copy-done.10) | copy-start | bytes 983044
  117.4 45.5 %collective-permute-start.6 = (bf16[8,80,256]{2,1,0:T(8,128)(2,1)S(1)}, bf16[8,80,256]{2,1,0:T(8,128)(2,1)S(1)}, u32[]{:S(2)}, u32[]{:S(2)}) collective-permute-start(bf16[8,80,256]{2,1,0:T(8,128)(2,1)S(1)} %get-tuple-element.34.refs_0_), channel_id=1, source_target_pairs={{0,4},{4,0},{8,12},{12,8},{16,20},{20,16},{24,28},{28,24},{1,5},{5... | collective-permute-start | bytes 983048 | tf_op jit(solution)/shard_map/ppermute | solution.py:200
  124.0 38.9 %collective-permute-start.8 = (bf16[8,80,256]{2,1,0:T(8,128)(2,1)S(1)}, bf16[8,80,256]{2,1,0:T(8,128)(2,1)S(1)}, u32[]{:S(2)}, u32[]{:S(2)}) collective-permute-start(bf16[8,80,256]{2,1,0:T(8,128)(2,1)S(1)} %collective-permute-done.7.refs_2_), channel_id=1, source_target_pairs={{0,4},{4,0},{8,12},{12,8},{16,20},{20,16},{24,28},{28,24},{1,5},{5... | collective-permute-start | bytes 983048 | tf_op jit(solution)/shard_map/ppermute | solution.py:200
  124.0 38.9 %collective-permute-start.10 = (bf16[8,80,256]{2,1,0:T(8,128)(2,1)}, bf16[8,80,256]{2,1,0:T(8,128)(2,1)S(1)}, u32[]{:S(2)}, u32[]{:S(2)}) collective-permute-start(bf16[8,80,256]{2,1,0:T(8,128)(2,1)} %collective-permute-done.9.refs_4_), channel_id=1, source_target_pairs={{0,4},{4,0},{8,12},{12,8},{16,20},{20,16},{24,28},{28,24},{1,5},{5... | collective-permute-start | bytes 983048 | tf_op jit(solution)/shard_map/ppermute | solution.py:200
  124.5 38.4 %collective-permute-start.12 = (bf16[8,80,256]{2,1,0:T(8,128)(2,1)}, bf16[8,80,256]{2,1,0:T(8,128)(2,1)S(1)}, u32[]{:S(2)}, u32[]{:S(2)}) collective-permute-start(bf16[8,80,256]{2,1,0:T(8,128)(2,1)} %collective-permute-done.11.refs_6_), channel_id=1, source_target_pairs={{0,4},{4,0},{8,12},{12,8},{16,20},{20,16},{24,28},{28,24},{1,5},{5... | collective-permute-start | bytes 983048 | tf_op jit(solution)/shard_map/ppermute | solution.py:200
  (22 other events, 40.3 us)

commit v2 on v0

v2 whole, which is shorter than its diff:
```python
import functools
import math

import jax
import jax.numpy as jnp
import ml_dtypes
import numpy as np
from jax import lax
from jax.experimental import pallas as pl
from jax.experimental.pallas import tpu as pltpu
from jax.sharding import PartitionSpec as P

FREQS = 128
FIRST_BIN = 64
EPSILON = 1e-06
PART_BINS = 8
CHUNK_PARTS = {4: [2, 2]}
RING = [(0, 1), (1, 1), (0, 2), (1, 2), (0, 3), (1, 3)]
DEPTH = 2
UNROLL = 4
AHEAD = 8
VMEM_LIMIT = 24 << 20
SPECTRA_VMEM = 48 << 20


def transform_table(nodes, chunk_bins, samples):
    sample_index = np.arange(samples, dtype=np.int64)[None, :]
    bin_index = (FIRST_BIN + np.arange(FREQS, dtype=np.int64))[:, None]
    angles = (bin_index * sample_index % samples).astype(np.float64) * (2.0 * math.pi / samples)
    parts = np.stack([np.cos(angles), -np.sin(angles)]).astype(np.float32).astype(ml_dtypes.bfloat16)
    return parts.reshape(2, nodes, -1, chunk_bins, samples).transpose(1, 2, 0, 3, 4).reshape(nodes, -1, samples)


def spectra_kernel(nodes, me_ref, count_ref, seg_hbm, avail_hbm, table_hbm, *refs):
    pieces = refs[:-6]
    seg_ref, avail_ref, table, table_sem, avail_sem, seg_sem = refs[-6:]
    slots = seg_ref.shape[0]
    height = table_hbm.shape[1]
    copies = [
        pltpu.make_async_copy(table_hbm.at[me_ref[0] ^ d], table.at[pl.ds(d * height, height)], table_sem.at[d])
        for d in range(nodes)
    ]
    copies.append(pltpu.make_async_copy(avail_hbm, avail_ref, avail_sem))

    def segment(w):
        return pltpu.make_async_copy(seg_hbm.at[w], seg_ref.at[w], seg_sem.at[w])

    for copy in copies:
        copy.start()
    for w in range(AHEAD):
        segment(w).start()
    for piece in pieces:
        piece[slots] = jnp.full(piece.shape[1:], count_ref[0], jnp.int32).astype(jnp.bfloat16)
    for copy in copies:
        copy.wait()

    def transform(w):
        raw = lax.dot_general(
            table[...], seg_ref[w], (((1,), (1,)), ((), ())), preferred_element_type=jnp.float32
        )
        live = jnp.where(w < count_ref[0], avail_ref[pl.ds(w, 1), :], 0).astype(jnp.float32)
        spectra = (raw * live).astype(jnp.bfloat16).astype(jnp.float32)
        energy = jnp.sum(spectra * spectra, axis=0, keepdims=True) / FREQS
        whitened = (spectra * lax.rsqrt(energy + EPSILON)).astype(jnp.bfloat16)
        low = 0
        for d in range(nodes):
            for piece in pieces[d::nodes]:
                high = low + piece.shape[1]
                piece[w] = whitened[low:high]
                low = high

    @pl.loop(0, slots, step=UNROLL)
    def _(w):
        for k in range(UNROLL):
            @pl.when(w + k + AHEAD < slots)
            def _():
                segment(w + k + AHEAD).start()
        for k in range(UNROLL):
            segment(w + k).wait()
        for k in range(UNROLL):
            transform(w + k)


def spectra_pieces(me, node_windows, segments, available, table, sizes):
    slots, chan, samples = segments.shape
    nodes = table.shape[0]
    pieces = [jax.ShapeDtypeStruct((slots + 1, size, chan), jnp.bfloat16) for size in sizes for _ in range(nodes)]
    hbm = pl.BlockSpec(memory_space=pltpu.HBM)
    smem = pl.BlockSpec(memory_space=pltpu.SMEM)
    out = pl.pallas_call(
        functools.partial(spectra_kernel, nodes),
        in_specs=[smem, smem, hbm, hbm, hbm],
        out_specs=[pl.BlockSpec(memory_space=pltpu.VMEM)] * len(pieces),
        out_shape=pieces,
        scratch_shapes=[
            pltpu.VMEM(segments.shape, jnp.bfloat16),
            pltpu.VMEM(available.shape, jnp.int32),
            pltpu.VMEM((2 * FREQS, samples), jnp.bfloat16),
            pltpu.SemaphoreType.DMA((nodes,)),
            pltpu.SemaphoreType.DMA,
            pltpu.SemaphoreType.DMA((slots,)),
        ],
        compiler_params=pltpu.CompilerParams(vmem_limit_bytes=SPECTRA_VMEM),
        cost_estimate=pl.CostEstimate(
            flops=2 * slots * chan * samples * 2 * FREQS, bytes_accessed=2 * slots * chan * samples, transcendentals=0
        ),
        name="spectra",
    )(me, node_windows, segments, available, table)
    return [list(out[g * nodes:(g + 1) * nodes]) for g in range(len(sizes))]


def pack_kernel(nodes, slots, parts, bins, windows, me_ref, *refs):
    pieces, (packed_ref, again_ref) = refs[:nodes], refs[nodes:]
    me = me_ref[0]
    chan = packed_ref.shape[2]
    out_rows, in_rows = bins * 2 * windows, slots * 2 * bins
    col = lax.broadcasted_iota(jnp.int32, (1, in_rows), 1)
    slot, half, fbin = col // (2 * bins), (col // bins) % 2, col % bins
    row = lax.broadcasted_iota(jnp.int32, (out_rows, in_rows), 0)
    counts = [piece[slots].astype(jnp.float32)[0:1, 0:1].astype(jnp.int32) for piece in pieces]
    packed = [jnp.zeros((out_rows, chan), jnp.float32) for _ in range(parts)]
    for d in range(nodes):
        start = jnp.zeros((1, 1), jnp.int32)
        for e in range(nodes):
            start = start + jnp.where((me ^ e) < (me ^ d), counts[e], 0)
        place = jnp.where(slot < counts[d], (fbin * 2 + half) * windows + start + slot, -1)
        select = jnp.where(row == place, 1.0, 0.0).astype(jnp.bfloat16)
        for p in range(parts):
            rows = pieces[d][:slots, p * 2 * bins:(p + 1) * 2 * bins].reshape(in_rows, chan)
            packed[p] += jnp.dot(select, rows, preferred_element_type=jnp.float32)
    for p in range(parts):
        block = packed[p].astype(jnp.bfloat16).reshape(bins, 2 * windows, chan)
        packed_ref[p * bins:(p + 1) * bins] = block
        again_ref[p * bins:(p + 1) * bins] = block


def pack_windows(me, pieces, held, parts, windows):
    slots, chan = pieces[0].shape[0] - 1, pieces[0].shape[2]
    nodes = len(pieces)
    bins = pieces[0].shape[1] // (2 * parts)
    whole = pl.BlockSpec(memory_space=pltpu.VMEM)
    anywhere = pl.BlockSpec(memory_space=pl.ANY)
    packed = jax.ShapeDtypeStruct((parts * bins, 2 * windows, chan), jnp.bfloat16)

    def kernel(me_ref, *refs):
        outs = refs[nodes + len(held):]
        pack_kernel(nodes, slots, parts, bins, windows, me_ref, *refs[:nodes], *outs[:2])

    result = pl.pallas_call(
        kernel,
        in_specs=[pl.BlockSpec(memory_space=pltpu.SMEM)] + [whole] * nodes + [anywhere] * len(held),
        out_specs=[whole] * 2 + [anywhere] * len(held),
        out_shape=[packed] * 2 + [jax.ShapeDtypeStruct(array.shape, array.dtype) for array in held],
        input_output_aliases={1 + nodes + k: 2 + k for k in range(len(held))},
        compiler_params=pltpu.CompilerParams(vmem_limit_bytes=VMEM_LIMIT),
        cost_estimate=pl.CostEstimate(flops=1 << 10, bytes_accessed=1 << 10, transcendentals=0),
        name="pack",
    )(me, *pieces, *held)
    return result[0], result[1], list(result[2:])


def conjugate_rows(block):
    depth, chan = block.shape
    i = lax.broadcasted_iota(jnp.int32, (depth, depth), 0)
    j = lax.broadcasted_iota(jnp.int32, (depth, depth), 1)
    half = depth // 2
    swap = jnp.where(i == j + half, 1.0, jnp.where(j == i + half, -1.0, 0.0)).astype(jnp.bfloat16)
    rows = jnp.transpose(block, (1, 0))
    return rows, jnp.dot(rows, swap, preferred_element_type=jnp.float32).astype(jnp.bfloat16)


def pairs_body(first, scale, place_ref, ours_ref, theirs_ref, *refs):
    out_ref, rows_ref = refs if first else refs[::-1]
    core = place_ref[0] % 2
    count, _, chan = ours_ref.shape
    for b in range(count):
        if first:
            rows_ref[b, :chan], rows_ref[b, chan:] = conjugate_rows(ours_ref[b])
        ours, theirs = ours_ref[b], theirs_ref[b]
        both = jnp.concatenate(
            [jnp.where(core == 0, ours, theirs), jnp.where(core == 0, theirs, ours)], axis=1
        )
        product = jnp.dot(rows_ref[b], both, preferred_element_type=jnp.float32) * scale
        product = product.astype(jnp.bfloat16)
        out_ref[0, b] = product[:chan]
        out_ref[1, b] = product[chan:]


def pair_products(place, ours, theirs, rows, out, held, bins, groups, first_bin, t, scale):
    chunk_bins, depth, chan = ours.shape
    steps = groups // 2
    per_step = math.gcd(math.gcd(chunk_bins, first_bin), 4)
    block = pl.BlockSpec((per_step, depth, chan), lambda i, p: (i, 0, 0))
    rows_spec = pl.BlockSpec((per_step, 2 * chan, depth), lambda i, p: (i, 0, 0))
    anywhere = pl.BlockSpec(memory_space=pl.ANY)
    first = rows is None
    operands, specs = [place, ours, theirs], [block, block]
    if not first:
        operands.append(rows)
        specs.append(rows_spec)
    out_spec = pl.BlockSpec(
        (2, per_step, chan, 2 * chan),
        lambda i, p: (0, first_bin // per_step + i, 0, lax.rem(p[0] // 2 - t + steps, steps)),
    )
    out_specs, out_shape = [], []
    aliases = {}
    if out is not None:
        aliases[len(operands)] = 0
        operands.append(out)
        specs.append(anywhere)
    out_specs.append(out_spec)
    out_shape.append(jax.ShapeDtypeStruct((2, bins, chan, groups * chan), jnp.bfloat16))
    if first:
        out_specs.append(rows_spec)
        out_shape.append(jax.ShapeDtypeStruct((chunk_bins, 2 * chan, depth), jnp.bfloat16))
    for array in held:
        aliases[len(operands)] = len(out_specs)
        operands.append(array)
        specs.append(anywhere)
        out_specs.append(anywhere)
        out_shape.append(jax.ShapeDtypeStruct(array.shape, array.dtype))

    def kernel(place_ref, *refs):
        ins, outs = refs[:len(specs)], refs[len(specs):]
        inner = ins[:2] + (outs[:2] if first else (ins[2], outs[0]))
        pairs_body(first, scale, place_ref, *inner)

    result = pl.pallas_call(
        kernel,
        grid_spec=pltpu.PrefetchScalarGridSpec(
            num_scalar_prefetch=1, grid=(chunk_bins // per_step,), in_specs=specs, out_specs=out_specs
        ),
        out_shape=out_shape,
        input_output_aliases=aliases,
        compiler_params=pltpu.CompilerParams(vmem_limit_bytes=VMEM_LIMIT),
        cost_estimate=pl.CostEstimate(flops=1 << 10, bytes_accessed=1 << 10, transcendentals=0),
        name="pairs",
    )(*operands)
    rows = result[1] if first else rows
    return result[0], rows, result[len(result) - len(held):]


def shards(nodes, groups, segments, available, node_windows):
    slots, chan, samples = segments.shape
    bins = FREQS // nodes
    part_bins = math.gcd(bins, PART_BINS)
    parts = CHUNK_PARTS.get(bins // part_bins, [1] * (bins // part_bins))
    starts = [sum(parts[:c]) * part_bins for c in range(len(parts))]
    chunks = len(parts)
    windows = slots * nodes * 5 // 8
    steps = groups // 2
    me = lax.axis_index("freq").astype(jnp.int32).reshape(1)
    place = lax.axis_index("chan").astype(jnp.int32).reshape(1)
    swap = [[(f, f ^ d) for f in range(nodes)] for d in range(nodes)]
    ring = [(i, (i + 2) % groups) for i in range(groups)]
    cores = [(i, i ^ 1) for i in range(groups)]

    table = jnp.asarray(transform_table(nodes, part_bins, samples))
    pieces = spectra_pieces(
        me, node_windows, segments, available, table, [2 * part_bins * count for count in parts]
    )
    ours, theirs, rows, travelling = {}, {}, {}, {}
    out = None
    scale = 1.0 / windows

    def meet(c, t):
        theirs[c, t] = lax.ppermute(ours[c, t], "chan", cores)

    def send(c, t):
        travelling[c, t] = lax.ppermute(travelling[c, t - 1], "chan", ring)

    def multiply(c, t, held=()):
        nonlocal out
        out, rows[c], kept = pair_products(
            place, ours[c, t], theirs[c, t], rows.get(c), out, list(held), bins, groups, starts[c], t, scale
        )
        return list(kept)

    for c in range(chunks):
        exchanged = [pieces[c][0]] + [lax.ppermute(pieces[c][d], "freq", swap[d]) for d in range(1, nodes)]
        held = pieces[c + 1][-1:] if c + 1 < chunks else []
        travelling[c, 0], ours[c, 0], kept = pack_windows(me, exchanged, held, parts[c], windows)
        if held:
            pieces[c + 1][-1:] = kept

    order = RING if chunks == 2 and steps == 4 else [(c, t) for t in range(1, steps) for c in range(chunks)]
    sent = 0

    def launch(done):
        nonlocal sent
        while sent < len(order) and sent < done + DEPTH:
            c, t = order[sent]
            if t > 1 and order.index((c, t - 1)) >= done:
                return
            send(c, t)
            sent += 1

    launch(0)
    meet(0, 0)
    multiply(0, 0)
    ready = []
    if chunks > 1:
        meet(1, 0)
        ready.append((1, 0))
    for k, now in enumerate(order):
        if ready:
            (travelling[now],) = multiply(*ready.pop(0), [travelling[now]])
        ours[now] = travelling[now]
        launch(k + 1)
        meet(*now)
        ready.append(now)
        if now[1] == 1 and now[0] not in rows and (now[0], 0) not in ready:
            meet(now[0], 0)
            multiply(now[0], 0)
    while ready:
        multiply(*ready.pop(0))
    return out


def solution(mesh):
    placed = (P("freq", "chan", None), P("freq", "chan"), P("freq"))
    return jax.shard_map(
        functools.partial(shards, mesh.shape["freq"], mesh.shape["chan"]),
        mesh=mesh,
        in_specs=placed,
        out_specs=P(None, "freq", "chan", None),
        check_vma=False,
    )
```

time: 337 us -> 128 us (0.38)
  waiting for transfers between devices: 149 us -> 61.7 us
  other arithmetic: 70.6 us -> 0 us
  matrix products: 65.5 us -> 0 us
  Pallas kernels: 0 us -> 48.7 us
  blocking collectives: 30.3 us -> 0 us
  starting transfers between devices: 0.01 us -> 13.9 us
  between operations: 14.1 us -> 0.71 us
  local copies, waits for them, and re-layouts: 7.5 us -> 2.63 us
    all_gather x1 -> x0, waiting for transfers between devices: 149 us -> none  [shards(): lax.all_gather(my_bins, 'chan', axis=3, tiled=True)]
    dot_general x3 -> x0, matrix products: 65.5 us -> none  [the longest x1 29.9 us: pair_products(): jnp.einsum('rfwi,rfwj->fij', rows_block, cols_block, preferred_element_ty...]
    convert_element_type x4 -> x0, other arithmetic: 65.3 us -> none  [the longest x1 63.9 us: pair_products(): (jnp.stack([real_part, imag_part]) * stack_scale).astype(jnp.bfloat16)]
    ppermute x0 -> x20, waiting for transfers between devices: none -> 61.7 us  [the longest x6 43.3 us: send(): travelling[c, t] = lax.ppermute(travelling[c, t - 1], 'chan', ring)]
    pallas_call x0 -> x11, Pallas kernels: none -> 48.7 us  [the longest x8 40.2 us: pair_products(): pl.pallas_call(kernel, grid_spec=pltpu.PrefetchScalarGridSpec(num_scalar_...]
    all_to_all x1 -> x0, blocking collectives: 30.3 us -> none  [shards(): lax.all_to_all(whitened, 'freq', split_axis=1, concat_axis=2, tiled=True)]
    ppermute x0 -> x20, starting transfers between devices: none -> 13.9 us  [the longest x6 9.5 us: shards(): lax.ppermute(pieces[c][d], 'freq', swap[d])]
  transfers between devices with their start and end apart: 1 -> 20, of which waited for: 1 -> 10; matrix products, arithmetic and copies ran while one was open for 1% -> 0% of each run, Pallas kernels for 0% -> 26%
where the time goes in v2:
time: 128 us
  waiting for transfers between devices  61.7 us (48%)
  Pallas kernels  48.7 us (38%)
  starting transfers between devices  13.9 us (11%)
  local copies, waits for them, and re-layouts  2.63 us (2%)
    ppermute x6, waiting for transfers between devices, send(): travelling[c, t] = lax.ppermute(travelling[c, t - 1], 'chan', ring)  43.3 us
    pallas_call x8, Pallas kernels, pair_products(): pl.pallas_call(kernel, grid_spec=pltpu.PrefetchScalarGridSpec(num_scalar_...  40.2 us
    ppermute x6, waiting for transfers between devices, shards(): lax.ppermute(pieces[c][d], 'freq', swap[d])  16.2 us
    ppermute x6, starting transfers between devices, shards(): lax.ppermute(pieces[c][d], 'freq', swap[d])  9.5 us
    pallas_call x1, Pallas kernels, spectra_pieces(): pl.pallas_call(functools.partial(spectra_kernel, nodes), in_specs=[smem,...  5.92 us
    ppermute x6, starting transfers between devices, send(): travelling[c, t] = lax.ppermute(travelling[c, t - 1], 'chan', ring)  4.36 us
    unnamed x6, local copies, waits for them, and re-layouts  2.63 us
    pallas_call x2, Pallas kernels, pack_windows(): pl.pallas_call(kernel, in_specs=[pl.BlockSpec(memory_space=pltpu.SMEM)] +...  2.62 us
  transfers between devices with their start and end apart: 20, of which 10 were waited for; matrix products, arithmetic and copies ran while one was open for 0% of the time, Pallas kernels for 26%

profile of v2, /device:TPU:0, one launch (start us, length us, event | category | flops | bytes accessed | tf_op | source)
XLA Modules:
  0.0 127.6 jit_solution(12057865800717640275)
XLA Ops:
  0.7 0.0 copy-start
  0.7 1.0 copy-done
  1.7 0.7 copy-done.1
  2.4 5.9 %spectra.1 = (bf16[17,32,256]{2,1,0:T(8,128)(2,1)S(1)}, bf16[17,32,256]{2,1,0:T(8,128)(2,1)S(1)}, bf16[17,32,256]{2,1,0:T(8,128)(2,1)S(1)}, bf16[17,32,256]{2,1,...) custom-call(s32[1]{0:T(128)} %bitcast.1.me_ref, ...), custom_call_target="tpu_custom_call" | custom-call | flops 2147483648 | bytes 8388608 | tf_op jit(solution)/shard_map/spectra/pallas_call | solution.py:90
  8.3 3.0 %collective-permute-start.2 = (bf16[17,32,256]{2,1,0:T(8,128)(2,1)S(1)}, bf16[17,32,256]{2,1,0:T(8,128)(2,1)S(1)}, u32[]{:S(2)}, u32[]{:S(2)}) collective-permute-start(bf16[17,32,256]{2,1,0:T(8,128)(2,1)S(1)} %get-tuple-element.37), channel_id=1, source_target_pairs={{0,1},{1,0},{2,3},{3,2},{4,5},{5,4},{6,7},{7,6},{8,9},{9,8},{10,11... | collective-permute-start | bytes 835592 | tf_op jit(solution)/shard_map/ppermute | solution.py:280
  11.3 1.5 %collective-permute-start.3 = (bf16[17,32,256]{2,1,0:T(8,128)(2,1)S(1)}, bf16[17,32,256]{2,1,0:T(8,128)(2,1)S(1)}, u32[]{:S(2)}, u32[]{:S(2)}) collective-permute-start(bf16[17,32,256]{2,1,0:T(8,128)(2,1)S(1)} %get-tuple-element.38), channel_id=1, source_target_pairs={{0,2},{1,3},{2,0},{3,1},{4,6},{5,7},{6,4},{7,5},{8,10},{9,11},{10,... | collective-permute-start | bytes 835592 | tf_op jit(solution)/shard_map/ppermute | solution.py:280
  12.9 0.0 collective-permute-start.4
  12.9 1.9 %collective-permute-start = (bf16[17,32,256]{2,1,0:T(8,128)(2,1)S(1)}, bf16[17,32,256]{2,1,0:T(8,128)(2,1)S(1)}, u32[]{:S(2)}, u32[]{:S(2)}) collective-permute-start(bf16[17,32,256]{2,1,0:T(8,128)(2,1)S(1)} %get-tuple-element.34), channel_id=1, source_target_pairs={{0,1},{1,0},{2,3},{3,2},{4,5},{5,4},{6,7},{7,6},{8,9},{9,8},{10,11... | collective-permute-start | bytes 835592 | tf_op jit(solution)/shard_map/ppermute | solution.py:280
  14.8 1.5 %collective-permute-start.1 = (bf16[17,32,256]{2,1,0:T(8,128)(2,1)S(1)}, bf16[17,32,256]{2,1,0:T(8,128)(2,1)S(1)}, u32[]{:S(2)}, u32[]{:S(2)}) collective-permute-start(bf16[17,32,256]{2,1,0:T(8,128)(2,1)S(1)} %get-tuple-element.35), channel_id=1, source_target_pairs={{0,2},{1,3},{2,0},{3,1},{4,6},{5,7},{6,4},{7,5},{8,10},{9,11},{10,... | collective-permute-start | bytes 835592 | tf_op jit(solution)/shard_map/ppermute | solution.py:280
  16.3 2.5 %collective-permute-done.2.refs_1_ = bf16[17,32,256]{2,1,0:T(8,128)(2,1)S(1)} collective-permute-done((bf16[17,32,256]{2,1,0:T(8,128)(2,1)S(1)}, bf16[17,32,256]{2,1,0:T(8,128)(2,1)S(1)}, u32[]{:S(2)}, u32[]{:S(2)}) %collective-permute-start.2) | collective-permute-done | bytes 278560 | tf_op jit(solution)/shard_map/ppermute | solution.py:280
  18.8 8.1 %collective-permute-done.3.refs_2_ = bf16[17,32,256]{2,1,0:T(8,128)(2,1)S(1)} collective-permute-done((bf16[17,32,256]{2,1,0:T(8,128)(2,1)S(1)}, bf16[17,32,256]{2,1,0:T(8,128)(2,1)S(1)}, u32[]{:S(2)}, u32[]{:S(2)}) %collective-permute-start.3) | collective-permute-done | bytes 278560 | tf_op jit(solution)/shard_map/ppermute | solution.py:280
  26.9 0.0 collective-permute-done.4.refs_3_
  26.9 1.7 %pack.2 = (bf16[16,80,256]{2,1,0:T(8,128)(2,1)}, bf16[16,80,256]{2,1,0:T(8,128)(2,1)S(1)}, bf16[17,32,256]{2,1,0:T(8,128)(2,1)S(1)}) custom-call(s32[1]{0:T(128)} %bitcast.1.me_ref, bf16[17,32,256]{2,1,0:T(8,128)(2,1)S(1)} %get-tuple-element.36.refs_0_, bf16[17,32,256]{2,1,0:T(8,128)(2,1)S(1)} %collective-permute-done.2.refs_1_, ...), custom_call_target="tpu_custom_call", output_to_operand_aliasing={{2}: (5, {})} | custom-call | flops 1024 | bytes 1024 | tf_op jit(solution)/shard_map/pack/pallas_call | solution.py:149
  28.6 1.5 %collective-permute-start.5 = (bf16[17,32,256]{2,1,0:T(8,128)(2,1)S(1)}, bf16[17,32,256]{2,1,0:T(8,128)(2,1)S(1)}, u32[]{:S(2)}, u32[]{:S(2)}) collective-permute-start(bf16[17,32,256]{2,1,0:T(8,128)(2,1)S(1)} %get-tuple-element.41), channel_id=1, source_target_pairs={{0,3},{1,2},{2,1},{3,0},{4,7},{5,6},{6,5},{7,4},{8,11},{9,10},{10,... | collective-permute-start | bytes 835592 | tf_op jit(solution)/shard_map/ppermute | solution.py:280
  30.1 1.6 %collective-permute-start.8 = (bf16[16,80,256]{2,1,0:T(8,128)(2,1)}, bf16[16,80,256]{2,1,0:T(8,128)(2,1)S(1)}, u32[]{:S(2)}, u32[]{:S(2)}) collective-permute-start(bf16[16,80,256]{2,1,0:T(8,128)(2,1)} %get-tuple-element.45), channel_id=1, source_target_pairs={{0,8},{4,12},{8,16},{12,20},{16,24},{20,28},{24,0},{28,4},{1,9},{5... | collective-permute-start | bytes 1966088 | tf_op jit(solution)/shard_map/ppermute | solution.py:270
  31.7 0.0 collective-permute-start.7
  31.7 0.0 collective-permute-done.refs_1_
  31.7 5.7 %collective-permute-done.1.refs_2_ = bf16[17,32,256]{2,1,0:T(8,128)(2,1)S(1)} collective-permute-done((bf16[17,32,256]{2,1,0:T(8,128)(2,1)S(1)}, bf16[17,32,256]{2,1,0:T(8,128)(2,1)S(1)}, u32[]{:S(2)}, u32[]{:S(2)}) %collective-permute-start.1) | collective-permute-done | bytes 278560 | tf_op jit(solution)/shard_map/ppermute | solution.py:280
  37.4 0.0 collective-permute-done.5.refs_3_
  37.4 0.9 pack.3
  38.3 0.9 copy-done.2
  39.2 0.0 collective-permute-start.6
  39.2 1.6 %collective-permute-start.10 = (bf16[16,80,256]{2,1,0:T(8,128)(2,1)}, bf16[16,80,256]{2,1,0:T(8,128)(2,1)S(1)}, u32[]{:S(2)}, u32[]{:S(2)}) collective-permute-start(bf16[16,80,256]{2,1,0:T(8,128)(2,1)} %copy-done.2), channel_id=1, source_target_pairs={{0,8},{4,12},{8,16},{12,20},{16,24},{20,28},{24,0},{28,4},{1,9},{5... | collective-permute-start | bytes 1966088 | tf_op jit(solution)/shard_map/ppermute | solution.py:270
  40.7 0.0 collective-permute-done.7.refs_1_
  40.7 5.8 %pairs.8 = (bf16[2,32,256,2048]{3,2,1,0:T(8,128)(2,1)}, bf16[16,512,80]{2,1,0:T(8,128)(2,1)S(1)}) custom-call(s32[1]{0:T(128)} %bitcast.place_ref, bf16[16,80,256]{2,1,0:T(8,128)(2,1)S(1)} %get-tuple-element.43.refs_0_, bf16[16,80,256]{2,1,0:T(8,128)(2,1)S(1)} %collective-permute-done.7.refs_1_), custom_call_target="tpu_custom_call" | custom-call | flops 1024 | bytes 1024 | tf_op jit(solution)/shard_map/pairs/pallas_call | solution.py:228
  46.5 0.6 collective-permute-done.8.refs_3_
  47.2 0.0 collective-permute-done.6.refs_1_
  47.2 5.8 %pairs.9 = (bf16[2,32,256,2048]{3,2,1,0:T(8,128)(2,1)}, bf16[16,512,80]{2,1,0:T(8,128)(2,1)S(1)}, bf16[16,80,256]{2,1,0:T(8,128)(2,1)S(1)}) custom-call(s32[1]{0:T(128)} %bitcast.place_ref, bf16[16,80,256]{2,1,0:T(8,128)(2,1)S(1)} %get-tuple-element.42.refs_0_, ...), custom_call_target="tpu_custom_call", output_to_operand_aliasing={{0}: (3, {}), {2}: (4, {})} | custom-call | flops 1024 | bytes 1024 | tf_op jit(solution)/shard_map/pairs/pallas_call | solution.py:228
  53.0 0.0 collective-permute-start.9
  53.0 1.2 collective-permute-start.12
  54.2 7.0 %collective-permute-done.10.refs_4_ = bf16[16,80,256]{2,1,0:T(8,128)(2,1)S(1)} collective-permute-done((bf16[16,80,256]{2,1,0:T(8,128)(2,1)}, bf16[16,80,256]{2,1,0:T(8,128)(2,1)S(1)}, u32[]{:S(2)}, u32[]{:S(2)}) %collective-permute-start.10) | collective-permute-done | bytes 655392 | tf_op jit(solution)/shard_map/ppermute | solution.py:270
  61.2 0.0 collective-permute-done.9.refs_1_
  61.2 4.8 %pairs.10 = (bf16[2,32,256,2048]{3,2,1,0:T(8,128)(2,1)}, bf16[16,80,256]{2,1,0:T(8,128)(2,1)S(1)}) custom-call(s32[1]{0:T(128)} %bitcast.place_ref, bf16[16,80,256]{2,1,0:T(8,128)(2,1)S(1)} %get-tuple-element.46.refs_0_, bf16[16,80,256]{2,1,0:T(8,128)(2,1)S(1)} %collective-permute-done.9.refs_1_, ...), custom_call_target="tpu_custom_call", output_to_operand_aliasing={{0}: (4, {}), {1}: (5, {})} | custom-call | flops 1024 | bytes 1024 | tf_op jit(solution)/shard_map/pairs/pallas_call | solution.py:228
  66.0 0.0 collective-permute-start.11
  66.0 9.3 %collective-permute-done.12.refs_4_ = bf16[16,80,256]{2,1,0:T(8,128)(2,1)S(1)} collective-permute-done((bf16[16,80,256]{2,1,0:T(8,128)(2,1)S(1)}, bf16[16,80,256]{2,1,0:T(8,128)(2,1)S(1)}, u32[]{:S(2)}, u32[]{:S(2)}) %collective-permute-start.12) | collective-permute-done | bytes 655392 | tf_op jit(solution)/shard_map/ppermute | solution.py:270
  75.3 0.0 collective-permute-done.11.refs_1_
  75.3 4.8 %pairs.11 = (bf16[2,32,256,2048]{3,2,1,0:T(8,128)(2,1)}, bf16[16,80,256]{2,1,0:T(8,128)(2,1)S(1)}) custom-call(s32[1]{0:T(128)} %bitcast.place_ref, bf16[16,80,256]{2,1,0:T(8,128)(2,1)S(1)} %get-tuple-element.50.refs_0_, bf16[16,80,256]{2,1,0:T(8,128)(2,1)S(1)} %collective-permute-done.11.refs_1_, ...), custom_call_target="tpu_custom_call", output_to_operand_aliasing={{0}: (4, {}), {1}: (5, {})} | custom-call | flops 1024 | bytes 1024 | tf_op jit(solution)/shard_map/pairs/pallas_call | solution.py:228
  80.0 9.3 %collective-permute-done.14.refs_4_ = bf16[16,80,256]{2,1,0:T(8,128)(2,1)S(1)} collective-permute-done((bf16[16,80,256]{2,1,0:T(8,128)(2,1)S(1)}, bf16[16,80,256]{2,1,0:T(8,128)(2,1)S(1)}, u32[]{:S(2)}, u32[]{:S(2)}) %collective-permute-start.14) | collective-permute-done | bytes 655392 | tf_op jit(solution)/shard_map/ppermute | solution.py:270
  89.3 4.8 %pairs.12 = (bf16[2,32,256,2048]{3,2,1,0:T(8,128)(2,1)}, bf16[16,80,256]{2,1,0:T(8,128)(2,1)S(1)}) custom-call(s32[1]{0:T(128)} %bitcast.place_ref, bf16[16,80,256]{2,1,0:T(8,128)(2,1)S(1)} %get-tuple-element.53.refs_0_, bf16[16,80,256]{2,1,0:T(8,128)(2,1)S(1)} %collective-permute-done.13.refs_1_, ...), custom_call_target="tpu_custom_call", output_to_operand_aliasing={{0}: (4, {}), {1}: (5, {})} | custom-call | flops 1024 | bytes 1024 | tf_op jit(solution)/shard_map/pairs/pallas_call | solution.py:228
  94.1 9.3 %collective-permute-done.16.refs_4_ = bf16[16,80,256]{2,1,0:T(8,128)(2,1)S(1)} collective-permute-done((bf16[16,80,256]{2,1,0:T(8,128)(2,1)S(1)}, bf16[16,80,256]{2,1,0:T(8,128)(2,1)S(1)}, u32[]{:S(2)}, u32[]{:S(2)}) %collective-permute-start.16) | collective-permute-done | bytes 655392 | tf_op jit(solution)/shard_map/ppermute | solution.py:270
  103.3 0.0 collective-permute-done.15.refs_1_
  103.3 4.8 %pairs.13 = (bf16[2,32,256,2048]{3,2,1,0:T(8,128)(2,1)}, bf16[16,80,256]{2,1,0:T(8,128)(2,1)S(1)}) custom-call(s32[1]{0:T(128)} %bitcast.place_ref, bf16[16,80,256]{2,1,0:T(8,128)(2,1)S(1)} %get-tuple-element.55.refs_0_, bf16[16,80,256]{2,1,0:T(8,128)(2,1)S(1)} %collective-permute-done.15.refs_1_, ...), custom_call_target="tpu_custom_call", output_to_operand_aliasing={{0}: (4, {}), {1}: (5, {})} | custom-call | flops 1024 | bytes 1024 | tf_op jit(solution)/shard_map/pairs/pallas_call | solution.py:228
  108.1 0.0 collective-permute-start.17
  108.1 7.9 %collective-permute-done.18.refs_4_ = bf16[16,80,256]{2,1,0:T(8,128)(2,1)S(1)} collective-permute-done((bf16[16,80,256]{2,1,0:T(8,128)(2,1)S(1)}, bf16[16,80,256]{2,1,0:T(8,128)(2,1)S(1)}, u32[]{:S(2)}, u32[]{:S(2)}) %collective-permute-start.18) | collective-permute-done | bytes 655392 | tf_op jit(solution)/shard_map/ppermute | solution.py:270
  116.0 4.8 %pairs.14 = (bf16[2,32,256,2048]{3,2,1,0:T(8,128)(2,1)}, bf16[16,80,256]{2,1,0:T(8,128)(2,1)S(1)}) custom-call(s32[1]{0:T(128)} %bitcast.place_ref, bf16[16,80,256]{2,1,0:T(8,128)(2,1)S(1)} %get-tuple-element.57.refs_0_, bf16[16,80,256]{2,1,0:T(8,128)(2,1)S(1)} %collective-permute-done.17.refs_1_, ...), custom_call_target="tpu_custom_call", output_to_operand_aliasing={{0}: (4, {}), {1}: (5, {})} | custom-call | flops 1024 | bytes 1024 | tf_op jit(solution)/shard_map/pairs/pallas_call | solution.py:228
  120.8 0.0 collective-permute-start.19
  120.8 2.1 %collective-permute-done.19.refs_1_ = bf16[16,80,256]{2,1,0:T(8,128)(2,1)S(1)} collective-permute-done((bf16[16,80,256]{2,1,0:T(8,128)(2,1)S(1)}, bf16[16,80,256]{2,1,0:T(8,128)(2,1)S(1)}, u32[]{:S(2)}, u32[]{:S(2)}) %collective-permute-start.19) | collective-permute-done | bytes 655392 | tf_op jit(solution)/shard_map/ppermute | solution.py:267
  122.9 4.8 %pairs.15 = bf16[2,32,256,2048]{3,2,1,0:T(8,128)(2,1)} custom-call(s32[1]{0:T(128)} %bitcast.place_ref, bf16[16,80,256]{2,1,0:T(8,128)(2,1)S(1)} %get-tuple-element.59.refs_0_, bf16[16,80,256]{2,1,0:T(8,128)(2,1)S(1)} %collective-permute-done.19.refs_1_, bf16[16,512,80]{2,1,0:T(8,128)(2,1)S(1)} %get-tuple-element.51.refs_2_, ...), custom_call_target="tpu_custom_call", output_to_operand_aliasing={{}: (4, {})} | custom-call | flops 1024 | bytes 1024 | tf_op jit(solution)/shard_map/pairs/pallas_call | solution.py:228
  (9 shorter events, 0.0 us)
Async XLA Ops:
  0.7 1.0 copy-start
  1.7 0.7 copy-start.1
  8.3 10.5 %collective-permute-start.2 = (bf16[17,32,256]{2,1,0:T(8,128)(2,1)S(1)}, bf16[17,32,256]{2,1,0:T(8,128)(2,1)S(1)}, u32[]{:S(2)}, u32[]{:S(2)}) collective-permute-start(bf16[17,32,256]{2,1,0:T(8,128)(2,1)S(1)} %get-tuple-element.37), channel_id=1, source_target_pairs={{0,1},{1,0},{2,3},{3,2},{4,5},{5,4},{6,7},{7,6},{8,9},{9,8},{10,11... | collective-permute-start | bytes 835592 | tf_op jit(solution)/shard_map/ppermute | solution.py:280
  11.3 15.6 %collective-permute-start.3 = (bf16[17,32,256]{2,1,0:T(8,128)(2,1)S(1)}, bf16[17,32,256]{2,1,0:T(8,128)(2,1)S(1)}, u32[]{:S(2)}, u32[]{:S(2)}) collective-permute-start(bf16[17,32,256]{2,1,0:T(8,128)(2,1)S(1)} %get-tuple-element.38), channel_id=1, source_target_pairs={{0,2},{1,3},{2,0},{3,1},{4,6},{5,7},{6,4},{7,5},{8,10},{9,11},{10,... | collective-permute-start | bytes 835592 | tf_op jit(solution)/shard_map/ppermute | solution.py:280
  12.9 14.0 %collective-permute-start.4 = (bf16[17,32,256]{2,1,0:T(8,128)(2,1)S(1)}, bf16[17,32,256]{2,1,0:T(8,128)(2,1)S(1)}, u32[]{:S(2)}, u32[]{:S(2)}) collective-permute-start(bf16[17,32,256]{2,1,0:T(8,128)(2,1)S(1)} %get-tuple-element.39), channel_id=1, source_target_pairs={{0,3},{1,2},{2,1},{3,0},{4,7},{5,6},{6,5},{7,4},{8,11},{9,10},{10,... | collective-permute-start | bytes 835592 | tf_op jit(solution)/shard_map/ppermute | solution.py:280
  12.9 18.8 %collective-permute-start = (bf16[17,32,256]{2,1,0:T(8,128)(2,1)S(1)}, bf16[17,32,256]{2,1,0:T(8,128)(2,1)S(1)}, u32[]{:S(2)}, u32[]{:S(2)}) collective-permute-start(bf16[17,32,256]{2,1,0:T(8,128)(2,1)S(1)} %get-tuple-element.34), channel_id=1, source_target_pairs={{0,1},{1,0},{2,3},{3,2},{4,5},{5,4},{6,7},{7,6},{8,9},{9,8},{10,11... | collective-permute-start | bytes 835592 | tf_op jit(solution)/shard_map/ppermute | solution.py:280
  14.8 22.5 %collective-permute-start.1 = (bf16[17,32,256]{2,1,0:T(8,128)(2,1)S(1)}, bf16[17,32,256]{2,1,0:T(8,128)(2,1)S(1)}, u32[]{:S(2)}, u32[]{:S(2)}) collective-permute-start(bf16[17,32,256]{2,1,0:T(8,128)(2,1)S(1)} %get-tuple-element.35), channel_id=1, source_target_pairs={{0,2},{1,3},{2,0},{3,1},{4,6},{5,7},{6,4},{7,5},{8,10},{9,11},{10,... | collective-permute-start | bytes 835592 | tf_op jit(solution)/shard_map/ppermute | solution.py:280
  28.6 8.7 %collective-permute-start.5 = (bf16[17,32,256]{2,1,0:T(8,128)(2,1)S(1)}, bf16[17,32,256]{2,1,0:T(8,128)(2,1)S(1)}, u32[]{:S(2)}, u32[]{:S(2)}) collective-permute-start(bf16[17,32,256]{2,1,0:T(8,128)(2,1)S(1)} %get-tuple-element.41), channel_id=1, source_target_pairs={{0,3},{1,2},{2,1},{3,0},{4,7},{5,6},{6,5},{7,4},{8,11},{9,10},{10,... | collective-permute-start | bytes 835592 | tf_op jit(solution)/shard_map/ppermute | solution.py:280
  30.1 17.0 %collective-permute-start.8 = (bf16[16,80,256]{2,1,0:T(8,128)(2,1)}, bf16[16,80,256]{2,1,0:T(8,128)(2,1)S(1)}, u32[]{:S(2)}, u32[]{:S(2)}) collective-permute-start(bf16[16,80,256]{2,1,0:T(8,128)(2,1)} %get-tuple-element.45), channel_id=1, source_target_pairs={{0,8},{4,12},{8,16},{12,20},{16,24},{20,28},{24,0},{28,4},{1,9},{5... | collective-permute-start | bytes 1966088 | tf_op jit(solution)/shard_map/ppermute | solution.py:270
  31.7 9.0 %collective-permute-start.7 = (bf16[16,80,256]{2,1,0:T(8,128)(2,1)S(1)}, bf16[16,80,256]{2,1,0:T(8,128)(2,1)S(1)}, u32[]{:S(2)}, u32[]{:S(2)}) collective-permute-start(bf16[16,80,256]{2,1,0:T(8,128)(2,1)S(1)} %get-tuple-element.43.refs_0_), channel_id=1, source_target_pairs={{0,4},{4,0},{8,12},{12,8},{16,20},{20,16},{24,28},{28,24},{1,5},{5... | collective-permute-start | bytes 1966088 | tf_op jit(solution)/shard_map/ppermute | solution.py:267
  38.3 0.9 copy-start.2
  39.2 8.0 %collective-permute-start.6 = (bf16[16,80,256]{2,1,0:T(8,128)(2,1)S(1)}, bf16[16,80,256]{2,1,0:T(8,128)(2,1)S(1)}, u32[]{:S(2)}, u32[]{:S(2)}) collective-permute-start(bf16[16,80,256]{2,1,0:T(8,128)(2,1)S(1)} %get-tuple-element.42.refs_0_), channel_id=1, source_target_pairs={{0,4},{4,0},{8,12},{12,8},{16,20},{20,16},{24,28},{28,24},{1,5},{5... | collective-permute-start | bytes 1966088 | tf_op jit(solution)/shard_map/ppermute | solution.py:267
  39.2 22.1 %collective-permute-start.10 = (bf16[16,80,256]{2,1,0:T(8,128)(2,1)}, bf16[16,80,256]{2,1,0:T(8,128)(2,1)S(1)}, u32[]{:S(2)}, u32[]{:S(2)}) collective-permute-start(bf16[16,80,256]{2,1,0:T(8,128)(2,1)} %copy-done.2), channel_id=1, source_target_pairs={{0,8},{4,12},{8,16},{12,20},{16,24},{20,28},{24,0},{28,4},{1,9},{5... | collective-permute-start | bytes 1966088 | tf_op jit(solution)/shard_map/ppermute | solution.py:270
  53.0 8.2 %collective-permute-start.9 = (bf16[16,80,256]{2,1,0:T(8,128)(2,1)S(1)}, bf16[16,80,256]{2,1,0:T(8,128)(2,1)S(1)}, u32[]{:S(2)}, u32[]{:S(2)}) collective-permute-start(bf16[16,80,256]{2,1,0:T(8,128)(2,1)S(1)} %get-tuple-element.46.refs_0_), channel_id=1, source_target_pairs={{0,4},{4,0},{8,12},{12,8},{16,20},{20,16},{24,28},{28,24},{1,5},{5... | collective-permute-start | bytes 1966088 | tf_op jit(solution)/shard_map/ppermute | solution.py:267
  53.0 22.3 %collective-permute-start.12 = (bf16[16,80,256]{2,1,0:T(8,128)(2,1)S(1)}, bf16[16,80,256]{2,1,0:T(8,128)(2,1)S(1)}, u32[]{:S(2)}, u32[]{:S(2)}) collective-permute-start(bf16[16,80,256]{2,1,0:T(8,128)(2,1)S(1)} %get-tuple-element.46.refs_0_), channel_id=1, source_target_pairs={{0,8},{4,12},{8,16},{12,20},{16,24},{20,28},{24,0},{28,4},{1,9},{5... | collective-permute-start | bytes 1966088 | tf_op jit(solution)/shard_map/ppermute | solution.py:270
  66.0 9.3 %collective-permute-start.11 = (bf16[16,80,256]{2,1,0:T(8,128)(2,1)S(1)}, bf16[16,80,256]{2,1,0:T(8,128)(2,1)S(1)}, u32[]{:S(2)}, u32[]{:S(2)}) collective-permute-start(bf16[16,80,256]{2,1,0:T(8,128)(2,1)S(1)} %get-tuple-element.50.refs_0_), channel_id=1, source_target_pairs={{0,4},{4,0},{8,12},{12,8},{16,20},{20,16},{24,28},{28,24},{1,5},{5... | collective-permute-start | bytes 1966088 | tf_op jit(solution)/shard_map/ppermute | solution.py:267
  66.0 23.3 %collective-permute-start.14 = (bf16[16,80,256]{2,1,0:T(8,128)(2,1)S(1)}, bf16[16,80,256]{2,1,0:T(8,128)(2,1)S(1)}, u32[]{:S(2)}, u32[]{:S(2)}) collective-permute-start(bf16[16,80,256]{2,1,0:T(8,128)(2,1)S(1)} %get-tuple-element.50.refs_0_), channel_id=1, source_target_pairs={{0,8},{4,12},{8,16},{12,20},{16,24},{20,28},{24,0},{28,4},{1,9},{5... | collective-permute-start | bytes 1966088 | tf_op jit(solution)/shard_map/ppermute | solution.py:270
  80.0 9.3 %collective-permute-start.13 = (bf16[16,80,256]{2,1,0:T(8,128)(2,1)S(1)}, bf16[16,80,256]{2,1,0:T(8,128)(2,1)S(1)}, u32[]{:S(2)}, u32[]{:S(2)}) collective-permute-start(bf16[16,80,256]{2,1,0:T(8,128)(2,1)S(1)} %get-tuple-element.53.refs_0_), channel_id=1, source_target_pairs={{0,4},{4,0},{8,12},{12,8},{16,20},{20,16},{24,28},{28,24},{1,5},{5... | collective-permute-start | bytes 1966088 | tf_op jit(solution)/shard_map/ppermute | solution.py:267
  80.0 23.3 %collective-permute-start.16 = (bf16[16,80,256]{2,1,0:T(8,128)(2,1)S(1)}, bf16[16,80,256]{2,1,0:T(8,128)(2,1)S(1)}, u32[]{:S(2)}, u32[]{:S(2)}) collective-permute-start(bf16[16,80,256]{2,1,0:T(8,128)(2,1)S(1)} %get-tuple-element.53.refs_0_), channel_id=1, source_target_pairs={{0,8},{4,12},{8,16},{12,20},{16,24},{20,28},{24,0},{28,4},{1,9},{5... | collective-permute-start | bytes 1966088 | tf_op jit(solution)/shard_map/ppermute | solution.py:270
  94.1 9.3 %collective-permute-start.15 = (bf16[16,80,256]{2,1,0:T(8,128)(2,1)S(1)}, bf16[16,80,256]{2,1,0:T(8,128)(2,1)S(1)}, u32[]{:S(2)}, u32[]{:S(2)}) collective-permute-start(bf16[16,80,256]{2,1,0:T(8,128)(2,1)S(1)} %get-tuple-element.55.refs_0_), channel_id=1, source_target_pairs={{0,4},{4,0},{8,12},{12,8},{16,20},{20,16},{24,28},{28,24},{1,5},{5... | collective-permute-start | bytes 1966088 | tf_op jit(solution)/shard_map/ppermute | solution.py:267
  94.1 21.9 %collective-permute-start.18 = (bf16[16,80,256]{2,1,0:T(8,128)(2,1)S(1)}, bf16[16,80,256]{2,1,0:T(8,128)(2,1)S(1)}, u32[]{:S(2)}, u32[]{:S(2)}) collective-permute-start(bf16[16,80,256]{2,1,0:T(8,128)(2,1)S(1)} %get-tuple-element.55.refs_0_), channel_id=1, source_target_pairs={{0,8},{4,12},{8,16},{12,20},{16,24},{20,28},{24,0},{28,4},{1,9},{5... | collective-permute-start | bytes 1966088 | tf_op jit(solution)/shard_map/ppermute | solution.py:270
  108.1 7.9 %collective-permute-start.17 = (bf16[16,80,256]{2,1,0:T(8,128)(2,1)S(1)}, bf16[16,80,256]{2,1,0:T(8,128)(2,1)S(1)}, u32[]{:S(2)}, u32[]{:S(2)}) collective-permute-start(bf16[16,80,256]{2,1,0:T(8,128)(2,1)S(1)} %get-tuple-element.57.refs_0_), channel_id=1, source_target_pairs={{0,4},{4,0},{8,12},{12,8},{16,20},{20,16},{24,28},{28,24},{1,5},{5... | collective-permute-start | bytes 1966088 | tf_op jit(solution)/shard_map/ppermute | solution.py:267
  120.8 2.1 %collective-permute-start.19 = (bf16[16,80,256]{2,1,0:T(8,128)(2,1)S(1)}, bf16[16,80,256]{2,1,0:T(8,128)(2,1)S(1)}, u32[]{:S(2)}, u32[]{:S(2)}) collective-permute-start(bf16[16,80,256]{2,1,0:T(8,128)(2,1)S(1)} %get-tuple-element.59.refs_0_), channel_id=1, source_target_pairs={{0,4},{4,0},{8,12},{12,8},{16,20},{20,16},{24,28},{28,24},{1,5},{5... | collective-permute-start | bytes 1966088 | tf_op jit(solution)/shard_map/ppermute | solution.py:267

commit v3 on v2

--- a/solution.py
+++ b/solution.py
@@ -303,7 +303,7 @@
         meet(1, 0)
         ready.append((1, 0))
     for k, now in enumerate(order):
-        if ready:
+        if ready and k + 1 < len(order):
             (travelling[now],) = multiply(*ready.pop(0), [travelling[now]])
         ours[now] = travelling[now]
         launch(k + 1)

time: 128 us -> 126 us (0.984)
  waiting for transfers between devices: 61.7 us -> 59.5 us
    ppermute x8, waiting for transfers between devices: 2.11 us -> 0.02 us  [meet(): theirs[c, t] = lax.ppermute(ours[c, t], 'chan', cores)]
  transfers between devices with their start and end apart: 20 -> 20, of which waited for: 10 -> 9; matrix products, arithmetic and copies ran while one was open for 0% -> 0% of each run, Pallas kernels for 26% -> 30%
where the time goes in v3:
time: 126 us
  waiting for transfers between devices  59.5 us (47%)
  Pallas kernels  48.7 us (39%)
  starting transfers between devices  13.9 us (11%)
  local copies, waits for them, and re-layouts  2.63 us (2%)
    ppermute x6, waiting for transfers between devices, send(): travelling[c, t] = lax.ppermute(travelling[c, t - 1], 'chan', ring)  43.3 us
    pallas_call x8, Pallas kernels, pair_products(): pl.pallas_call(kernel, grid_spec=pltpu.PrefetchScalarGridSpec(num_scalar_...  40.2 us
    ppermute x6, waiting for transfers between devices, shards(): lax.ppermute(pieces[c][d], 'freq', swap[d])  16.2 us
    ppermute x6, starting transfers between devices, shards(): lax.ppermute(pieces[c][d], 'freq', swap[d])  9.5 us
    pallas_call x1, Pallas kernels, spectra_pieces(): pl.pallas_call(functools.partial(spectra_kernel, nodes), in_specs=[smem,...  5.92 us
    ppermute x6, starting transfers between devices, send(): travelling[c, t] = lax.ppermute(travelling[c, t - 1], 'chan', ring)  4.4 us
    unnamed x6, local copies, waits for them, and re-layouts  2.63 us
    pallas_call x2, Pallas kernels, pack_windows(): pl.pallas_call(kernel, in_specs=[pl.BlockSpec(memory_space=pltpu.SMEM)] +...  2.61 us
  transfers between devices with their start and end apart: 20, of which 9 were waited for; matrix products, arithmetic and copies ran while one was open for 0% of the time, Pallas kernels for 30%

profile of v3, /device:TPU:0, one launch (start us, length us, event | category | flops | bytes accessed | tf_op | source)
XLA Modules:
  0.0 125.5 jit_solution(15728779202191431837)
XLA Ops:
  0.7 0.0 copy-start
  0.7 1.0 copy-done
  1.7 0.7 copy-done.1
  2.4 5.9 %spectra.1 = (bf16[17,32,256]{2,1,0:T(8,128)(2,1)S(1)}, bf16[17,32,256]{2,1,0:T(8,128)(2,1)S(1)}, bf16[17,32,256]{2,1,0:T(8,128)(2,1)S(1)}, bf16[17,32,256]{2,1,...) custom-call(s32[1]{0:T(128)} %bitcast.1.me_ref, ...), custom_call_target="tpu_custom_call" | custom-call | flops 2147483648 | bytes 8388608 | tf_op jit(solution)/shard_map/spectra/pallas_call | solution.py:90
  8.3 3.0 %collective-permute-start.2 = (bf16[17,32,256]{2,1,0:T(8,128)(2,1)S(1)}, bf16[17,32,256]{2,1,0:T(8,128)(2,1)S(1)}, u32[]{:S(2)}, u32[]{:S(2)}) collective-permute-start(bf16[17,32,256]{2,1,0:T(8,128)(2,1)S(1)} %get-tuple-element.35), channel_id=1, source_target_pairs={{0,1},{1,0},{2,3},{3,2},{4,5},{5,4},{6,7},{7,6},{8,9},{9,8},{10,11... | collective-permute-start | bytes 835592 | tf_op jit(solution)/shard_map/ppermute | solution.py:280
  11.3 1.5 %collective-permute-start.3 = (bf16[17,32,256]{2,1,0:T(8,128)(2,1)S(1)}, bf16[17,32,256]{2,1,0:T(8,128)(2,1)S(1)}, u32[]{:S(2)}, u32[]{:S(2)}) collective-permute-start(bf16[17,32,256]{2,1,0:T(8,128)(2,1)S(1)} %get-tuple-element.36), channel_id=1, source_target_pairs={{0,2},{1,3},{2,0},{3,1},{4,6},{5,7},{6,4},{7,5},{8,10},{9,11},{10,... | collective-permute-start | bytes 835592 | tf_op jit(solution)/shard_map/ppermute | solution.py:280
  12.9 0.0 collective-permute-start.4
  12.9 1.9 %collective-permute-start = (bf16[17,32,256]{2,1,0:T(8,128)(2,1)S(1)}, bf16[17,32,256]{2,1,0:T(8,128)(2,1)S(1)}, u32[]{:S(2)}, u32[]{:S(2)}) collective-permute-start(bf16[17,32,256]{2,1,0:T(8,128)(2,1)S(1)} %get-tuple-element.32), channel_id=1, source_target_pairs={{0,1},{1,0},{2,3},{3,2},{4,5},{5,4},{6,7},{7,6},{8,9},{9,8},{10,11... | collective-permute-start | bytes 835592 | tf_op jit(solution)/shard_map/ppermute | solution.py:280
  14.8 1.5 %collective-permute-start.1 = (bf16[17,32,256]{2,1,0:T(8,128)(2,1)S(1)}, bf16[17,32,256]{2,1,0:T(8,128)(2,1)S(1)}, u32[]{:S(2)}, u32[]{:S(2)}) collective-permute-start(bf16[17,32,256]{2,1,0:T(8,128)(2,1)S(1)} %get-tuple-element.33), channel_id=1, source_target_pairs={{0,2},{1,3},{2,0},{3,1},{4,6},{5,7},{6,4},{7,5},{8,10},{9,11},{10,... | collective-permute-start | bytes 835592 | tf_op jit(solution)/shard_map/ppermute | solution.py:280
  16.3 2.5 %collective-permute-done.2.refs_1_ = bf16[17,32,256]{2,1,0:T(8,128)(2,1)S(1)} collective-permute-done((bf16[17,32,256]{2,1,0:T(8,128)(2,1)S(1)}, bf16[17,32,256]{2,1,0:T(8,128)(2,1)S(1)}, u32[]{:S(2)}, u32[]{:S(2)}) %collective-permute-start.2) | collective-permute-done | bytes 278560 | tf_op jit(solution)/shard_map/ppermute | solution.py:280
  18.8 8.1 %collective-permute-done.3.refs_2_ = bf16[17,32,256]{2,1,0:T(8,128)(2,1)S(1)} collective-permute-done((bf16[17,32,256]{2,1,0:T(8,128)(2,1)S(1)}, bf16[17,32,256]{2,1,0:T(8,128)(2,1)S(1)}, u32[]{:S(2)}, u32[]{:S(2)}) %collective-permute-start.3) | collective-permute-done | bytes 278560 | tf_op jit(solution)/shard_map/ppermute | solution.py:280
  26.9 0.0 collective-permute-done.4.refs_3_
  26.9 1.7 %pack.2 = (bf16[16,80,256]{2,1,0:T(8,128)(2,1)}, bf16[16,80,256]{2,1,0:T(8,128)(2,1)S(1)}, bf16[17,32,256]{2,1,0:T(8,128)(2,1)S(1)}) custom-call(s32[1]{0:T(128)} %bitcast.1.me_ref, bf16[17,32,256]{2,1,0:T(8,128)(2,1)S(1)} %get-tuple-element.34.refs_0_, bf16[17,32,256]{2,1,0:T(8,128)(2,1)S(1)} %collective-permute-done.2.refs_1_, ...), custom_call_target="tpu_custom_call", output_to_operand_aliasing={{2}: (5, {})} | custom-call | flops 1024 | bytes 1024 | tf_op jit(solution)/shard_map/pack/pallas_call | solution.py:149
  28.6 1.5 %collective-permute-start.5 = (bf16[17,32,256]{2,1,0:T(8,128)(2,1)S(1)}, bf16[17,32,256]{2,1,0:T(8,128)(2,1)S(1)}, u32[]{:S(2)}, u32[]{:S(2)}) collective-permute-start(bf16[17,32,256]{2,1,0:T(8,128)(2,1)S(1)} %get-tuple-element.39), channel_id=1, source_target_pairs={{0,3},{1,2},{2,1},{3,0},{4,7},{5,6},{6,5},{7,4},{8,11},{9,10},{10,... | collective-permute-start | bytes 835592 | tf_op jit(solution)/shard_map/ppermute | solution.py:280
  30.1 1.6 %collective-permute-start.8 = (bf16[16,80,256]{2,1,0:T(8,128)(2,1)}, bf16[16,80,256]{2,1,0:T(8,128)(2,1)S(1)}, u32[]{:S(2)}, u32[]{:S(2)}) collective-permute-start(bf16[16,80,256]{2,1,0:T(8,128)(2,1)} %get-tuple-element.43), channel_id=1, source_target_pairs={{0,8},{4,12},{8,16},{12,20},{16,24},{20,28},{24,0},{28,4},{1,9},{5... | collective-permute-start | bytes 1966088 | tf_op jit(solution)/shard_map/ppermute | solution.py:270
  31.7 0.0 collective-permute-start.7
  31.7 0.0 collective-permute-done.refs_1_
  31.7 5.7 %collective-permute-done.1.refs_2_ = bf16[17,32,256]{2,1,0:T(8,128)(2,1)S(1)} collective-permute-done((bf16[17,32,256]{2,1,0:T(8,128)(2,1)S(1)}, bf16[17,32,256]{2,1,0:T(8,128)(2,1)S(1)}, u32[]{:S(2)}, u32[]{:S(2)}) %collective-permute-start.1) | collective-permute-done | bytes 278560 | tf_op jit(solution)/shard_map/ppermute | solution.py:280
  37.4 0.0 collective-permute-done.5.refs_3_
  37.4 0.9 pack.3
  38.3 0.9 copy-done.2
  39.2 0.0 collective-permute-start.6
  39.2 1.6 %collective-permute-start.10 = (bf16[16,80,256]{2,1,0:T(8,128)(2,1)}, bf16[16,80,256]{2,1,0:T(8,128)(2,1)S(1)}, u32[]{:S(2)}, u32[]{:S(2)}) collective-permute-start(bf16[16,80,256]{2,1,0:T(8,128)(2,1)} %copy-done.2), channel_id=1, source_target_pairs={{0,8},{4,12},{8,16},{12,20},{16,24},{20,28},{24,0},{28,4},{1,9},{5... | collective-permute-start | bytes 1966088 | tf_op jit(solution)/shard_map/ppermute | solution.py:270
  40.7 0.0 collective-permute-done.7.refs_1_
  40.7 5.8 %pairs.8 = (bf16[2,32,256,2048]{3,2,1,0:T(8,128)(2,1)}, bf16[16,512,80]{2,1,0:T(8,128)(2,1)S(1)}) custom-call(s32[1]{0:T(128)} %bitcast.place_ref, bf16[16,80,256]{2,1,0:T(8,128)(2,1)S(1)} %get-tuple-element.41.refs_0_, bf16[16,80,256]{2,1,0:T(8,128)(2,1)S(1)} %collective-permute-done.7.refs_1_), custom_call_target="tpu_custom_call" | custom-call | flops 1024 | bytes 1024 | tf_op jit(solution)/shard_map/pairs/pallas_call | solution.py:228
  46.6 0.6 collective-permute-done.8.refs_3_
  47.1 0.0 collective-permute-done.6.refs_1_
  47.1 5.8 %pairs.9 = (bf16[2,32,256,2048]{3,2,1,0:T(8,128)(2,1)}, bf16[16,512,80]{2,1,0:T(8,128)(2,1)S(1)}, bf16[16,80,256]{2,1,0:T(8,128)(2,1)S(1)}) custom-call(s32[1]{0:T(128)} %bitcast.place_ref, bf16[16,80,256]{2,1,0:T(8,128)(2,1)S(1)} %get-tuple-element.40.refs_0_, ...), custom_call_target="tpu_custom_call", output_to_operand_aliasing={{0}: (3, {}), {2}: (4, {})} | custom-call | flops 1024 | bytes 1024 | tf_op jit(solution)/shard_map/pairs/pallas_call | solution.py:228
  53.0 0.0 collective-permute-start.9
  53.0 1.3 collective-permute-start.12
  54.2 7.0 %collective-permute-done.10.refs_4_ = bf16[16,80,256]{2,1,0:T(8,128)(2,1)S(1)} collective-permute-done((bf16[16,80,256]{2,1,0:T(8,128)(2,1)}, bf16[16,80,256]{2,1,0:T(8,128)(2,1)S(1)}, u32[]{:S(2)}, u32[]{:S(2)}) %collective-permute-start.10) | collective-permute-done | bytes 655392 | tf_op jit(solution)/shard_map/ppermute | solution.py:270
  61.2 0.0 collective-permute-done.9.refs_1_
  61.2 4.8 %pairs.10 = (bf16[2,32,256,2048]{3,2,1,0:T(8,128)(2,1)}, bf16[16,80,256]{2,1,0:T(8,128)(2,1)S(1)}) custom-call(s32[1]{0:T(128)} %bitcast.place_ref, bf16[16,80,256]{2,1,0:T(8,128)(2,1)S(1)} %get-tuple-element.44.refs_0_, bf16[16,80,256]{2,1,0:T(8,128)(2,1)S(1)} %collective-permute-done.9.refs_1_, ...), custom_call_target="tpu_custom_call", output_to_operand_aliasing={{0}: (4, {}), {1}: (5, {})} | custom-call | flops 1024 | bytes 1024 | tf_op jit(solution)/shard_map/pairs/pallas_call | solution.py:228
  65.9 0.0 collective-permute-start.11
  65.9 9.3 %collective-permute-done.12.refs_4_ = bf16[16,80,256]{2,1,0:T(8,128)(2,1)S(1)} collective-permute-done((bf16[16,80,256]{2,1,0:T(8,128)(2,1)S(1)}, bf16[16,80,256]{2,1,0:T(8,128)(2,1)S(1)}, u32[]{:S(2)}, u32[]{:S(2)}) %collective-permute-start.12) | collective-permute-done | bytes 655392 | tf_op jit(solution)/shard_map/ppermute | solution.py:270
  75.2 4.7 %pairs.11 = (bf16[2,32,256,2048]{3,2,1,0:T(8,128)(2,1)}, bf16[16,80,256]{2,1,0:T(8,128)(2,1)S(1)}) custom-call(s32[1]{0:T(128)} %bitcast.place_ref, bf16[16,80,256]{2,1,0:T(8,128)(2,1)S(1)} %get-tuple-element.48.refs_0_, bf16[16,80,256]{2,1,0:T(8,128)(2,1)S(1)} %collective-permute-done.11.refs_1_, ...), custom_call_target="tpu_custom_call", output_to_operand_aliasing={{0}: (4, {}), {1}: (5, {})} | custom-call | flops 1024 | bytes 1024 | tf_op jit(solution)/shard_map/pairs/pallas_call | solution.py:228
  80.0 0.0 collective-permute-start.13
  80.0 9.3 %collective-permute-done.14.refs_4_ = bf16[16,80,256]{2,1,0:T(8,128)(2,1)S(1)} collective-permute-done((bf16[16,80,256]{2,1,0:T(8,128)(2,1)S(1)}, bf16[16,80,256]{2,1,0:T(8,128)(2,1)S(1)}, u32[]{:S(2)}, u32[]{:S(2)}) %collective-permute-start.14) | collective-permute-done | bytes 655392 | tf_op jit(solution)/shard_map/ppermute | solution.py:270
  89.3 0.0 collective-permute-done.13.refs_1_
  89.3 4.8 %pairs.12 = (bf16[2,32,256,2048]{3,2,1,0:T(8,128)(2,1)}, bf16[16,80,256]{2,1,0:T(8,128)(2,1)S(1)}) custom-call(s32[1]{0:T(128)} %bitcast.place_ref, bf16[16,80,256]{2,1,0:T(8,128)(2,1)S(1)} %get-tuple-element.51.refs_0_, bf16[16,80,256]{2,1,0:T(8,128)(2,1)S(1)} %collective-permute-done.13.refs_1_, ...), custom_call_target="tpu_custom_call", output_to_operand_aliasing={{0}: (4, {}), {1}: (5, {})} | custom-call | flops 1024 | bytes 1024 | tf_op jit(solution)/shard_map/pairs/pallas_call | solution.py:228
  94.0 0.0 collective-permute-start.17
  94.0 0.0 collective-permute-start.15
  94.0 9.3 %collective-permute-done.18.refs_4_ = bf16[16,80,256]{2,1,0:T(8,128)(2,1)S(1)} collective-permute-done((bf16[16,80,256]{2,1,0:T(8,128)(2,1)S(1)}, bf16[16,80,256]{2,1,0:T(8,128)(2,1)S(1)}, u32[]{:S(2)}, u32[]{:S(2)}) %collective-permute-start.18) | collective-permute-done | bytes 655392 | tf_op jit(solution)/shard_map/ppermute | solution.py:270
  103.3 4.8 %pairs.13 = (bf16[2,32,256,2048]{3,2,1,0:T(8,128)(2,1)}, bf16[16,80,256]{2,1,0:T(8,128)(2,1)S(1)}) custom-call(s32[1]{0:T(128)} %bitcast.place_ref, bf16[16,80,256]{2,1,0:T(8,128)(2,1)S(1)} %get-tuple-element.53.refs_0_, bf16[16,80,256]{2,1,0:T(8,128)(2,1)S(1)} %collective-permute-done.17.refs_1_, ...), custom_call_target="tpu_custom_call", output_to_operand_aliasing={{0}: (4, {}), {1}: (5, {})} | custom-call | flops 1024 | bytes 1024 | tf_op jit(solution)/shard_map/pairs/pallas_call | solution.py:228
  108.1 7.9 %collective-permute-done.15.refs_0_ = bf16[16,80,256]{2,1,0:T(8,128)(2,1)S(1)} collective-permute-done((bf16[16,80,256]{2,1,0:T(8,128)(2,1)S(1)}, bf16[16,80,256]{2,1,0:T(8,128)(2,1)S(1)}, u32[]{:S(2)}, u32[]{:S(2)}) %collective-permute-start.15) | collective-permute-done | bytes 655392 | tf_op jit(solution)/shard_map/ppermute | solution.py:270
  116.0 4.8 %pairs.14.refs_3_ = bf16[2,32,256,2048]{3,2,1,0:T(8,128)(2,1)} custom-call(s32[1]{0:T(128)} %bitcast.place_ref, bf16[16,80,256]{2,1,0:T(8,128)(2,1)S(1)} %get-tuple-element.55.refs_0_, bf16[16,80,256]{2,1,0:T(8,128)(2,1)S(1)} %collective-permute-done.19.refs_1_, bf16[16,512,80]{2,1,0:T(8,128)(2,1)S(1)} %get-tuple-element.45.refs_2_, ...), custom_call_target="tpu_custom_call", output_to_operand_aliasing={{}: (4, {})} | custom-call | flops 1024 | bytes 1024 | tf_op jit(solution)/shard_map/pairs/pallas_call | solution.py:228
  120.8 0.0 collective-permute-done.16.refs_1_
  120.8 4.8 %pairs.15 = bf16[2,32,256,2048]{3,2,1,0:T(8,128)(2,1)} custom-call(s32[1]{0:T(128)} %bitcast.place_ref, bf16[16,80,256]{2,1,0:T(8,128)(2,1)S(1)} %collective-permute-done.15.refs_0_, bf16[16,80,256]{2,1,0:T(8,128)(2,1)S(1)} %collective-permute-done.16.refs_1_, bf16[16,512,80]{2,1,0:T(8,128)(2,1)S(1)} %get-tuple-element.49.refs_2_, ...), custom_call_target="tpu_custom_call", output_to_operand_aliasing={{}: (4, {})} | custom-call | flops 1024 | bytes 1024 | tf_op jit(solution)/shard_map/pairs/pallas_call | solution.py:228
  (9 shorter events, 0.0 us)
Async XLA Ops:
  0.7 1.0 copy-start
  1.7 0.7 copy-start.1
  8.3 10.5 %collective-permute-start.2 = (bf16[17,32,256]{2,1,0:T(8,128)(2,1)S(1)}, bf16[17,32,256]{2,1,0:T(8,128)(2,1)S(1)}, u32[]{:S(2)}, u32[]{:S(2)}) collective-permute-start(bf16[17,32,256]{2,1,0:T(8,128)(2,1)S(1)} %get-tuple-element.35), channel_id=1, source_target_pairs={{0,1},{1,0},{2,3},{3,2},{4,5},{5,4},{6,7},{7,6},{8,9},{9,8},{10,11... | collective-permute-start | bytes 835592 | tf_op jit(solution)/shard_map/ppermute | solution.py:280
  11.3 15.6 %collective-permute-start.3 = (bf16[17,32,256]{2,1,0:T(8,128)(2,1)S(1)}, bf16[17,32,256]{2,1,0:T(8,128)(2,1)S(1)}, u32[]{:S(2)}, u32[]{:S(2)}) collective-permute-start(bf16[17,32,256]{2,1,0:T(8,128)(2,1)S(1)} %get-tuple-element.36), channel_id=1, source_target_pairs={{0,2},{1,3},{2,0},{3,1},{4,6},{5,7},{6,4},{7,5},{8,10},{9,11},{10,... | collective-permute-start | bytes 835592 | tf_op jit(solution)/shard_map/ppermute | solution.py:280
  12.9 14.0 %collective-permute-start.4 = (bf16[17,32,256]{2,1,0:T(8,128)(2,1)S(1)}, bf16[17,32,256]{2,1,0:T(8,128)(2,1)S(1)}, u32[]{:S(2)}, u32[]{:S(2)}) collective-permute-start(bf16[17,32,256]{2,1,0:T(8,128)(2,1)S(1)} %get-tuple-element.37), channel_id=1, source_target_pairs={{0,3},{1,2},{2,1},{3,0},{4,7},{5,6},{6,5},{7,4},{8,11},{9,10},{10,... | collective-permute-start | bytes 835592 | tf_op jit(solution)/shard_map/ppermute | solution.py:280
  12.9 18.8 %collective-permute-start = (bf16[17,32,256]{2,1,0:T(8,128)(2,1)S(1)}, bf16[17,32,256]{2,1,0:T(8,128)(2,1)S(1)}, u32[]{:S(2)}, u32[]{:S(2)}) collective-permute-start(bf16[17,32,256]{2,1,0:T(8,128)(2,1)S(1)} %get-tuple-element.32), channel_id=1, source_target_pairs={{0,1},{1,0},{2,3},{3,2},{4,5},{5,4},{6,7},{7,6},{8,9},{9,8},{10,11... | collective-permute-start | bytes 835592 | tf_op jit(solution)/shard_map/ppermute | solution.py:280
  14.8 22.5 %collective-permute-start.1 = (bf16[17,32,256]{2,1,0:T(8,128)(2,1)S(1)}, bf16[17,32,256]{2,1,0:T(8,128)(2,1)S(1)}, u32[]{:S(2)}, u32[]{:S(2)}) collective-permute-start(bf16[17,32,256]{2,1,0:T(8,128)(2,1)S(1)} %get-tuple-element.33), channel_id=1, source_target_pairs={{0,2},{1,3},{2,0},{3,1},{4,6},{5,7},{6,4},{7,5},{8,10},{9,11},{10,... | collective-permute-start | bytes 835592 | tf_op jit(solution)/shard_map/ppermute | solution.py:280
  28.6 8.7 %collective-permute-start.5 = (bf16[17,32,256]{2,1,0:T(8,128)(2,1)S(1)}, bf16[17,32,256]{2,1,0:T(8,128)(2,1)S(1)}, u32[]{:S(2)}, u32[]{:S(2)}) collective-permute-start(bf16[17,32,256]{2,1,0:T(8,128)(2,1)S(1)} %get-tuple-element.39), channel_id=1, source_target_pairs={{0,3},{1,2},{2,1},{3,0},{4,7},{5,6},{6,5},{7,4},{8,11},{9,10},{10,... | collective-permute-start | bytes 835592 | tf_op jit(solution)/shard_map/ppermute | solution.py:280
  30.1 17.0 %collective-permute-start.8 = (bf16[16,80,256]{2,1,0:T(8,128)(2,1)}, bf16[16,80,256]{2,1,0:T(8,128)(2,1)S(1)}, u32[]{:S(2)}, u32[]{:S(2)}) collective-permute-start(bf16[16,80,256]{2,1,0:T(8,128)(2,1)} %get-tuple-element.43), channel_id=1, source_target_pairs={{0,8},{4,12},{8,16},{12,20},{16,24},{20,28},{24,0},{28,4},{1,9},{5... | collective-permute-start | bytes 1966088 | tf_op jit(solution)/shard_map/ppermute | solution.py:270
  31.7 9.0 %collective-permute-start.7 = (bf16[16,80,256]{2,1,0:T(8,128)(2,1)S(1)}, bf16[16,80,256]{2,1,0:T(8,128)(2,1)S(1)}, u32[]{:S(2)}, u32[]{:S(2)}) collective-permute-start(bf16[16,80,256]{2,1,0:T(8,128)(2,1)S(1)} %get-tuple-element.41.refs_0_), channel_id=1, source_target_pairs={{0,4},{4,0},{8,12},{12,8},{16,20},{20,16},{24,28},{28,24},{1,5},{5... | collective-permute-start | bytes 1966088 | tf_op jit(solution)/shard_map/ppermute | solution.py:267
  38.3 0.9 copy-start.2
  39.2 8.0 %collective-permute-start.6 = (bf16[16,80,256]{2,1,0:T(8,128)(2,1)S(1)}, bf16[16,80,256]{2,1,0:T(8,128)(2,1)S(1)}, u32[]{:S(2)}, u32[]{:S(2)}) collective-permute-start(bf16[16,80,256]{2,1,0:T(8,128)(2,1)S(1)} %get-tuple-element.40.refs_0_), channel_id=1, source_target_pairs={{0,4},{4,0},{8,12},{12,8},{16,20},{20,16},{24,28},{28,24},{1,5},{5... | collective-permute-start | bytes 1966088 | tf_op jit(solution)/shard_map/ppermute | solution.py:267
  39.2 22.0 %collective-permute-start.10 = (bf16[16,80,256]{2,1,0:T(8,128)(2,1)}, bf16[16,80,256]{2,1,0:T(8,128)(2,1)S(1)}, u32[]{:S(2)}, u32[]{:S(2)}) collective-permute-start(bf16[16,80,256]{2,1,0:T(8,128)(2,1)} %copy-done.2), channel_id=1, source_target_pairs={{0,8},{4,12},{8,16},{12,20},{16,24},{20,28},{24,0},{28,4},{1,9},{5... | collective-permute-start | bytes 1966088 | tf_op jit(solution)/shard_map/ppermute | solution.py:270
  53.0 8.2 %collective-permute-start.9 = (bf16[16,80,256]{2,1,0:T(8,128)(2,1)S(1)}, bf16[16,80,256]{2,1,0:T(8,128)(2,1)S(1)}, u32[]{:S(2)}, u32[]{:S(2)}) collective-permute-start(bf16[16,80,256]{2,1,0:T(8,128)(2,1)S(1)} %get-tuple-element.44.refs_0_), channel_id=1, source_target_pairs={{0,4},{4,0},{8,12},{12,8},{16,20},{20,16},{24,28},{28,24},{1,5},{5... | collective-permute-start | bytes 1966088 | tf_op jit(solution)/shard_map/ppermute | solution.py:267
  53.0 22.3 %collective-permute-start.12 = (bf16[16,80,256]{2,1,0:T(8,128)(2,1)S(1)}, bf16[16,80,256]{2,1,0:T(8,128)(2,1)S(1)}, u32[]{:S(2)}, u32[]{:S(2)}) collective-permute-start(bf16[16,80,256]{2,1,0:T(8,128)(2,1)S(1)} %get-tuple-element.44.refs_0_), channel_id=1, source_target_pairs={{0,8},{4,12},{8,16},{12,20},{16,24},{20,28},{24,0},{28,4},{1,9},{5... | collective-permute-start | bytes 1966088 | tf_op jit(solution)/shard_map/ppermute | solution.py:270
  65.9 9.3 %collective-permute-start.11 = (bf16[16,80,256]{2,1,0:T(8,128)(2,1)S(1)}, bf16[16,80,256]{2,1,0:T(8,128)(2,1)S(1)}, u32[]{:S(2)}, u32[]{:S(2)}) collective-permute-start(bf16[16,80,256]{2,1,0:T(8,128)(2,1)S(1)} %get-tuple-element.48.refs_0_), channel_id=1, source_target_pairs={{0,4},{4,0},{8,12},{12,8},{16,20},{20,16},{24,28},{28,24},{1,5},{5... | collective-permute-start | bytes 1966088 | tf_op jit(solution)/shard_map/ppermute | solution.py:267
  65.9 23.3 %collective-permute-start.14 = (bf16[16,80,256]{2,1,0:T(8,128)(2,1)S(1)}, bf16[16,80,256]{2,1,0:T(8,128)(2,1)S(1)}, u32[]{:S(2)}, u32[]{:S(2)}) collective-permute-start(bf16[16,80,256]{2,1,0:T(8,128)(2,1)S(1)} %get-tuple-element.48.refs_0_), channel_id=1, source_target_pairs={{0,8},{4,12},{8,16},{12,20},{16,24},{20,28},{24,0},{28,4},{1,9},{5... | collective-permute-start | bytes 1966088 | tf_op jit(solution)/shard_map/ppermute | solution.py:270
  80.0 9.3 %collective-permute-start.13 = (bf16[16,80,256]{2,1,0:T(8,128)(2,1)S(1)}, bf16[16,80,256]{2,1,0:T(8,128)(2,1)S(1)}, u32[]{:S(2)}, u32[]{:S(2)}) collective-permute-start(bf16[16,80,256]{2,1,0:T(8,128)(2,1)S(1)} %get-tuple-element.51.refs_0_), channel_id=1, source_target_pairs={{0,4},{4,0},{8,12},{12,8},{16,20},{20,16},{24,28},{28,24},{1,5},{5... | collective-permute-start | bytes 1966088 | tf_op jit(solution)/shard_map/ppermute | solution.py:267
  80.0 23.3 %collective-permute-start.18 = (bf16[16,80,256]{2,1,0:T(8,128)(2,1)S(1)}, bf16[16,80,256]{2,1,0:T(8,128)(2,1)S(1)}, u32[]{:S(2)}, u32[]{:S(2)}) collective-permute-start(bf16[16,80,256]{2,1,0:T(8,128)(2,1)S(1)} %get-tuple-element.51.refs_0_), channel_id=1, source_target_pairs={{0,8},{4,12},{8,16},{12,20},{16,24},{20,28},{24,0},{28,4},{1,9},{5... | collective-permute-start | bytes 1966088 | tf_op jit(solution)/shard_map/ppermute | solution.py:270
  94.0 9.3 %collective-permute-start.17 = (bf16[16,80,256]{2,1,0:T(8,128)(2,1)S(1)}, bf16[16,80,256]{2,1,0:T(8,128)(2,1)S(1)}, u32[]{:S(2)}, u32[]{:S(2)}) collective-permute-start(bf16[16,80,256]{2,1,0:T(8,128)(2,1)S(1)} %get-tuple-element.53.refs_0_), channel_id=1, source_target_pairs={{0,4},{4,0},{8,12},{12,8},{16,20},{20,16},{24,28},{28,24},{1,5},{5... | collective-permute-start | bytes 1966088 | tf_op jit(solution)/shard_map/ppermute | solution.py:267
  94.0 22.0 %collective-permute-start.15 = (bf16[16,80,256]{2,1,0:T(8,128)(2,1)S(1)}, bf16[16,80,256]{2,1,0:T(8,128)(2,1)S(1)}, u32[]{:S(2)}, u32[]{:S(2)}) collective-permute-start(bf16[16,80,256]{2,1,0:T(8,128)(2,1)S(1)} %get-tuple-element.53.refs_0_), channel_id=1, source_target_pairs={{0,8},{4,12},{8,16},{12,20},{16,24},{20,28},{24,0},{28,4},{1,9},{5... | collective-permute-start | bytes 1966088 | tf_op jit(solution)/shard_map/ppermute | solution.py:270
  108.1 7.9 %collective-permute-start.19 = (bf16[16,80,256]{2,1,0:T(8,128)(2,1)S(1)}, bf16[16,80,256]{2,1,0:T(8,128)(2,1)S(1)}, u32[]{:S(2)}, u32[]{:S(2)}) collective-permute-start(bf16[16,80,256]{2,1,0:T(8,128)(2,1)S(1)} %get-tuple-element.55.refs_0_), channel_id=1, source_target_pairs={{0,4},{4,0},{8,12},{12,8},{16,20},{20,16},{24,28},{28,24},{1,5},{5... | collective-permute-start | bytes 1966088 | tf_op jit(solution)/shard_map/ppermute | solution.py:267
  116.0 4.8 %collective-permute-start.16 = (bf16[16,80,256]{2,1,0:T(8,128)(2,1)S(1)}, bf16[16,80,256]{2,1,0:T(8,128)(2,1)S(1)}, u32[]{:S(2)}, u32[]{:S(2)}) collective-permute-start(bf16[16,80,256]{2,1,0:T(8,128)(2,1)S(1)} %collective-permute-done.15.refs_0_), channel_id=1, source_target_pairs={{0,4},{4,0},{8,12},{12,8},{16,20},{20,16},{24,28},{28,24},{1,5},{5... | collective-permute-start | bytes 1966088 | tf_op jit(solution)/shard_map/ppermute | solution.py:267

commit v4 on v3

--- a/solution.py
+++ b/solution.py
@@ -276,9 +276,9 @@
         )
         return list(kept)
 
-    for c in range(chunks):
+    for c in reversed(range(chunks)):
         exchanged = [pieces[c][0]] + [lax.ppermute(pieces[c][d], "freq", swap[d]) for d in range(1, nodes)]
-        held = pieces[c + 1][-1:] if c + 1 < chunks else []
+        held = []
         travelling[c, 0], ours[c, 0], kept = pack_windows(me, exchanged, held, parts[c], windows)
         if held:
             pieces[c + 1][-1:] = kept

time: 126 us -> 125 us (level)
  waiting for transfers between devices: 59.5 us -> 56.3 us
  starting transfers between devices: 13.9 us -> 16 us
    ppermute x6, waiting for transfers between devices: 43.3 us -> 41.6 us  [send(): travelling[c, t] = lax.ppermute(travelling[c, t - 1], 'chan', ring)]
    ppermute x6, waiting for transfers between devices: 16.2 us -> 14.7 us  [shards(): lax.ppermute(pieces[c][d], 'freq', swap[d])]
    ppermute x6, starting transfers between devices: 9.5 us -> 11 us  [shards(): lax.ppermute(pieces[c][d], 'freq', swap[d])]
  transfers between devices with their start and end apart: 20 -> 20, of which waited for: 9 -> 9; matrix products, arithmetic and copies ran while one was open for 0% -> 0% of each run, Pallas kernels for 30% -> 31%
where the time goes in v4:
time: 125 us; the launch traced here: 124 us
  waiting for transfers between devices  56.3 us (45%)
  Pallas kernels  48.8 us (39%)
  starting transfers between devices  16 us (13%)
  local copies, waits for them, and re-layouts  2.63 us (2%)
    ppermute x6, waiting for transfers between devices, send(): travelling[c, t] = lax.ppermute(travelling[c, t - 1], 'chan', ring)  41.6 us
    pallas_call x8, Pallas kernels, pair_products(): pl.pallas_call(kernel, grid_spec=pltpu.PrefetchScalarGridSpec(num_scalar_...  40.2 us
    ppermute x6, waiting for transfers between devices, shards(): lax.ppermute(pieces[c][d], 'freq', swap[d])  14.7 us
    ppermute x6, starting transfers between devices, shards(): lax.ppermute(pieces[c][d], 'freq', swap[d])  11 us
    pallas_call x1, Pallas kernels, spectra_pieces(): pl.pallas_call(functools.partial(spectra_kernel, nodes), in_specs=[smem,...  5.92 us
    ppermute x6, starting transfers between devices, send(): travelling[c, t] = lax.ppermute(travelling[c, t - 1], 'chan', ring)  4.74 us
    unnamed x6, local copies, waits for them, and re-layouts  2.63 us
    pallas_call x2, Pallas kernels, pack_windows(): pl.pallas_call(kernel, in_specs=[pl.BlockSpec(memory_space=pltpu.SMEM)] +...  2.61 us
  transfers between devices with their start and end apart: 20, of which 9 were waited for; matrix products, arithmetic and copies ran while one was open for 0% of the time, Pallas kernels for 31%

profile of v4, /device:TPU:0, one launch (start us, length us, event | category | flops | bytes accessed | tf_op | source)
XLA Modules:
  0.0 124.4 jit_solution(6561787814645105561)
XLA Ops:
  0.7 0.0 copy-start
  0.7 1.0 copy-done
  1.7 0.7 copy-done.1
  2.4 5.9 %spectra.1 = (bf16[17,32,256]{2,1,0:T(8,128)(2,1)S(1)}, bf16[17,32,256]{2,1,0:T(8,128)(2,1)S(1)}, bf16[17,32,256]{2,1,0:T(8,128)(2,1)S(1)}, bf16[17,32,256]{2,1,...) custom-call(s32[1]{0:T(128)} %bitcast.1.me_ref, ...), custom_call_target="tpu_custom_call" | custom-call | flops 2147483648 | bytes 8388608 | tf_op jit(solution)/shard_map/spectra/pallas_call | solution.py:90
  8.3 3.0 %collective-permute-start.4 = (bf16[17,32,256]{2,1,0:T(8,128)(2,1)S(1)}, bf16[17,32,256]{2,1,0:T(8,128)(2,1)S(1)}, u32[]{:S(2)}, u32[]{:S(2)}) collective-permute-start(bf16[17,32,256]{2,1,0:T(8,128)(2,1)S(1)} %get-tuple-element.36), channel_id=1, source_target_pairs={{0,1},{1,0},{2,3},{3,2},{4,5},{5,4},{6,7},{7,6},{8,9},{9,8},{10,11... | collective-permute-start | bytes 835592 | tf_op jit(solution)/shard_map/ppermute | solution.py:280
  11.3 1.5 %collective-permute-start.5 = (bf16[17,32,256]{2,1,0:T(8,128)(2,1)S(1)}, bf16[17,32,256]{2,1,0:T(8,128)(2,1)S(1)}, u32[]{:S(2)}, u32[]{:S(2)}) collective-permute-start(bf16[17,32,256]{2,1,0:T(8,128)(2,1)S(1)} %get-tuple-element.37), channel_id=1, source_target_pairs={{0,2},{1,3},{2,0},{3,1},{4,6},{5,7},{6,4},{7,5},{8,10},{9,11},{10,... | collective-permute-start | bytes 835592 | tf_op jit(solution)/shard_map/ppermute | solution.py:280
  12.9 0.0 collective-permute-start.6
  12.9 1.9 %collective-permute-start = (bf16[17,32,256]{2,1,0:T(8,128)(2,1)S(1)}, bf16[17,32,256]{2,1,0:T(8,128)(2,1)S(1)}, u32[]{:S(2)}, u32[]{:S(2)}) collective-permute-start(bf16[17,32,256]{2,1,0:T(8,128)(2,1)S(1)} %get-tuple-element.31), channel_id=1, source_target_pairs={{0,1},{1,0},{2,3},{3,2},{4,5},{5,4},{6,7},{7,6},{8,9},{9,8},{10,11... | collective-permute-start | bytes 835592 | tf_op jit(solution)/shard_map/ppermute | solution.py:280
  14.8 1.5 %collective-permute-start.1 = (bf16[17,32,256]{2,1,0:T(8,128)(2,1)S(1)}, bf16[17,32,256]{2,1,0:T(8,128)(2,1)S(1)}, u32[]{:S(2)}, u32[]{:S(2)}) collective-permute-start(bf16[17,32,256]{2,1,0:T(8,128)(2,1)S(1)} %get-tuple-element.32), channel_id=1, source_target_pairs={{0,2},{1,3},{2,0},{3,1},{4,6},{5,7},{6,4},{7,5},{8,10},{9,11},{10,... | collective-permute-start | bytes 835592 | tf_op jit(solution)/shard_map/ppermute | solution.py:280
  16.3 2.5 %collective-permute-done.4.refs_1_ = bf16[17,32,256]{2,1,0:T(8,128)(2,1)S(1)} collective-permute-done((bf16[17,32,256]{2,1,0:T(8,128)(2,1)S(1)}, bf16[17,32,256]{2,1,0:T(8,128)(2,1)S(1)}, u32[]{:S(2)}, u32[]{:S(2)}) %collective-permute-start.4) | collective-permute-done | bytes 278560 | tf_op jit(solution)/shard_map/ppermute | solution.py:280
  18.8 3.0 %collective-permute-start.2 = (bf16[17,32,256]{2,1,0:T(8,128)(2,1)S(1)}, bf16[17,32,256]{2,1,0:T(8,128)(2,1)S(1)}, u32[]{:S(2)}, u32[]{:S(2)}) collective-permute-start(bf16[17,32,256]{2,1,0:T(8,128)(2,1)S(1)} %get-tuple-element.33), channel_id=1, source_target_pairs={{0,3},{1,2},{2,1},{3,0},{4,7},{5,6},{6,5},{7,4},{8,11},{9,10},{10,... | collective-permute-start | bytes 835592 | tf_op jit(solution)/shard_map/ppermute | solution.py:280
  21.8 5.1 %collective-permute-done.5.refs_2_ = bf16[17,32,256]{2,1,0:T(8,128)(2,1)S(1)} collective-permute-done((bf16[17,32,256]{2,1,0:T(8,128)(2,1)S(1)}, bf16[17,32,256]{2,1,0:T(8,128)(2,1)S(1)}, u32[]{:S(2)}, u32[]{:S(2)}) %collective-permute-start.5) | collective-permute-done | bytes 278560 | tf_op jit(solution)/shard_map/ppermute | solution.py:280
  26.9 1.7 %pack.3 = (bf16[16,80,256]{2,1,0:T(8,128)(2,1)}, bf16[16,80,256]{2,1,0:T(8,128)(2,1)S(1)}) custom-call(s32[1]{0:T(128)} %bitcast.1.me_ref, bf16[17,32,256]{2,1,0:T(8,128)(2,1)S(1)} %get-tuple-element.35.refs_0_, bf16[17,32,256]{2,1,0:T(8,128)(2,1)S(1)} %collective-permute-done.4.refs_1_, bf16[17,32,256]{2,1,0:T(8,128)(2,1)S(1)} %collective-permute-done.5.refs_2_, ...), custom_call_target="tpu_custom_call" | custom-call | flops 1024 | bytes 1024 | tf_op jit(solution)/shard_map/pack/pallas_call | solution.py:149
  28.6 1.6 %collective-permute-start.8 = (bf16[16,80,256]{2,1,0:T(8,128)(2,1)}, bf16[16,80,256]{2,1,0:T(8,128)(2,1)S(1)}, u32[]{:S(2)}, u32[]{:S(2)}) collective-permute-start(bf16[16,80,256]{2,1,0:T(8,128)(2,1)} %get-tuple-element.41), channel_id=1, source_target_pairs={{0,8},{4,12},{8,16},{12,20},{16,24},{20,28},{24,0},{28,4},{1,9},{5... | collective-permute-start | bytes 1966088 | tf_op jit(solution)/shard_map/ppermute | solution.py:270
  30.2 0.0 collective-permute-start.7
  30.2 0.6 collective-permute-done.refs_1_
  30.8 6.6 %collective-permute-done.1.refs_2_ = bf16[17,32,256]{2,1,0:T(8,128)(2,1)S(1)} collective-permute-done((bf16[17,32,256]{2,1,0:T(8,128)(2,1)S(1)}, bf16[17,32,256]{2,1,0:T(8,128)(2,1)S(1)}, u32[]{:S(2)}, u32[]{:S(2)}) %collective-permute-start.1) | collective-permute-done | bytes 278560 | tf_op jit(solution)/shard_map/ppermute | solution.py:280
  37.4 0.0 collective-permute-done.2.refs_3_
  37.4 0.9 pack.2
  38.3 0.9 copy-done.2
  39.2 0.0 collective-permute-start.3
  39.2 1.6 %collective-permute-start.10 = (bf16[16,80,256]{2,1,0:T(8,128)(2,1)}, bf16[16,80,256]{2,1,0:T(8,128)(2,1)S(1)}, u32[]{:S(2)}, u32[]{:S(2)}) collective-permute-start(bf16[16,80,256]{2,1,0:T(8,128)(2,1)} %copy-done.2), channel_id=1, source_target_pairs={{0,8},{4,12},{8,16},{12,20},{16,24},{20,28},{24,0},{28,4},{1,9},{5... | collective-permute-start | bytes 1966088 | tf_op jit(solution)/shard_map/ppermute | solution.py:270
  40.7 5.8 %pairs.8 = (bf16[2,32,256,2048]{3,2,1,0:T(8,128)(2,1)}, bf16[16,512,80]{2,1,0:T(8,128)(2,1)S(1)}) custom-call(s32[1]{0:T(128)} %bitcast.place_ref, bf16[16,80,256]{2,1,0:T(8,128)(2,1)S(1)} %get-tuple-element.39.refs_0_, bf16[16,80,256]{2,1,0:T(8,128)(2,1)S(1)} %collective-permute-done.7.refs_1_), custom_call_target="tpu_custom_call" | custom-call | flops 1024 | bytes 1024 | tf_op jit(solution)/shard_map/pairs/pallas_call | solution.py:228
  46.6 0.0 collective-permute-done.8.refs_3_
  46.6 5.8 %pairs.9 = (bf16[2,32,256,2048]{3,2,1,0:T(8,128)(2,1)}, bf16[16,512,80]{2,1,0:T(8,128)(2,1)S(1)}, bf16[16,80,256]{2,1,0:T(8,128)(2,1)S(1)}) custom-call(s32[1]{0:T(128)} %bitcast.place_ref, bf16[16,80,256]{2,1,0:T(8,128)(2,1)S(1)} %get-tuple-element.34.refs_0_, ...), custom_call_target="tpu_custom_call", output_to_operand_aliasing={{0}: (3, {}), {2}: (4, {})} | custom-call | flops 1024 | bytes 1024 | tf_op jit(solution)/shard_map/pairs/pallas_call | solution.py:228
  52.4 0.2 collective-permute-start.9
  52.6 1.6 %collective-permute-start.12 = (bf16[16,80,256]{2,1,0:T(8,128)(2,1)S(1)}, bf16[16,80,256]{2,1,0:T(8,128)(2,1)S(1)}, u32[]{:S(2)}, u32[]{:S(2)}) collective-permute-start(bf16[16,80,256]{2,1,0:T(8,128)(2,1)S(1)} %get-tuple-element.42.refs_0_), channel_id=1, source_target_pairs={{0,8},{4,12},{8,16},{12,20},{16,24},{20,28},{24,0},{28,4},{1,9},{5... | collective-permute-start | bytes 1966088 | tf_op jit(solution)/shard_map/ppermute | solution.py:270
  54.2 4.6 %collective-permute-done.10.refs_4_ = bf16[16,80,256]{2,1,0:T(8,128)(2,1)S(1)} collective-permute-done((bf16[16,80,256]{2,1,0:T(8,128)(2,1)}, bf16[16,80,256]{2,1,0:T(8,128)(2,1)S(1)}, u32[]{:S(2)}, u32[]{:S(2)}) %collective-permute-start.10) | collective-permute-done | bytes 655392 | tf_op jit(solution)/shard_map/ppermute | solution.py:270
  58.9 0.0 collective-permute-done.9.refs_1_
  58.9 4.8 %pairs.10 = (bf16[2,32,256,2048]{3,2,1,0:T(8,128)(2,1)}, bf16[16,80,256]{2,1,0:T(8,128)(2,1)S(1)}) custom-call(s32[1]{0:T(128)} %bitcast.place_ref, bf16[16,80,256]{2,1,0:T(8,128)(2,1)S(1)} %get-tuple-element.42.refs_0_, bf16[16,80,256]{2,1,0:T(8,128)(2,1)S(1)} %collective-permute-done.9.refs_1_, ...), custom_call_target="tpu_custom_call", output_to_operand_aliasing={{0}: (4, {}), {1}: (5, {})} | custom-call | flops 1024 | bytes 1024 | tf_op jit(solution)/shard_map/pairs/pallas_call | solution.py:228
  63.6 9.3 %collective-permute-done.12.refs_4_ = bf16[16,80,256]{2,1,0:T(8,128)(2,1)S(1)} collective-permute-done((bf16[16,80,256]{2,1,0:T(8,128)(2,1)S(1)}, bf16[16,80,256]{2,1,0:T(8,128)(2,1)S(1)}, u32[]{:S(2)}, u32[]{:S(2)}) %collective-permute-start.12) | collective-permute-done | bytes 655392 | tf_op jit(solution)/shard_map/ppermute | solution.py:270
  72.9 0.0 collective-permute-done.11.refs_1_
  72.9 4.8 %pairs.11 = (bf16[2,32,256,2048]{3,2,1,0:T(8,128)(2,1)}, bf16[16,80,256]{2,1,0:T(8,128)(2,1)S(1)}) custom-call(s32[1]{0:T(128)} %bitcast.place_ref, bf16[16,80,256]{2,1,0:T(8,128)(2,1)S(1)} %get-tuple-element.46.refs_0_, bf16[16,80,256]{2,1,0:T(8,128)(2,1)S(1)} %collective-permute-done.11.refs_1_, ...), custom_call_target="tpu_custom_call", output_to_operand_aliasing={{0}: (4, {}), {1}: (5, {})} | custom-call | flops 1024 | bytes 1024 | tf_op jit(solution)/shard_map/pairs/pallas_call | solution.py:228
  77.7 0.0 collective-permute-start.13
  77.7 0.0 collective-permute-start.18
  77.7 9.3 %collective-permute-done.14.refs_4_ = bf16[16,80,256]{2,1,0:T(8,128)(2,1)S(1)} collective-permute-done((bf16[16,80,256]{2,1,0:T(8,128)(2,1)S(1)}, bf16[16,80,256]{2,1,0:T(8,128)(2,1)S(1)}, u32[]{:S(2)}, u32[]{:S(2)}) %collective-permute-start.14) | collective-permute-done | bytes 655392 | tf_op jit(solution)/shard_map/ppermute | solution.py:270
  86.9 0.0 collective-permute-done.13.refs_1_
  86.9 4.7 %pairs.12 = (bf16[2,32,256,2048]{3,2,1,0:T(8,128)(2,1)}, bf16[16,80,256]{2,1,0:T(8,128)(2,1)S(1)}) custom-call(s32[1]{0:T(128)} %bitcast.place_ref, bf16[16,80,256]{2,1,0:T(8,128)(2,1)S(1)} %get-tuple-element.49.refs_0_, bf16[16,80,256]{2,1,0:T(8,128)(2,1)S(1)} %collective-permute-done.13.refs_1_, ...), custom_call_target="tpu_custom_call", output_to_operand_aliasing={{0}: (4, {}), {1}: (5, {})} | custom-call | flops 1024 | bytes 1024 | tf_op jit(solution)/shard_map/pairs/pallas_call | solution.py:228
  91.7 0.0 collective-permute-start.17
  91.7 0.0 collective-permute-start.15
  91.7 9.3 %collective-permute-done.18.refs_4_ = bf16[16,80,256]{2,1,0:T(8,128)(2,1)S(1)} collective-permute-done((bf16[16,80,256]{2,1,0:T(8,128)(2,1)S(1)}, bf16[16,80,256]{2,1,0:T(8,128)(2,1)S(1)}, u32[]{:S(2)}, u32[]{:S(2)}) %collective-permute-start.18) | collective-permute-done | bytes 655392 | tf_op jit(solution)/shard_map/ppermute | solution.py:270
  101.0 0.0 collective-permute-done.17.refs_1_
  101.0 4.8 %pairs.13 = (bf16[2,32,256,2048]{3,2,1,0:T(8,128)(2,1)}, bf16[16,80,256]{2,1,0:T(8,128)(2,1)S(1)}) custom-call(s32[1]{0:T(128)} %bitcast.place_ref, bf16[16,80,256]{2,1,0:T(8,128)(2,1)S(1)} %get-tuple-element.51.refs_0_, bf16[16,80,256]{2,1,0:T(8,128)(2,1)S(1)} %collective-permute-done.17.refs_1_, ...), custom_call_target="tpu_custom_call", output_to_operand_aliasing={{0}: (4, {}), {1}: (5, {})} | custom-call | flops 1024 | bytes 1024 | tf_op jit(solution)/shard_map/pairs/pallas_call | solution.py:228
  105.8 9.1 %collective-permute-done.15.refs_0_ = bf16[16,80,256]{2,1,0:T(8,128)(2,1)S(1)} collective-permute-done((bf16[16,80,256]{2,1,0:T(8,128)(2,1)S(1)}, bf16[16,80,256]{2,1,0:T(8,128)(2,1)S(1)}, u32[]{:S(2)}, u32[]{:S(2)}) %collective-permute-start.15) | collective-permute-done | bytes 655392 | tf_op jit(solution)/shard_map/ppermute | solution.py:270
  114.8 0.0 collective-permute-start.16
  114.8 0.0 collective-permute-done.19.refs_1_
  114.8 4.8 %pairs.14.refs_3_ = bf16[2,32,256,2048]{3,2,1,0:T(8,128)(2,1)} custom-call(s32[1]{0:T(128)} %bitcast.place_ref, bf16[16,80,256]{2,1,0:T(8,128)(2,1)S(1)} %get-tuple-element.53.refs_0_, bf16[16,80,256]{2,1,0:T(8,128)(2,1)S(1)} %collective-permute-done.19.refs_1_, bf16[16,512,80]{2,1,0:T(8,128)(2,1)S(1)} %get-tuple-element.43.refs_2_, ...), custom_call_target="tpu_custom_call", output_to_operand_aliasing={{}: (4, {})} | custom-call | flops 1024 | bytes 1024 | tf_op jit(solution)/shard_map/pairs/pallas_call | solution.py:228
  119.6 4.8 %pairs.15 = bf16[2,32,256,2048]{3,2,1,0:T(8,128)(2,1)} custom-call(s32[1]{0:T(128)} %bitcast.place_ref, bf16[16,80,256]{2,1,0:T(8,128)(2,1)S(1)} %collective-permute-done.15.refs_0_, bf16[16,80,256]{2,1,0:T(8,128)(2,1)S(1)} %collective-permute-done.16.refs_1_, bf16[16,512,80]{2,1,0:T(8,128)(2,1)S(1)} %get-tuple-element.47.refs_2_, ...), custom_call_target="tpu_custom_call", output_to_operand_aliasing={{}: (4, {})} | custom-call | flops 1024 | bytes 1024 | tf_op jit(solution)/shard_map/pairs/pallas_call | solution.py:228
  (9 shorter events, 0.0 us)
Async XLA Ops:
  0.7 1.0 copy-start
  1.7 0.7 copy-start.1
  8.3 10.5 %collective-permute-start.4 = (bf16[17,32,256]{2,1,0:T(8,128)(2,1)S(1)}, bf16[17,32,256]{2,1,0:T(8,128)(2,1)S(1)}, u32[]{:S(2)}, u32[]{:S(2)}) collective-permute-start(bf16[17,32,256]{2,1,0:T(8,128)(2,1)S(1)} %get-tuple-element.36), channel_id=1, source_target_pairs={{0,1},{1,0},{2,3},{3,2},{4,5},{5,4},{6,7},{7,6},{8,9},{9,8},{10,11... | collective-permute-start | bytes 835592 | tf_op jit(solution)/shard_map/ppermute | solution.py:280
  11.3 15.6 %collective-permute-start.5 = (bf16[17,32,256]{2,1,0:T(8,128)(2,1)S(1)}, bf16[17,32,256]{2,1,0:T(8,128)(2,1)S(1)}, u32[]{:S(2)}, u32[]{:S(2)}) collective-permute-start(bf16[17,32,256]{2,1,0:T(8,128)(2,1)S(1)} %get-tuple-element.37), channel_id=1, source_target_pairs={{0,2},{1,3},{2,0},{3,1},{4,6},{5,7},{6,4},{7,5},{8,10},{9,11},{10,... | collective-permute-start | bytes 835592 | tf_op jit(solution)/shard_map/ppermute | solution.py:280
  12.9 14.0 %collective-permute-start.6 = (bf16[17,32,256]{2,1,0:T(8,128)(2,1)S(1)}, bf16[17,32,256]{2,1,0:T(8,128)(2,1)S(1)}, u32[]{:S(2)}, u32[]{:S(2)}) collective-permute-start(bf16[17,32,256]{2,1,0:T(8,128)(2,1)S(1)} %get-tuple-element.38), channel_id=1, source_target_pairs={{0,3},{1,2},{2,1},{3,0},{4,7},{5,6},{6,5},{7,4},{8,11},{9,10},{10,... | collective-permute-start | bytes 835592 | tf_op jit(solution)/shard_map/ppermute | solution.py:280
  12.9 17.9 %collective-permute-start = (bf16[17,32,256]{2,1,0:T(8,128)(2,1)S(1)}, bf16[17,32,256]{2,1,0:T(8,128)(2,1)S(1)}, u32[]{:S(2)}, u32[]{:S(2)}) collective-permute-start(bf16[17,32,256]{2,1,0:T(8,128)(2,1)S(1)} %get-tuple-element.31), channel_id=1, source_target_pairs={{0,1},{1,0},{2,3},{3,2},{4,5},{5,4},{6,7},{7,6},{8,9},{9,8},{10,11... | collective-permute-start | bytes 835592 | tf_op jit(solution)/shard_map/ppermute | solution.py:280
  14.8 22.5 %collective-permute-start.1 = (bf16[17,32,256]{2,1,0:T(8,128)(2,1)S(1)}, bf16[17,32,256]{2,1,0:T(8,128)(2,1)S(1)}, u32[]{:S(2)}, u32[]{:S(2)}) collective-permute-start(bf16[17,32,256]{2,1,0:T(8,128)(2,1)S(1)} %get-tuple-element.32), channel_id=1, source_target_pairs={{0,2},{1,3},{2,0},{3,1},{4,6},{5,7},{6,4},{7,5},{8,10},{9,11},{10,... | collective-permute-start | bytes 835592 | tf_op jit(solution)/shard_map/ppermute | solution.py:280
  18.8 18.5 %collective-permute-start.2 = (bf16[17,32,256]{2,1,0:T(8,128)(2,1)S(1)}, bf16[17,32,256]{2,1,0:T(8,128)(2,1)S(1)}, u32[]{:S(2)}, u32[]{:S(2)}) collective-permute-start(bf16[17,32,256]{2,1,0:T(8,128)(2,1)S(1)} %get-tuple-element.33), channel_id=1, source_target_pairs={{0,3},{1,2},{2,1},{3,0},{4,7},{5,6},{6,5},{7,4},{8,11},{9,10},{10,... | collective-permute-start | bytes 835592 | tf_op jit(solution)/shard_map/ppermute | solution.py:280
  28.6 17.9 %collective-permute-start.8 = (bf16[16,80,256]{2,1,0:T(8,128)(2,1)}, bf16[16,80,256]{2,1,0:T(8,128)(2,1)S(1)}, u32[]{:S(2)}, u32[]{:S(2)}) collective-permute-start(bf16[16,80,256]{2,1,0:T(8,128)(2,1)} %get-tuple-element.41), channel_id=1, source_target_pairs={{0,8},{4,12},{8,16},{12,20},{16,24},{20,28},{24,0},{28,4},{1,9},{5... | collective-permute-start | bytes 1966088 | tf_op jit(solution)/shard_map/ppermute | solution.py:270
  30.2 10.5 %collective-permute-start.7 = (bf16[16,80,256]{2,1,0:T(8,128)(2,1)S(1)}, bf16[16,80,256]{2,1,0:T(8,128)(2,1)S(1)}, u32[]{:S(2)}, u32[]{:S(2)}) collective-permute-start(bf16[16,80,256]{2,1,0:T(8,128)(2,1)S(1)} %get-tuple-element.39.refs_0_), channel_id=1, source_target_pairs={{0,4},{4,0},{8,12},{12,8},{16,20},{20,16},{24,28},{28,24},{1,5},{5... | collective-permute-start | bytes 1966088 | tf_op jit(solution)/shard_map/ppermute | solution.py:267
  38.3 0.9 copy-start.2
  39.2 7.4 %collective-permute-start.3 = (bf16[16,80,256]{2,1,0:T(8,128)(2,1)S(1)}, bf16[16,80,256]{2,1,0:T(8,128)(2,1)S(1)}, u32[]{:S(2)}, u32[]{:S(2)}) collective-permute-start(bf16[16,80,256]{2,1,0:T(8,128)(2,1)S(1)} %get-tuple-element.34.refs_0_), channel_id=1, source_target_pairs={{0,4},{4,0},{8,12},{12,8},{16,20},{20,16},{24,28},{28,24},{1,5},{5... | collective-permute-start | bytes 1966088 | tf_op jit(solution)/shard_map/ppermute | solution.py:267
  39.2 19.7 %collective-permute-start.10 = (bf16[16,80,256]{2,1,0:T(8,128)(2,1)}, bf16[16,80,256]{2,1,0:T(8,128)(2,1)S(1)}, u32[]{:S(2)}, u32[]{:S(2)}) collective-permute-start(bf16[16,80,256]{2,1,0:T(8,128)(2,1)} %copy-done.2), channel_id=1, source_target_pairs={{0,8},{4,12},{8,16},{12,20},{16,24},{20,28},{24,0},{28,4},{1,9},{5... | collective-permute-start | bytes 1966088 | tf_op jit(solution)/shard_map/ppermute | solution.py:270
  52.4 6.5 %collective-permute-start.9 = (bf16[16,80,256]{2,1,0:T(8,128)(2,1)S(1)}, bf16[16,80,256]{2,1,0:T(8,128)(2,1)S(1)}, u32[]{:S(2)}, u32[]{:S(2)}) collective-permute-start(bf16[16,80,256]{2,1,0:T(8,128)(2,1)S(1)} %get-tuple-element.42.refs_0_), channel_id=1, source_target_pairs={{0,4},{4,0},{8,12},{12,8},{16,20},{20,16},{24,28},{28,24},{1,5},{5... | collective-permute-start | bytes 1966088 | tf_op jit(solution)/shard_map/ppermute | solution.py:267
  52.6 20.3 %collective-permute-start.12 = (bf16[16,80,256]{2,1,0:T(8,128)(2,1)S(1)}, bf16[16,80,256]{2,1,0:T(8,128)(2,1)S(1)}, u32[]{:S(2)}, u32[]{:S(2)}) collective-permute-start(bf16[16,80,256]{2,1,0:T(8,128)(2,1)S(1)} %get-tuple-element.42.refs_0_), channel_id=1, source_target_pairs={{0,8},{4,12},{8,16},{12,20},{16,24},{20,28},{24,0},{28,4},{1,9},{5... | collective-permute-start | bytes 1966088 | tf_op jit(solution)/shard_map/ppermute | solution.py:270
  63.6 9.3 %collective-permute-start.11 = (bf16[16,80,256]{2,1,0:T(8,128)(2,1)S(1)}, bf16[16,80,256]{2,1,0:T(8,128)(2,1)S(1)}, u32[]{:S(2)}, u32[]{:S(2)}) collective-permute-start(bf16[16,80,256]{2,1,0:T(8,128)(2,1)S(1)} %get-tuple-element.46.refs_0_), channel_id=1, source_target_pairs={{0,4},{4,0},{8,12},{12,8},{16,20},{20,16},{24,28},{28,24},{1,5},{5... | collective-permute-start | bytes 1966088 | tf_op jit(solution)/shard_map/ppermute | solution.py:267
  63.6 23.3 %collective-permute-start.14 = (bf16[16,80,256]{2,1,0:T(8,128)(2,1)S(1)}, bf16[16,80,256]{2,1,0:T(8,128)(2,1)S(1)}, u32[]{:S(2)}, u32[]{:S(2)}) collective-permute-start(bf16[16,80,256]{2,1,0:T(8,128)(2,1)S(1)} %get-tuple-element.46.refs_0_), channel_id=1, source_target_pairs={{0,8},{4,12},{8,16},{12,20},{16,24},{20,28},{24,0},{28,4},{1,9},{5... | collective-permute-start | bytes 1966088 | tf_op jit(solution)/shard_map/ppermute | solution.py:270
  77.7 9.3 %collective-permute-start.13 = (bf16[16,80,256]{2,1,0:T(8,128)(2,1)S(1)}, bf16[16,80,256]{2,1,0:T(8,128)(2,1)S(1)}, u32[]{:S(2)}, u32[]{:S(2)}) collective-permute-start(bf16[16,80,256]{2,1,0:T(8,128)(2,1)S(1)} %get-tuple-element.49.refs_0_), channel_id=1, source_target_pairs={{0,4},{4,0},{8,12},{12,8},{16,20},{20,16},{24,28},{28,24},{1,5},{5... | collective-permute-start | bytes 1966088 | tf_op jit(solution)/shard_map/ppermute | solution.py:267
  77.7 23.3 %collective-permute-start.18 = (bf16[16,80,256]{2,1,0:T(8,128)(2,1)S(1)}, bf16[16,80,256]{2,1,0:T(8,128)(2,1)S(1)}, u32[]{:S(2)}, u32[]{:S(2)}) collective-permute-start(bf16[16,80,256]{2,1,0:T(8,128)(2,1)S(1)} %get-tuple-element.49.refs_0_), channel_id=1, source_target_pairs={{0,8},{4,12},{8,16},{12,20},{16,24},{20,28},{24,0},{28,4},{1,9},{5... | collective-permute-start | bytes 1966088 | tf_op jit(solution)/shard_map/ppermute | solution.py:270
  91.7 9.3 %collective-permute-start.17 = (bf16[16,80,256]{2,1,0:T(8,128)(2,1)S(1)}, bf16[16,80,256]{2,1,0:T(8,128)(2,1)S(1)}, u32[]{:S(2)}, u32[]{:S(2)}) collective-permute-start(bf16[16,80,256]{2,1,0:T(8,128)(2,1)S(1)} %get-tuple-element.51.refs_0_), channel_id=1, source_target_pairs={{0,4},{4,0},{8,12},{12,8},{16,20},{20,16},{24,28},{28,24},{1,5},{5... | collective-permute-start | bytes 1966088 | tf_op jit(solution)/shard_map/ppermute | solution.py:267
  91.7 23.1 %collective-permute-start.15 = (bf16[16,80,256]{2,1,0:T(8,128)(2,1)S(1)}, bf16[16,80,256]{2,1,0:T(8,128)(2,1)S(1)}, u32[]{:S(2)}, u32[]{:S(2)}) collective-permute-start(bf16[16,80,256]{2,1,0:T(8,128)(2,1)S(1)} %get-tuple-element.51.refs_0_), channel_id=1, source_target_pairs={{0,8},{4,12},{8,16},{12,20},{16,24},{20,28},{24,0},{28,4},{1,9},{5... | collective-permute-start | bytes 1966088 | tf_op jit(solution)/shard_map/ppermute | solution.py:270
  105.7 9.1 %collective-permute-start.19 = (bf16[16,80,256]{2,1,0:T(8,128)(2,1)S(1)}, bf16[16,80,256]{2,1,0:T(8,128)(2,1)S(1)}, u32[]{:S(2)}, u32[]{:S(2)}) collective-permute-start(bf16[16,80,256]{2,1,0:T(8,128)(2,1)S(1)} %get-tuple-element.53.refs_0_), channel_id=1, source_target_pairs={{0,4},{4,0},{8,12},{12,8},{16,20},{20,16},{24,28},{28,24},{1,5},{5... | collective-permute-start | bytes 1966088 | tf_op jit(solution)/shard_map/ppermute | solution.py:267
  114.8 4.8 %collective-permute-start.16 = (bf16[16,80,256]{2,1,0:T(8,128)(2,1)S(1)}, bf16[16,80,256]{2,1,0:T(8,128)(2,1)S(1)}, u32[]{:S(2)}, u32[]{:S(2)}) collective-permute-start(bf16[16,80,256]{2,1,0:T(8,128)(2,1)S(1)} %collective-permute-done.15.refs_0_), channel_id=1, source_target_pairs={{0,4},{4,0},{8,12},{12,8},{16,20},{20,16},{24,28},{28,24},{1,5},{5... | collective-permute-start | bytes 1966088 | tf_op jit(solution)/shard_map/ppermute | solution.py:267

commit v5 on v4

--- a/solution.py
+++ b/solution.py
@@ -240,6 +240,20 @@
     return result[0], rows, result[len(result) - len(held):]
 
 
+def tie(arrays):
+    anywhere = pl.BlockSpec(memory_space=pl.ANY)
+    return pl.pallas_call(
+        lambda *refs: None,
+        in_specs=[anywhere] * len(arrays),
+        out_specs=[anywhere] * len(arrays),
+        out_shape=[jax.ShapeDtypeStruct(array.shape, array.dtype) for array in arrays],
+        input_output_aliases={k: k for k in range(len(arrays))},
+        compiler_params=pltpu.CompilerParams(vmem_limit_bytes=1 << 20),
+        cost_estimate=pl.CostEstimate(flops=1, bytes_accessed=1, transcendentals=0),
+        name="tie",
+    )(*arrays)
+
+
 def shards(nodes, groups, segments, available, node_windows):
     slots, chan, samples = segments.shape
     bins = FREQS // nodes
@@ -305,9 +319,22 @@
     for k, now in enumerate(order):
         if ready and k + 1 < len(order):
             (travelling[now],) = multiply(*ready.pop(0), [travelling[now]])
+        elif ready:
+            while len(ready) > 1:
+                multiply(*ready.pop(0))
+            c, t = ready.pop(0)
+            half = ours[c, t].shape[0] // 2
+            for b in (0, half):
+                mine = ours[c, t][b:b + half]
+                out, _, _ = pair_products(
+                    place, mine, lax.ppermute(mine, "chan", cores), rows[c][b:b + half], out, [],
+                    bins, groups, starts[c] + b, t, scale,
+                )
+            travelling[now], out = tie([travelling[now], out])
         ours[now] = travelling[now]
         launch(k + 1)
-        meet(*now)
+        if k + 2 != len(order) or chunks < 2:
+            meet(*now)
         ready.append(now)
         if now[1] == 1 and now[0] not in rows and (now[0], 0) not in ready:
             meet(now[0], 0)

time: 125 us -> 122 us (0.976)
  waiting for transfers between devices: 56.3 us -> 52.1 us
    ppermute x6, waiting for transfers between devices: 41.6 us -> 34.4 us  [send(): travelling[c, t] = lax.ppermute(travelling[c, t - 1], 'chan', ring)]
    ppermute x8 -> x7, waiting for transfers between devices: 0.02 us -> 2.11 us  [meet(): theirs[c, t] = lax.ppermute(ours[c, t], 'chan', cores)]
    pallas_call x8 -> x9, Pallas kernels: 40.2 us -> 40.9 us  [pair_products(): pl.pallas_call(kernel, grid_spec=pltpu.PrefetchScalarGridSpec(num_scalar_...]
  transfers between devices with their start and end apart: 20 -> 21, of which waited for: 9 -> 11; matrix products, arithmetic and copies ran while one was open for 0% -> 0% of each run, Pallas kernels for 31% -> 32%
where the time goes in v5:
time: 122 us
  waiting for transfers between devices  52.1 us (43%)
  Pallas kernels  49.4 us (40%)
  starting transfers between devices  16.6 us (14%)
  local copies, waits for them, and re-layouts  2.84 us (2%)
    pallas_call x9, Pallas kernels, pair_products(): pl.pallas_call(kernel, grid_spec=pltpu.PrefetchScalarGridSpec(num_scalar_...  40.9 us
    ppermute x6, waiting for transfers between devices, send(): travelling[c, t] = lax.ppermute(travelling[c, t - 1], 'chan', ring)  34.4 us
    ppermute x6, waiting for transfers between devices, shards(): lax.ppermute(pieces[c][d], 'freq', swap[d])  14.7 us
    ppermute x6, starting transfers between devices, shards(): lax.ppermute(pieces[c][d], 'freq', swap[d])  11 us
    pallas_call x1, Pallas kernels, spectra_pieces(): pl.pallas_call(functools.partial(spectra_kernel, nodes), in_specs=[smem,...  5.92 us
    ppermute x6, starting transfers between devices, send(): travelling[c, t] = lax.ppermute(travelling[c, t - 1], 'chan', ring)  4.74 us
    pallas_call x2, Pallas kernels, pack_windows(): pl.pallas_call(kernel, in_specs=[pl.BlockSpec(memory_space=pltpu.SMEM)] +...  2.62 us
    unnamed x6, local copies, waits for them, and re-layouts  2.61 us
  transfers between devices with their start and end apart: 21, of which 11 were waited for; matrix products, arithmetic and copies ran while one was open for 0% of the time, Pallas kernels for 32%

profile of v5, /device:TPU:0, one launch (start us, length us, event | category | flops | bytes accessed | tf_op | source)
XLA Modules:
  0.0 121.7 jit_solution(16883191125792550232)
XLA Ops:
  0.7 0.0 copy-start
  0.7 1.0 copy-done
  1.7 0.7 copy-done.1
  2.4 5.9 %spectra.1 = (bf16[17,32,256]{2,1,0:T(8,128)(2,1)S(1)}, bf16[17,32,256]{2,1,0:T(8,128)(2,1)S(1)}, bf16[17,32,256]{2,1,0:T(8,128)(2,1)S(1)}, bf16[17,32,256]{2,1,...) custom-call(s32[1]{0:T(128)} %bitcast.1.me_ref, ...), custom_call_target="tpu_custom_call" | custom-call | flops 2147483648 | bytes 8388608 | tf_op jit(solution)/shard_map/spectra/pallas_call | solution.py:90
  8.3 3.0 %collective-permute-start.4 = (bf16[17,32,256]{2,1,0:T(8,128)(2,1)S(1)}, bf16[17,32,256]{2,1,0:T(8,128)(2,1)S(1)}, u32[]{:S(2)}, u32[]{:S(2)}) collective-permute-start(bf16[17,32,256]{2,1,0:T(8,128)(2,1)S(1)} %get-tuple-element.38), channel_id=1, source_target_pairs={{0,1},{1,0},{2,3},{3,2},{4,5},{5,4},{6,7},{7,6},{8,9},{9,8},{10,11... | collective-permute-start | bytes 835592 | tf_op jit(solution)/shard_map/ppermute | solution.py:294
  11.3 1.5 %collective-permute-start.5 = (bf16[17,32,256]{2,1,0:T(8,128)(2,1)S(1)}, bf16[17,32,256]{2,1,0:T(8,128)(2,1)S(1)}, u32[]{:S(2)}, u32[]{:S(2)}) collective-permute-start(bf16[17,32,256]{2,1,0:T(8,128)(2,1)S(1)} %get-tuple-element.39), channel_id=1, source_target_pairs={{0,2},{1,3},{2,0},{3,1},{4,6},{5,7},{6,4},{7,5},{8,10},{9,11},{10,... | collective-permute-start | bytes 835592 | tf_op jit(solution)/shard_map/ppermute | solution.py:294
  12.9 0.0 collective-permute-start.6
  12.9 1.9 %collective-permute-start = (bf16[17,32,256]{2,1,0:T(8,128)(2,1)S(1)}, bf16[17,32,256]{2,1,0:T(8,128)(2,1)S(1)}, u32[]{:S(2)}, u32[]{:S(2)}) collective-permute-start(bf16[17,32,256]{2,1,0:T(8,128)(2,1)S(1)} %get-tuple-element.33), channel_id=1, source_target_pairs={{0,1},{1,0},{2,3},{3,2},{4,5},{5,4},{6,7},{7,6},{8,9},{9,8},{10,11... | collective-permute-start | bytes 835592 | tf_op jit(solution)/shard_map/ppermute | solution.py:294
  14.8 1.5 %collective-permute-start.1 = (bf16[17,32,256]{2,1,0:T(8,128)(2,1)S(1)}, bf16[17,32,256]{2,1,0:T(8,128)(2,1)S(1)}, u32[]{:S(2)}, u32[]{:S(2)}) collective-permute-start(bf16[17,32,256]{2,1,0:T(8,128)(2,1)S(1)} %get-tuple-element.34), channel_id=1, source_target_pairs={{0,2},{1,3},{2,0},{3,1},{4,6},{5,7},{6,4},{7,5},{8,10},{9,11},{10,... | collective-permute-start | bytes 835592 | tf_op jit(solution)/shard_map/ppermute | solution.py:294
  16.3 2.5 %collective-permute-done.4.refs_1_ = bf16[17,32,256]{2,1,0:T(8,128)(2,1)S(1)} collective-permute-done((bf16[17,32,256]{2,1,0:T(8,128)(2,1)S(1)}, bf16[17,32,256]{2,1,0:T(8,128)(2,1)S(1)}, u32[]{:S(2)}, u32[]{:S(2)}) %collective-permute-start.4) | collective-permute-done | bytes 278560 | tf_op jit(solution)/shard_map/ppermute | solution.py:294
  18.8 3.0 %collective-permute-start.2 = (bf16[17,32,256]{2,1,0:T(8,128)(2,1)S(1)}, bf16[17,32,256]{2,1,0:T(8,128)(2,1)S(1)}, u32[]{:S(2)}, u32[]{:S(2)}) collective-permute-start(bf16[17,32,256]{2,1,0:T(8,128)(2,1)S(1)} %get-tuple-element.35), channel_id=1, source_target_pairs={{0,3},{1,2},{2,1},{3,0},{4,7},{5,6},{6,5},{7,4},{8,11},{9,10},{10,... | collective-permute-start | bytes 835592 | tf_op jit(solution)/shard_map/ppermute | solution.py:294
  21.8 5.1 %collective-permute-done.5.refs_2_ = bf16[17,32,256]{2,1,0:T(8,128)(2,1)S(1)} collective-permute-done((bf16[17,32,256]{2,1,0:T(8,128)(2,1)S(1)}, bf16[17,32,256]{2,1,0:T(8,128)(2,1)S(1)}, u32[]{:S(2)}, u32[]{:S(2)}) %collective-permute-start.5) | collective-permute-done | bytes 278560 | tf_op jit(solution)/shard_map/ppermute | solution.py:294
  26.9 1.7 %pack.3 = (bf16[16,80,256]{2,1,0:T(8,128)(2,1)}, bf16[16,80,256]{2,1,0:T(8,128)(2,1)S(1)}) custom-call(s32[1]{0:T(128)} %bitcast.1.me_ref, bf16[17,32,256]{2,1,0:T(8,128)(2,1)S(1)} %get-tuple-element.37.refs_0_, bf16[17,32,256]{2,1,0:T(8,128)(2,1)S(1)} %collective-permute-done.4.refs_1_, bf16[17,32,256]{2,1,0:T(8,128)(2,1)S(1)} %collective-permute-done.5.refs_2_, ...), custom_call_target="tpu_custom_call" | custom-call | flops 1024 | bytes 1024 | tf_op jit(solution)/shard_map/pack/pallas_call | solution.py:149
  28.6 1.6 %collective-permute-start.8 = (bf16[16,80,256]{2,1,0:T(8,128)(2,1)}, bf16[16,80,256]{2,1,0:T(8,128)(2,1)S(1)}, u32[]{:S(2)}, u32[]{:S(2)}) collective-permute-start(bf16[16,80,256]{2,1,0:T(8,128)(2,1)} %get-tuple-element.43), channel_id=1, source_target_pairs={{0,8},{4,12},{8,16},{12,20},{16,24},{20,28},{24,0},{28,4},{1,9},{5... | collective-permute-start | bytes 1966088 | tf_op jit(solution)/shard_map/ppermute | solution.py:284
  30.2 0.0 collective-permute-start.7
  30.2 0.6 collective-permute-done.refs_1_
  30.8 6.6 %collective-permute-done.1.refs_2_ = bf16[17,32,256]{2,1,0:T(8,128)(2,1)S(1)} collective-permute-done((bf16[17,32,256]{2,1,0:T(8,128)(2,1)S(1)}, bf16[17,32,256]{2,1,0:T(8,128)(2,1)S(1)}, u32[]{:S(2)}, u32[]{:S(2)}) %collective-permute-start.1) | collective-permute-done | bytes 278560 | tf_op jit(solution)/shard_map/ppermute | solution.py:294
  37.4 0.0 collective-permute-done.2.refs_3_
  37.4 0.9 pack.2
  38.3 0.9 copy-done.2
  39.1 1.6 %collective-permute-start.10 = (bf16[16,80,256]{2,1,0:T(8,128)(2,1)}, bf16[16,80,256]{2,1,0:T(8,128)(2,1)S(1)}, u32[]{:S(2)}, u32[]{:S(2)}) collective-permute-start(bf16[16,80,256]{2,1,0:T(8,128)(2,1)} %copy-done.2), channel_id=1, source_target_pairs={{0,8},{4,12},{8,16},{12,20},{16,24},{20,28},{24,0},{28,4},{1,9},{5... | collective-permute-start | bytes 1966088 | tf_op jit(solution)/shard_map/ppermute | solution.py:284
  40.7 0.0 collective-permute-done.7.refs_1_
  40.7 5.8 %pairs.9 = (bf16[2,32,256,2048]{3,2,1,0:T(8,128)(2,1)}, bf16[16,512,80]{2,1,0:T(8,128)(2,1)S(1)}) custom-call(s32[1]{0:T(128)} %bitcast.place_ref, bf16[16,80,256]{2,1,0:T(8,128)(2,1)S(1)} %get-tuple-element.41.refs_0_, bf16[16,80,256]{2,1,0:T(8,128)(2,1)S(1)} %collective-permute-done.7.refs_1_), custom_call_target="tpu_custom_call" | custom-call | flops 1024 | bytes 1024 | tf_op jit(solution)/shard_map/pairs/pallas_call | solution.py:228
  46.5 5.8 %pairs.10 = (bf16[2,32,256,2048]{3,2,1,0:T(8,128)(2,1)}, bf16[16,512,80]{2,1,0:T(8,128)(2,1)S(1)}, bf16[16,80,256]{2,1,0:T(8,128)(2,1)S(1)}) custom-call(s32[1]{0:T(128)} %bitcast.place_ref, bf16[16,80,256]{2,1,0:T(8,128)(2,1)S(1)} %get-tuple-element.36.refs_0_, ...), custom_call_target="tpu_custom_call", output_to_operand_aliasing={{0}: (3, {}), {2}: (4, {})} | custom-call | flops 1024 | bytes 1024 | tf_op jit(solution)/shard_map/pairs/pallas_call | solution.py:228
  52.4 0.2 collective-permute-start.9
  52.6 1.6 %collective-permute-start.12 = (bf16[16,80,256]{2,1,0:T(8,128)(2,1)S(1)}, bf16[16,80,256]{2,1,0:T(8,128)(2,1)S(1)}, u32[]{:S(2)}, u32[]{:S(2)}) collective-permute-start(bf16[16,80,256]{2,1,0:T(8,128)(2,1)S(1)} %get-tuple-element.44.refs_0_), channel_id=1, source_target_pairs={{0,8},{4,12},{8,16},{12,20},{16,24},{20,28},{24,0},{28,4},{1,9},{5... | collective-permute-start | bytes 1966088 | tf_op jit(solution)/shard_map/ppermute | solution.py:284
  54.2 4.7 %collective-permute-done.10.refs_4_ = bf16[16,80,256]{2,1,0:T(8,128)(2,1)S(1)} collective-permute-done((bf16[16,80,256]{2,1,0:T(8,128)(2,1)}, bf16[16,80,256]{2,1,0:T(8,128)(2,1)S(1)}, u32[]{:S(2)}, u32[]{:S(2)}) %collective-permute-start.10) | collective-permute-done | bytes 655392 | tf_op jit(solution)/shard_map/ppermute | solution.py:284
  58.9 4.7 %pairs.11 = (bf16[2,32,256,2048]{3,2,1,0:T(8,128)(2,1)}, bf16[16,80,256]{2,1,0:T(8,128)(2,1)S(1)}) custom-call(s32[1]{0:T(128)} %bitcast.place_ref, bf16[16,80,256]{2,1,0:T(8,128)(2,1)S(1)} %get-tuple-element.44.refs_0_, bf16[16,80,256]{2,1,0:T(8,128)(2,1)S(1)} %collective-permute-done.9.refs_1_, ...), custom_call_target="tpu_custom_call", output_to_operand_aliasing={{0}: (4, {}), {1}: (5, {})} | custom-call | flops 1024 | bytes 1024 | tf_op jit(solution)/shard_map/pairs/pallas_call | solution.py:228
  63.6 0.0 collective-permute-start.11
  63.6 0.0 collective-permute-start.14
  63.6 9.3 %collective-permute-done.12.refs_4_ = bf16[16,80,256]{2,1,0:T(8,128)(2,1)S(1)} collective-permute-done((bf16[16,80,256]{2,1,0:T(8,128)(2,1)S(1)}, bf16[16,80,256]{2,1,0:T(8,128)(2,1)S(1)}, u32[]{:S(2)}, u32[]{:S(2)}) %collective-permute-start.12) | collective-permute-done | bytes 655392 | tf_op jit(solution)/shard_map/ppermute | solution.py:284
  72.9 0.0 collective-permute-done.11.refs_1_
  72.9 4.8 %pairs.12 = (bf16[2,32,256,2048]{3,2,1,0:T(8,128)(2,1)}, bf16[16,80,256]{2,1,0:T(8,128)(2,1)S(1)}) custom-call(s32[1]{0:T(128)} %bitcast.place_ref, bf16[16,80,256]{2,1,0:T(8,128)(2,1)S(1)} %get-tuple-element.48.refs_0_, bf16[16,80,256]{2,1,0:T(8,128)(2,1)S(1)} %collective-permute-done.11.refs_1_, ...), custom_call_target="tpu_custom_call", output_to_operand_aliasing={{0}: (4, {}), {1}: (5, {})} | custom-call | flops 1024 | bytes 1024 | tf_op jit(solution)/shard_map/pairs/pallas_call | solution.py:228
  77.7 0.0 collective-permute-start.17
  77.7 9.3 %collective-permute-done.14.refs_4_ = bf16[16,80,256]{2,1,0:T(8,128)(2,1)S(1)} collective-permute-done((bf16[16,80,256]{2,1,0:T(8,128)(2,1)S(1)}, bf16[16,80,256]{2,1,0:T(8,128)(2,1)S(1)}, u32[]{:S(2)}, u32[]{:S(2)}) %collective-permute-start.14) | collective-permute-done | bytes 655392 | tf_op jit(solution)/shard_map/ppermute | solution.py:284
  87.0 4.8 %pairs.13 = (bf16[2,32,256,2048]{3,2,1,0:T(8,128)(2,1)}, bf16[16,80,256]{2,1,0:T(8,128)(2,1)S(1)}) custom-call(s32[1]{0:T(128)} %bitcast.place_ref, bf16[16,80,256]{2,1,0:T(8,128)(2,1)S(1)} %get-tuple-element.51.refs_0_, bf16[16,80,256]{2,1,0:T(8,128)(2,1)S(1)} %collective-permute-done.13.refs_1_, ...), custom_call_target="tpu_custom_call", output_to_operand_aliasing={{0}: (4, {}), {1}: (5, {})} | custom-call | flops 1024 | bytes 1024 | tf_op jit(solution)/shard_map/pairs/pallas_call | solution.py:228
  91.7 0.0 collective-permute-start.15
  91.7 9.3 %collective-permute-done.17.refs_4_ = bf16[16,80,256]{2,1,0:T(8,128)(2,1)S(1)} collective-permute-done((bf16[16,80,256]{2,1,0:T(8,128)(2,1)S(1)}, bf16[16,80,256]{2,1,0:T(8,128)(2,1)S(1)}, u32[]{:S(2)}, u32[]{:S(2)}) %collective-permute-start.17) | collective-permute-done | bytes 655392 | tf_op jit(solution)/shard_map/ppermute | solution.py:284
  101.0 4.8 %pairs.14 = (bf16[2,32,256,2048]{3,2,1,0:T(8,128)(2,1)}, bf16[16,80,256]{2,1,0:T(8,128)(2,1)S(1)}) custom-call(s32[1]{0:T(128)} %bitcast.place_ref, bf16[16,80,256]{2,1,0:T(8,128)(2,1)S(1)} %get-tuple-element.53.refs_0_, bf16[16,80,256]{2,1,0:T(8,128)(2,1)S(1)} %collective-permute-done.16.refs_1_, ...), custom_call_target="tpu_custom_call", output_to_operand_aliasing={{0}: (4, {}), {1}: (5, {})} | custom-call | flops 1024 | bytes 1024 | tf_op jit(solution)/shard_map/pairs/pallas_call | solution.py:228
  105.8 0.1 collective-permute-start.19
  105.9 0.5 collective-permute-start.18
  106.4 0.2 fusion
  106.6 0.9 collective-permute-done.19.refs_1_
  107.5 2.7 %pairs.15.refs_3_ = bf16[2,32,256,2048]{3,2,1,0:T(8,128)(2,1)} custom-call(s32[1]{0:T(128)} %bitcast.place_ref, bf16[8,80,256]{2,1,0:T(8,128)(2,1)S(1)} %get-tuple-element.61.refs_0_, bf16[8,80,256]{2,1,0:T(8,128)(2,1)S(1)} %collective-permute-done.19.refs_1_, bf16[8,512,80]{2,1,0:T(8,128)(2,1)S(1)} %get-tuple-element.59.refs_2_, ...), custom_call_target="tpu_custom_call", output_to_operand_aliasing={{}: (4, {})} | custom-call | flops 1024 | bytes 1024 | tf_op jit(solution)/shard_map/pairs/pallas_call | solution.py:228
  110.3 2.7 %pairs.16.refs_1_ = bf16[2,32,256,2048]{3,2,1,0:T(8,128)(2,1)} custom-call(s32[1]{0:T(128)} %bitcast.place_ref, bf16[8,80,256]{2,1,0:T(8,128)(2,1)S(1)} %get-tuple-element.62.refs_0_, bf16[8,80,256]{2,1,0:T(8,128)(2,1)S(1)} %collective-permute-done.18.refs_1_, bf16[8,512,80]{2,1,0:T(8,128)(2,1)S(1)} %get-tuple-element.60.refs_2_, ...), custom_call_target="tpu_custom_call", output_to_operand_aliasing={{}: (4, {})} | custom-call | flops 1024 | bytes 1024 | tf_op jit(solution)/shard_map/pairs/pallas_call | solution.py:228
  113.0 1.8 %collective-permute-done.15.refs_0_ = bf16[16,80,256]{2,1,0:T(8,128)(2,1)S(1)} collective-permute-done((bf16[16,80,256]{2,1,0:T(8,128)(2,1)S(1)}, bf16[16,80,256]{2,1,0:T(8,128)(2,1)S(1)}, u32[]{:S(2)}, u32[]{:S(2)}) %collective-permute-start.15) | collective-permute-done | bytes 655392 | tf_op jit(solution)/shard_map/ppermute | solution.py:284
  114.8 2.1 %collective-permute-done.20.refs_1_ = bf16[16,80,256]{2,1,0:T(8,128)(2,1)S(1)} collective-permute-done((bf16[16,80,256]{2,1,0:T(8,128)(2,1)S(1)}, bf16[16,80,256]{2,1,0:T(8,128)(2,1)S(1)}, u32[]{:S(2)}, u32[]{:S(2)}) %collective-permute-start.20) | collective-permute-done | bytes 655392 | tf_op jit(solution)/shard_map/ppermute | solution.py:281
  116.9 4.8 %pairs.17 = bf16[2,32,256,2048]{3,2,1,0:T(8,128)(2,1)} custom-call(s32[1]{0:T(128)} %bitcast.place_ref, bf16[16,80,256]{2,1,0:T(8,128)(2,1)S(1)} %get-tuple-element.57.refs_0_, bf16[16,80,256]{2,1,0:T(8,128)(2,1)S(1)} %collective-permute-done.20.refs_1_, bf16[16,512,80]{2,1,0:T(8,128)(2,1)S(1)} %get-tuple-element.49.refs_2_, ...), custom_call_target="tpu_custom_call", output_to_operand_aliasing={{}: (4, {})} | custom-call | flops 1024 | bytes 1024 | tf_op jit(solution)/shard_map/pairs/pallas_call | solution.py:228
  (15 shorter events, 0.1 us)
Async XLA Ops:
  0.7 1.0 copy-start
  1.7 0.7 copy-start.1
  8.3 10.5 %collective-permute-start.4 = (bf16[17,32,256]{2,1,0:T(8,128)(2,1)S(1)}, bf16[17,32,256]{2,1,0:T(8,128)(2,1)S(1)}, u32[]{:S(2)}, u32[]{:S(2)}) collective-permute-start(bf16[17,32,256]{2,1,0:T(8,128)(2,1)S(1)} %get-tuple-element.38), channel_id=1, source_target_pairs={{0,1},{1,0},{2,3},{3,2},{4,5},{5,4},{6,7},{7,6},{8,9},{9,8},{10,11... | collective-permute-start | bytes 835592 | tf_op jit(solution)/shard_map/ppermute | solution.py:294
  11.3 15.6 %collective-permute-start.5 = (bf16[17,32,256]{2,1,0:T(8,128)(2,1)S(1)}, bf16[17,32,256]{2,1,0:T(8,128)(2,1)S(1)}, u32[]{:S(2)}, u32[]{:S(2)}) collective-permute-start(bf16[17,32,256]{2,1,0:T(8,128)(2,1)S(1)} %get-tuple-element.39), channel_id=1, source_target_pairs={{0,2},{1,3},{2,0},{3,1},{4,6},{5,7},{6,4},{7,5},{8,10},{9,11},{10,... | collective-permute-start | bytes 835592 | tf_op jit(solution)/shard_map/ppermute | solution.py:294
  12.9 14.0 %collective-permute-start.6 = (bf16[17,32,256]{2,1,0:T(8,128)(2,1)S(1)}, bf16[17,32,256]{2,1,0:T(8,128)(2,1)S(1)}, u32[]{:S(2)}, u32[]{:S(2)}) collective-permute-start(bf16[17,32,256]{2,1,0:T(8,128)(2,1)S(1)} %get-tuple-element.40), channel_id=1, source_target_pairs={{0,3},{1,2},{2,1},{3,0},{4,7},{5,6},{6,5},{7,4},{8,11},{9,10},{10,... | collective-permute-start | bytes 835592 | tf_op jit(solution)/shard_map/ppermute | solution.py:294
  12.9 17.9 %collective-permute-start = (bf16[17,32,256]{2,1,0:T(8,128)(2,1)S(1)}, bf16[17,32,256]{2,1,0:T(8,128)(2,1)S(1)}, u32[]{:S(2)}, u32[]{:S(2)}) collective-permute-start(bf16[17,32,256]{2,1,0:T(8,128)(2,1)S(1)} %get-tuple-element.33), channel_id=1, source_target_pairs={{0,1},{1,0},{2,3},{3,2},{4,5},{5,4},{6,7},{7,6},{8,9},{9,8},{10,11... | collective-permute-start | bytes 835592 | tf_op jit(solution)/shard_map/ppermute | solution.py:294
  14.8 22.5 %collective-permute-start.1 = (bf16[17,32,256]{2,1,0:T(8,128)(2,1)S(1)}, bf16[17,32,256]{2,1,0:T(8,128)(2,1)S(1)}, u32[]{:S(2)}, u32[]{:S(2)}) collective-permute-start(bf16[17,32,256]{2,1,0:T(8,128)(2,1)S(1)} %get-tuple-element.34), channel_id=1, source_target_pairs={{0,2},{1,3},{2,0},{3,1},{4,6},{5,7},{6,4},{7,5},{8,10},{9,11},{10,... | collective-permute-start | bytes 835592 | tf_op jit(solution)/shard_map/ppermute | solution.py:294
  18.8 18.5 %collective-permute-start.2 = (bf16[17,32,256]{2,1,0:T(8,128)(2,1)S(1)}, bf16[17,32,256]{2,1,0:T(8,128)(2,1)S(1)}, u32[]{:S(2)}, u32[]{:S(2)}) collective-permute-start(bf16[17,32,256]{2,1,0:T(8,128)(2,1)S(1)} %get-tuple-element.35), channel_id=1, source_target_pairs={{0,3},{1,2},{2,1},{3,0},{4,7},{5,6},{6,5},{7,4},{8,11},{9,10},{10,... | collective-permute-start | bytes 835592 | tf_op jit(solution)/shard_map/ppermute | solution.py:294
  28.6 17.9 %collective-permute-start.8 = (bf16[16,80,256]{2,1,0:T(8,128)(2,1)}, bf16[16,80,256]{2,1,0:T(8,128)(2,1)S(1)}, u32[]{:S(2)}, u32[]{:S(2)}) collective-permute-start(bf16[16,80,256]{2,1,0:T(8,128)(2,1)} %get-tuple-element.43), channel_id=1, source_target_pairs={{0,8},{4,12},{8,16},{12,20},{16,24},{20,28},{24,0},{28,4},{1,9},{5... | collective-permute-start | bytes 1966088 | tf_op jit(solution)/shard_map/ppermute | solution.py:284
  30.2 10.5 %collective-permute-start.7 = (bf16[16,80,256]{2,1,0:T(8,128)(2,1)S(1)}, bf16[16,80,256]{2,1,0:T(8,128)(2,1)S(1)}, u32[]{:S(2)}, u32[]{:S(2)}) collective-permute-start(bf16[16,80,256]{2,1,0:T(8,128)(2,1)S(1)} %get-tuple-element.41.refs_0_), channel_id=1, source_target_pairs={{0,4},{4,0},{8,12},{12,8},{16,20},{20,16},{24,28},{28,24},{1,5},{5... | collective-permute-start | bytes 1966088 | tf_op jit(solution)/shard_map/ppermute | solution.py:281
  38.3 0.9 copy-start.2
  39.1 7.4 %collective-permute-start.3 = (bf16[16,80,256]{2,1,0:T(8,128)(2,1)S(1)}, bf16[16,80,256]{2,1,0:T(8,128)(2,1)S(1)}, u32[]{:S(2)}, u32[]{:S(2)}) collective-permute-start(bf16[16,80,256]{2,1,0:T(8,128)(2,1)S(1)} %get-tuple-element.36.refs_0_), channel_id=1, source_target_pairs={{0,4},{4,0},{8,12},{12,8},{16,20},{20,16},{24,28},{28,24},{1,5},{5... | collective-permute-start | bytes 1966088 | tf_op jit(solution)/shard_map/ppermute | solution.py:281
  39.1 19.8 %collective-permute-start.10 = (bf16[16,80,256]{2,1,0:T(8,128)(2,1)}, bf16[16,80,256]{2,1,0:T(8,128)(2,1)S(1)}, u32[]{:S(2)}, u32[]{:S(2)}) collective-permute-start(bf16[16,80,256]{2,1,0:T(8,128)(2,1)} %copy-done.2), channel_id=1, source_target_pairs={{0,8},{4,12},{8,16},{12,20},{16,24},{20,28},{24,0},{28,4},{1,9},{5... | collective-permute-start | bytes 1966088 | tf_op jit(solution)/shard_map/ppermute | solution.py:284
  52.4 6.5 %collective-permute-start.9 = (bf16[16,80,256]{2,1,0:T(8,128)(2,1)S(1)}, bf16[16,80,256]{2,1,0:T(8,128)(2,1)S(1)}, u32[]{:S(2)}, u32[]{:S(2)}) collective-permute-start(bf16[16,80,256]{2,1,0:T(8,128)(2,1)S(1)} %get-tuple-element.44.refs_0_), channel_id=1, source_target_pairs={{0,4},{4,0},{8,12},{12,8},{16,20},{20,16},{24,28},{28,24},{1,5},{5... | collective-permute-start | bytes 1966088 | tf_op jit(solution)/shard_map/ppermute | solution.py:281
  52.6 20.3 %collective-permute-start.12 = (bf16[16,80,256]{2,1,0:T(8,128)(2,1)S(1)}, bf16[16,80,256]{2,1,0:T(8,128)(2,1)S(1)}, u32[]{:S(2)}, u32[]{:S(2)}) collective-permute-start(bf16[16,80,256]{2,1,0:T(8,128)(2,1)S(1)} %get-tuple-element.44.refs_0_), channel_id=1, source_target_pairs={{0,8},{4,12},{8,16},{12,20},{16,24},{20,28},{24,0},{28,4},{1,9},{5... | collective-permute-start | bytes 1966088 | tf_op jit(solution)/shard_map/ppermute | solution.py:284
  63.6 9.3 %collective-permute-start.11 = (bf16[16,80,256]{2,1,0:T(8,128)(2,1)S(1)}, bf16[16,80,256]{2,1,0:T(8,128)(2,1)S(1)}, u32[]{:S(2)}, u32[]{:S(2)}) collective-permute-start(bf16[16,80,256]{2,1,0:T(8,128)(2,1)S(1)} %get-tuple-element.48.refs_0_), channel_id=1, source_target_pairs={{0,4},{4,0},{8,12},{12,8},{16,20},{20,16},{24,28},{28,24},{1,5},{5... | collective-permute-start | bytes 1966088 | tf_op jit(solution)/shard_map/ppermute | solution.py:281
  63.6 23.3 %collective-permute-start.14 = (bf16[16,80,256]{2,1,0:T(8,128)(2,1)S(1)}, bf16[16,80,256]{2,1,0:T(8,128)(2,1)S(1)}, u32[]{:S(2)}, u32[]{:S(2)}) collective-permute-start(bf16[16,80,256]{2,1,0:T(8,128)(2,1)S(1)} %get-tuple-element.48.refs_0_), channel_id=1, source_target_pairs={{0,8},{4,12},{8,16},{12,20},{16,24},{20,28},{24,0},{28,4},{1,9},{5... | collective-permute-start | bytes 1966088 | tf_op jit(solution)/shard_map/ppermute | solution.py:284
  77.7 9.3 %collective-permute-start.13 = (bf16[16,80,256]{2,1,0:T(8,128)(2,1)S(1)}, bf16[16,80,256]{2,1,0:T(8,128)(2,1)S(1)}, u32[]{:S(2)}, u32[]{:S(2)}) collective-permute-start(bf16[16,80,256]{2,1,0:T(8,128)(2,1)S(1)} %get-tuple-element.51.refs_0_), channel_id=1, source_target_pairs={{0,4},{4,0},{8,12},{12,8},{16,20},{20,16},{24,28},{28,24},{1,5},{5... | collective-permute-start | bytes 1966088 | tf_op jit(solution)/shard_map/ppermute | solution.py:281
  77.7 23.3 %collective-permute-start.17 = (bf16[16,80,256]{2,1,0:T(8,128)(2,1)S(1)}, bf16[16,80,256]{2,1,0:T(8,128)(2,1)S(1)}, u32[]{:S(2)}, u32[]{:S(2)}) collective-permute-start(bf16[16,80,256]{2,1,0:T(8,128)(2,1)S(1)} %get-tuple-element.51.refs_0_), channel_id=1, source_target_pairs={{0,8},{4,12},{8,16},{12,20},{16,24},{20,28},{24,0},{28,4},{1,9},{5... | collective-permute-start | bytes 1966088 | tf_op jit(solution)/shard_map/ppermute | solution.py:284
  91.7 9.3 %collective-permute-start.16 = (bf16[16,80,256]{2,1,0:T(8,128)(2,1)S(1)}, bf16[16,80,256]{2,1,0:T(8,128)(2,1)S(1)}, u32[]{:S(2)}, u32[]{:S(2)}) collective-permute-start(bf16[16,80,256]{2,1,0:T(8,128)(2,1)S(1)} %get-tuple-element.53.refs_0_), channel_id=1, source_target_pairs={{0,4},{4,0},{8,12},{12,8},{16,20},{20,16},{24,28},{28,24},{1,5},{5... | collective-permute-start | bytes 1966088 | tf_op jit(solution)/shard_map/ppermute | solution.py:281
  91.7 23.1 %collective-permute-start.15 = (bf16[16,80,256]{2,1,0:T(8,128)(2,1)S(1)}, bf16[16,80,256]{2,1,0:T(8,128)(2,1)S(1)}, u32[]{:S(2)}, u32[]{:S(2)}) collective-permute-start(bf16[16,80,256]{2,1,0:T(8,128)(2,1)S(1)} %get-tuple-element.53.refs_0_), channel_id=1, source_target_pairs={{0,8},{4,12},{8,16},{12,20},{16,24},{20,28},{24,0},{28,4},{1,9},{5... | collective-permute-start | bytes 1966088 | tf_op jit(solution)/shard_map/ppermute | solution.py:284
  105.8 1.7 %collective-permute-start.19 = (bf16[8,80,256]{2,1,0:T(8,128)(2,1)S(1)}, bf16[8,80,256]{2,1,0:T(8,128)(2,1)S(1)}, u32[]{:S(2)}, u32[]{:S(2)}) collective-permute-start(bf16[8,80,256]{2,1,0:T(8,128)(2,1)S(1)} %get-tuple-element.61.refs_0_), channel_id=1, source_target_pairs={{0,4},{4,0},{8,12},{12,8},{16,20},{20,16},{24,28},{28,24},{1,5},{5... | collective-permute-start | bytes 983048 | tf_op jit(solution)/shard_map/ppermute | solution.py:330
  105.9 4.3 %collective-permute-start.18 = (bf16[8,80,256]{2,1,0:T(8,128)(2,1)S(1)}, bf16[8,80,256]{2,1,0:T(8,128)(2,1)S(1)}, u32[]{:S(2)}, u32[]{:S(2)}) collective-permute-start(bf16[8,80,256]{2,1,0:T(8,128)(2,1)S(1)} %get-tuple-element.62.refs_0_), channel_id=1, source_target_pairs={{0,4},{4,0},{8,12},{12,8},{16,20},{20,16},{24,28},{28,24},{1,5},{5... | collective-permute-start | bytes 983048 | tf_op jit(solution)/shard_map/ppermute | solution.py:330
  114.8 2.1 %collective-permute-start.20 = (bf16[16,80,256]{2,1,0:T(8,128)(2,1)S(1)}, bf16[16,80,256]{2,1,0:T(8,128)(2,1)S(1)}, u32[]{:S(2)}, u32[]{:S(2)}) collective-permute-start(bf16[16,80,256]{2,1,0:T(8,128)(2,1)S(1)} %get-tuple-element.57.refs_0_), channel_id=1, source_target_pairs={{0,4},{4,0},{8,12},{12,8},{16,20},{20,16},{24,28},{28,24},{1,5},{5... | collective-permute-start | bytes 1966088 | tf_op jit(solution)/shard_map/ppermute | solution.py:281
